TPU v7x, 256 devices: a whole 4x4x8 slice. The times are simulated.
256 devices in a mesh: gx: 16 (over x, z_lo), gy: 16 (over z_hi, y, core).
Axes of the slice: x: 4, y: 4, z: 8 (z_hi: 2, z_lo: 4; z = z_hi * 4 + z_lo), core: 2. Of those that a mesh axis runs over, the one named last changes fastest.
Arguments:
- migrated: float32 [256, 256, 128], P('gx', 'gy'), may hold values from -18 to 18
- prior_sample: float32 [256, 256, 128], P('gx', 'gy'), may hold values from -6 to 6
- damping: float32 [256, 256, 128], P('gx', 'gy'), may hold values from 0.2 to 2
- psf_bank: float32 [32, 32, 32, 32], replicated, may hold values from 0.05 to 3
- psf_index: int32 [16, 16, 6], P('gx', 'gy'), may hold values from 0 to 31
- z_shift: int32 [16, 16], P('gx', 'gy'), may hold values from 0 to 15
Outputs:
- solution: float32 [256, 256, 128], P('gx', 'gy')
- residual: float32 [256, 256, 128], P('gx', 'gy')
All inputs are finite; a program needn't handle non-finite values.
Results may differ from a plain program's by a relative error of at most 0.0001.
Values sent between devices are 32-bit elements; how exact they have to be, the bound alone decides.
No kernel may reach another device: no remote copies, remote signals or barrier semaphores. Data moves between devices by JAX's collectives and lax.ppermute only.
A program may use at most 192 MiB of HBM per device.

v0:
```python
import math

import numpy as np
import jax
import jax.numpy as jnp
from jax import lax
from jax.experimental import pallas as pl
from jax.experimental.pallas import tpu as pltpu
from jax.sharding import PartitionSpec as P

PATCH = 32
HALF = 16
NPZ = 6
KZ = 17
LANES = 128
SUB = 8
VMEM = pltpu.VMEM


def z_table():
    table = np.zeros((160, 2 * LANES))
    taper = np.sin(math.pi * (np.arange(PATCH) + 0.5) / PATCH)
    for p in range(NPZ):
        for cell in range(PATCH):
            for kz in range(KZ):
                phase = 2.0 * math.pi * (kz * cell % PATCH) / PATCH
                row = 16 + 16 * p + cell
                table[row, KZ * p + kz] = taper[cell] * math.cos(phase)
                if 0 < kz < HALF:
                    table[row, LANES + KZ * p + kz] = -taper[cell] * math.sin(phase)
    return table.astype(np.float32)


def pick_table():
    table = np.zeros((NPZ, PATCH, 2 * LANES))
    for p in range(NPZ):
        for kz in range(KZ):
            table[p, kz, KZ * p + kz] = 1.0
            if 0 < kz < HALF:
                table[p, PATCH - kz, LANES + KZ * p + kz] = 1.0
    return table.astype(np.float32)


TAPER = [math.sin(math.pi * (i + 0.5) / PATCH) for i in range(PATCH)]


def twiddle(value, k, n, sign):
    k %= n
    re, im = value
    if k == 0:
        return value
    if 4 * k == n:
        return (-im, re) if sign > 0 else (im, -re)
    if 2 * k == n:
        return (-re, -im)
    if 4 * k == 3 * n:
        return (im, -re) if sign > 0 else (-im, re)
    c = math.cos(2.0 * math.pi * k / n)
    s = sign * math.sin(2.0 * math.pi * k / n)
    if 8 * k % n == 0:
        h = abs(c)
        cs, ss = (1 if c > 0 else -1), (1 if s > 0 else -1)
        if cs == ss:
            a, b = re - im, re + im
            return (a * (h * cs), b * (h * cs))
        a, b = re + im, im - re
        return (a * (h * cs), b * (h * cs))
    return (re * c - im * s, re * s + im * c)


def add(a, b):
    return (a[0] + b[0], a[1] + b[1])


def sub(a, b):
    return (a[0] - b[0], a[1] - b[1])


def dft4(x, sign):
    a, b = add(x[0], x[2]), sub(x[0], x[2])
    c, d = add(x[1], x[3]), twiddle(sub(x[1], x[3]), 1, 4, sign)
    return [add(a, c), add(b, d), sub(a, c), sub(b, d)]


def dft8(x, sign):
    even = dft4(x[0::2], sign)
    odd = [twiddle(v, k, 8, sign) for k, v in enumerate(dft4(x[1::2], sign))]
    return [add(even[k], odd[k]) for k in range(4)] + [sub(even[k], odd[k]) for k in range(4)]


def dft32(load, sign):
    first = []
    for n2 in range(8):
        part = dft4([load(8 * n1 + n2) for n1 in range(4)], sign)
        first.append([twiddle(v, n2 * k1, 32, sign) for k1, v in enumerate(part)])
    out = [None] * 32
    for k1 in range(4):
        part = dft8([first[n2][k1] for n2 in range(8)], sign)
        for k2 in range(8):
            out[k1 + 4 * k2] = part[k2]
    return out


def halves(value):
    high = value.astype(jnp.bfloat16)
    return high, (value - high.astype(jnp.float32)).astype(jnp.bfloat16)


def dot(a, b, contract_b):
    return lax.dot_general(a, b, (((1,), (contract_b,)), ((), ())), preferred_element_type=jnp.float32)


def dot3(a, b, contract_b):
    return dot(a[0], b[0], contract_b) + (dot(a[1], b[0], contract_b) + dot(a[0], b[1], contract_b))


def spectra_kernel(index_ref, bank_ref, pick_ref, out_ref, cubes, back, sems):
    copies = [
        pltpu.make_async_copy(bank_ref.at[index_ref[p]], cubes.at[p], sems.at[p]) for p in range(NPZ)
    ]
    for copy in copies:
        copy.start()
    total = None
    for p, copy in enumerate(copies):
        copy.wait()
        high, low = halves(cubes[p].reshape(PATCH * PATCH, PATCH))
        pick = pick_ref[p].astype(jnp.bfloat16)
        part = dot(high, pick, 0) + dot(low, pick, 0)
        total = part if total is None else total + part
    out_ref[...] = total[:, :LANES]
    back[...] = total[:, LANES:]
    row = lax.broadcasted_iota(jnp.int32, (SUB, LANES), 0)
    mirror = (SUB - row) % SUB
    for kx in range(PATCH):
        source = (PATCH - kx) % PATCH
        turned = [
            jnp.take_along_axis(back[pl.ds(source * PATCH + SUB * g, SUB), :], mirror, axis=0, mode="promise_in_bounds") for g in range(4)
        ]
        for g in range(4):
            rows = pl.ds(kx * PATCH + SUB * g, SUB)
            mirrored = jnp.where(row == 0, turned[(4 - g) % 4], turned[3 - g])
            out_ref[rows, :] = out_ref[rows, :] + mirrored


def spectra_of(index, bank):
    return pl.pallas_call(
        spectra_kernel,
        out_shape=jax.ShapeDtypeStruct((PATCH * PATCH, LANES), jnp.float32),
        in_specs=[
            pl.BlockSpec(memory_space=pltpu.SMEM),
            pl.BlockSpec(memory_space=pltpu.HBM),
            pl.BlockSpec(memory_space=VMEM),
        ],
        out_specs=pl.BlockSpec(memory_space=VMEM),
        scratch_shapes=[
            VMEM((NPZ, PATCH, PATCH, PATCH), jnp.float32),
            VMEM((PATCH * PATCH, LANES), jnp.float32),
            pltpu.SemaphoreType.DMA((NPZ,)),
        ],
        compiler_params=pltpu.CompilerParams(vmem_limit_bytes=50 * 2**20),
        cost_estimate=pl.CostEstimate(flops=400_000_000, bytes_accessed=8_000_000, transcendentals=0),
        name="spectra",
    )(index, bank, pick_table())


def patches_kernel(shift_ref, table_ref, spectra_ref, damping_ref, b00, b10, b01, b11,
                   o00, o10, o01, o11, sums_ref, real, imag):
    window = halves(pltpu.roll(table_ref[...], shift_ref[0] + 144, 0)[:LANES])
    for xq, yq, block in ((0, 0, b00), (1, 0, b10), (0, 1, b01), (1, 1, b11)):
        result = dot3(halves(block[...].reshape(HALF * HALF, LANES)), window, 0)
        for i in range(HALF):
            rows = pl.ds((HALF * xq + i) * PATCH + HALF * yq, HALF)
            real[rows, :] = result[HALF * i : HALF * (i + 1), :LANES]
            imag[rows, :] = result[HALF * i : HALF * (i + 1), LANES:]

    def strided(h, y):
        return pl.ds(SUB * PATCH * h + y, SUB, stride=PATCH)

    for h in range(4):
        out = dft32(lambda y: (real[strided(h, y), :] * TAPER[y], imag[strided(h, y), :] * TAPER[y]), -1)
        for k, (re, im) in enumerate(out):
            real[strided(h, k), :] = re
            imag[strided(h, k), :] = im

    energy = jnp.zeros((SUB, LANES), jnp.float32)
    for g in range(4):
        def rows(x):
            return pl.ds(x * PATCH + SUB * g, SUB)

        out = dft32(lambda x: (real[rows(x), :] * TAPER[x], imag[rows(x), :] * TAPER[x]), -1)
        scaled = []
        for k, (re, im) in enumerate(out):
            s = spectra_ref[rows(k), :]
            sre, sim = s * re, s * im
            energy = energy + (sre * re + sim * im)
            scaled.append((sre, sim))
        out = dft32(lambda k: scaled[k], 1)
        for x, (re, im) in enumerate(out):
            real[rows(x), :] = re * (TAPER[x] / PATCH**3)
            imag[rows(x), :] = im * (TAPER[x] / PATCH**3)

    field = b00[...]
    square = field * field
    rr = jnp.sum(square)
    dd = jnp.sum(square * damping_ref[...]) + jnp.sum(energy) * (1.0 / PATCH**3)
    lane = lax.broadcasted_iota(jnp.int32, sums_ref.shape, len(sums_ref.shape) - 1)
    sums_ref[...] = jnp.where(lane == 0, rr, jnp.where(lane == 1, dd, 0.0))

    for h in range(4):
        out = dft32(lambda k: (real[strided(h, k), :], imag[strided(h, k), :]), 1)
        for y, (re, im) in enumerate(out):
            real[strided(h, y), :] = re * TAPER[y]
            imag[strided(h, y), :] = im * TAPER[y]

    for xq in range(2):
        rows = pl.ds(xq * 512, 512)
        both = jnp.concatenate([real[rows, :], imag[rows, :]], axis=1)
        result = dot3(halves(both), window, 1).reshape(HALF, PATCH, LANES)
        near, far = ((o00, o01), (o10, o11))[xq]
        near[...] = result[:, :HALF]
        far[...] = result[:, HALF:]


def patches(shift, spectra, damping, blocks):
    block = jax.ShapeDtypeStruct(blocks[0].shape, jnp.float32)
    vmem = pl.BlockSpec(memory_space=VMEM)
    return pl.pallas_call(
        patches_kernel,
        out_shape=[block] * 4 + [jax.ShapeDtypeStruct((256, 1, LANES), jnp.float32)],
        in_specs=[pl.BlockSpec(memory_space=pltpu.SMEM)] + [vmem] * 7,
        out_specs=[vmem] * 5,
        scratch_shapes=[VMEM((PATCH * PATCH, LANES), jnp.float32)] * 2,
        compiler_params=pltpu.CompilerParams(vmem_limit_bytes=32 * 2**20),
        cost_estimate=pl.CostEstimate(flops=800_000_000, bytes_accessed=4_000_000, transcendentals=0),
        name="patches",
    )(shift, z_table(), spectra, damping, *blocks)


def finish_kernel(sums_ref, rhs_ref, damping_ref, own, r10, r01, r11, solution_ref, residual_ref):
    totals = jnp.sum(sums_ref[...], axis=(0, 1), keepdims=True)[0]
    lane = lax.broadcasted_iota(jnp.int32, totals.shape, 1)
    rr = jnp.sum(jnp.where(lane == 0, totals, 0.0), axis=1, keepdims=True)
    dd = jnp.sum(jnp.where(lane == 1, totals, 0.0), axis=1, keepdims=True)
    alpha = (rr / dd)[None]
    rhs = rhs_ref[...]
    image = ((own[...] + r10[...]) + (r01[...] + r11[...])) + damping_ref[...] * rhs
    solution_ref[...] = alpha * rhs
    residual_ref[...] = rhs - alpha * image


def finish(sums, rhs, damping, parts):
    block = jax.ShapeDtypeStruct(rhs.shape, jnp.float32)
    vmem = pl.BlockSpec(memory_space=VMEM)
    return pl.pallas_call(
        finish_kernel,
        out_shape=[block, block],
        in_specs=[vmem] * 7,
        out_specs=[vmem] * 2,
        compiler_params=pltpu.CompilerParams(vmem_limit_bytes=8 * 2**20),
        cost_estimate=pl.CostEstimate(flops=1_000_000, bytes_accessed=1_000_000, transcendentals=0),
        name="finish",
    )(sums, rhs, damping, *parts)


def moved(x, by_x, by_y):
    nx, ny = lax.axis_size("gx"), lax.axis_size("gy")
    pairs = [
        (i * ny + j, (i + by_x) * ny + j + by_y)
        for i in range(nx)
        for j in range(ny)
        if 0 <= i + by_x < nx and 0 <= j + by_y < ny
    ]
    return lax.ppermute(x, ("gx", "gy"), pairs)


def body(migrated, prior_sample, damping, psf_bank, psf_index, z_shift):
    rhs = migrated + damping * prior_sample
    halo = [moved(rhs, -1, 0), moved(rhs, 0, -1), moved(rhs, -1, -1)]
    spectra = spectra_of(psf_index.reshape(NPZ), psf_bank)
    own, o10, o01, o11, sums = patches(z_shift.reshape(1), spectra, damping, [rhs] + halo)
    sums = lax.all_to_all(sums, ("gx", "gy"), 0, 0)
    back = [moved(o10, 1, 0), moved(o01, 0, 1), moved(o11, 1, 1)]
    return tuple(finish(sums, rhs, damping, [own] + back))


def solution(mesh):
    block = P("gx", "gy", None)
    return jax.shard_map(
        body,
        mesh=mesh,
        in_specs=(block, block, block, P(), block, P("gx", "gy")),
        out_specs=(block, block),
        check_vma=False,
    )
```

profile of v0, /device:TPU:27, one launch (start us, length us, event | category | flops | bytes accessed | tf_op | source)
XLA Modules:
  0.0 59.5 jit_solution(8641241879166957442)
XLA Ops:
  0.6 0.0 copy-start.3
  0.6 0.0 copy-start
  0.7 1.1 %multiply_add_fusion.b00.rhs_ref = f32[16,16,128]{2,1,0:T(8,128)S(1)} fusion(f32[16,16,128]{2,1,0:T(8,128)} %param.8, f32[16,16,128]{2,1,0:T(8,128)} %damping_ref.3, f32[16,16,128]{2,1,0:T(8,128)} %param.9), kind=kLoop, calls=%fused_computation | loop fusion | flops 65536 | bytes 524288 | tf_op jit(solution)/shard_map/add | solution.py:277
  1.8 6.8 %collective-permute-start.2 = (f32[16,16,128]{2,1,0:T(8,128)S(1)}, f32[16,16,128]{2,1,0:T(8,128)S(1)}, u32[]{:S(2)}, u32[]{:S(2)}) collective-permute-start(f32[16,16,128]{2,1,0:T(8,128)S(1)} %multiply_add_fusion.b00.rhs_ref), channel_id=1, source_target_pairs={{17,0},{18,1},{19,2},{20,3},{21,4},{22,5},{23,6},{24,7},{25,8},{26... | collective-permute-start | bytes 393224 | tf_op jit(solution)/shard_map/ppermute | solution.py:273
  8.5 1.9 %collective-permute-start.1 = (f32[16,16,128]{2,1,0:T(8,128)S(1)}, f32[16,16,128]{2,1,0:T(8,128)S(1)}, u32[]{:S(2)}, u32[]{:S(2)}) collective-permute-start(f32[16,16,128]{2,1,0:T(8,128)S(1)} %multiply_add_fusion.b00.rhs_ref), channel_id=1, source_target_pairs={{1,0},{2,1},{3,2},{4,3},{5,4},{6,5},{7,6},{8,7},{9,8},{10,9},{11,1... | collective-permute-start | bytes 393224 | tf_op jit(solution)/shard_map/ppermute | solution.py:273
  10.5 2.0 %collective-permute-start = (f32[16,16,128]{2,1,0:T(8,128)S(1)}, f32[16,16,128]{2,1,0:T(8,128)S(1)}, u32[]{:S(2)}, u32[]{:S(2)}) collective-permute-start(f32[16,16,128]{2,1,0:T(8,128)S(1)} %multiply_add_fusion.b00.rhs_ref), channel_id=1, source_target_pairs={{16,0},{17,1},{18,2},{19,3},{20,4},{21,5},{22,6},{23,7},{24,8},{25... | collective-permute-start | bytes 393224 | tf_op jit(solution)/shard_map/ppermute | solution.py:273
  13.2 0.0 copy-start.1
  13.2 0.9 %copy-done.1 = f32[6,32,256]{2,1,0:T(8,128)S(1)} copy-done((f32[6,32,256]{2,1,0:T(8,128)S(1)}, f32[6,32,256]{2,1,0:T(8,128)}, u32[]{:S(2)}) %copy-start.1) | copy-done | bytes 196632
  14.1 0.0 copy-start.2
  14.1 0.7 %copy-done.2 = s32[1,1,6]{2,1,0:T(1,128)S(1)} copy-done((s32[1,1,6]{2,1,0:T(1,128)S(1)}, s32[1,1,6]{2,1,0:T(1,128)}, u32[]{:S(2)}) %copy-start.2) | copy-done | bytes 48
  14.7 5.1 %spectra.1.spectra_ref = f32[1024,128]{1,0:T(8,128)S(1)} custom-call(s32[6]{0:T(128)S(1)} %bitcast.3, f32[32,32,32,32]{3,2,1,0:T(8,128)} %bank_ref.1, f32[6,32,256]{2,1,0:T(8,128)S(1)} %copy-done.1), custom_call_target="tpu_custom_call" | custom-call | flops 400000000 | bytes 8000000 | tf_op jit(solution)/shard_map/spectra/pallas_call | solution.py:146
  19.9 0.0 collective-permute-done.2.b11
  19.9 2.2 %collective-permute-done.1.b01 = f32[16,16,128]{2,1,0:T(8,128)S(1)} collective-permute-done((f32[16,16,128]{2,1,0:T(8,128)S(1)}, f32[16,16,128]{2,1,0:T(8,128)S(1)}, u32[]{:S(2)}, u32[]{:S(2)}) %collective-permute-start.1) | collective-permute-done | bytes 131104 | tf_op jit(solution)/shard_map/ppermute | solution.py:273
  22.1 0.0 collective-permute-done.b10
  22.1 0.0 copy-done.3
  22.1 0.0 copy-done
  22.1 5.5 %patches.1 = (f32[16,16,128]{2,1,0:T(8,128)S(1)}, f32[16,16,128]{2,1,0:T(8,128)S(1)}, f32[16,16,128]{2,1,0:T(8,128)S(1)}, f32[16,16,128]{2,1,0:T(8,128)S(1)}, f32[256,1,128]{2,1,0:T(1,128)}) custom-call(s32[1]{0:T(128)} %bitcast.2.shift_ref, f32[160,256]{1,0:T(8,128)S(1)} %copy-done.3, f32[1024,128]{1,0:T(8,128)S(1)} %spectra.1.spectra_ref, ...), custom_call_target="tpu_custom_call" | custom-call | flops 800000000 | bytes 4000000 | tf_op jit(solution)/shard_map/patches/pallas_call | solution.py:227
  27.6 11.0 %all-to-all-start = ((f32[256,1,128]{2,1,0:T(1,128)}), f32[256,1,128]{2,1,0:T(1,128)S(1)}, u32[]{:S(2)}, u32[]{:S(2)}) async-start(f32[256,1,128]{2,1,0:T(1,128)} %get-tuple-element.7), calls=%async_computation | async-start | bytes 262144 | tf_op jit(solution)/shard_map/all_to_all | solution.py:281
  38.6 3.4 %collective-permute-start.3 = (f32[16,16,128]{2,1,0:T(8,128)S(1)}, f32[16,16,128]{2,1,0:T(8,128)S(1)}, u32[]{:S(2)}, u32[]{:S(2)}) collective-permute-start(f32[16,16,128]{2,1,0:T(8,128)S(1)} %get-tuple-element.9), channel_id=1, source_target_pairs={{0,16},{1,17},{2,18},{3,19},{4,20},{5,21},{6,22},{7,23},{8,24},{9,... | collective-permute-start | bytes 393224 | tf_op jit(solution)/shard_map/ppermute | solution.py:273
  42.0 7.5 %collective-permute-start.4 = (f32[16,16,128]{2,1,0:T(8,128)S(1)}, f32[16,16,128]{2,1,0:T(8,128)S(1)}, u32[]{:S(2)}, u32[]{:S(2)}) collective-permute-start(f32[16,16,128]{2,1,0:T(8,128)S(1)} %get-tuple-element.10), channel_id=1, source_target_pairs={{0,1},{1,2},{2,3},{3,4},{4,5},{5,6},{6,7},{7,8},{8,9},{9,10},{10,1... | collective-permute-start | bytes 393224 | tf_op jit(solution)/shard_map/ppermute | solution.py:273
  49.5 1.9 %collective-permute-start.5 = (f32[16,16,128]{2,1,0:T(8,128)S(1)}, f32[16,16,128]{2,1,0:T(8,128)S(1)}, u32[]{:S(2)}, u32[]{:S(2)}) collective-permute-start(f32[16,16,128]{2,1,0:T(8,128)S(1)} %get-tuple-element.11), channel_id=1, source_target_pairs={{0,17},{1,18},{2,19},{3,20},{4,21},{5,22},{6,23},{7,24},{8,25},{9,... | collective-permute-start | bytes 393224 | tf_op jit(solution)/shard_map/ppermute | solution.py:273
  51.4 0.0 collective-permute-done.3.r10
  51.4 0.0 collective-permute-done.4.r01
  51.4 7.0 %collective-permute-done.5.r11 = f32[16,16,128]{2,1,0:T(8,128)S(1)} collective-permute-done((f32[16,16,128]{2,1,0:T(8,128)S(1)}, f32[16,16,128]{2,1,0:T(8,128)S(1)}, u32[]{:S(2)}, u32[]{:S(2)}) %collective-permute-start.5) | collective-permute-done | bytes 131104 | tf_op jit(solution)/shard_map/ppermute | solution.py:273
  58.5 0.0 all-to-all-done.sums_ref
  58.5 1.1 %finish.1 = (f32[16,16,128]{2,1,0:T(8,128)}, f32[16,16,128]{2,1,0:T(8,128)}) custom-call(f32[256,1,128]{2,1,0:T(1,128)S(1)} %all-to-all-done.sums_ref, f32[16,16,128]{2,1,0:T(8,128)S(1)} %multiply_add_fusion.b00.rhs_ref, f32[16,16,128]{2,1,0:T(8,128)S(1)} %copy-done, f32[16,16,128]{2,1,0:T(8,128)S(1)} %get-tuple-element.8.own, ...), custom_call_target="tpu_custom_call" | custom-call | flops 1000000 | bytes 1000000 | tf_op jit(solution)/shard_map/finish/pallas_call | solution.py:254
Async XLA Ops:
  0.6 21.5 %copy-start.3 = (f32[160,256]{1,0:T(8,128)S(1)}, f32[160,256]{1,0:T(8,128)}, u32[]{:S(2)}) copy-start(f32[160,256]{1,0:T(8,128)} %constant.5.clone.table_ref) | copy-start | bytes 491524
  0.6 21.4 %copy-start = (f32[16,16,128]{2,1,0:T(8,128)S(1)}, f32[16,16,128]{2,1,0:T(8,128)}, u32[]{:S(2)}) copy-start(f32[16,16,128]{2,1,0:T(8,128)} %damping_ref.3) | copy-start | bytes 393220
  1.8 18.1 %collective-permute-start.2 = (f32[16,16,128]{2,1,0:T(8,128)S(1)}, f32[16,16,128]{2,1,0:T(8,128)S(1)}, u32[]{:S(2)}, u32[]{:S(2)}) collective-permute-start(f32[16,16,128]{2,1,0:T(8,128)S(1)} %multiply_add_fusion.b00.rhs_ref), channel_id=1, source_target_pairs={{17,0},{18,1},{19,2},{20,3},{21,4},{22,5},{23,6},{24,7},{25,8},{26... | collective-permute-start | bytes 393224 | tf_op jit(solution)/shard_map/ppermute | solution.py:273
  8.5 13.5 %collective-permute-start.1 = (f32[16,16,128]{2,1,0:T(8,128)S(1)}, f32[16,16,128]{2,1,0:T(8,128)S(1)}, u32[]{:S(2)}, u32[]{:S(2)}) collective-permute-start(f32[16,16,128]{2,1,0:T(8,128)S(1)} %multiply_add_fusion.b00.rhs_ref), channel_id=1, source_target_pairs={{1,0},{2,1},{3,2},{4,3},{5,4},{6,5},{7,6},{8,7},{9,8},{10,9},{11,1... | collective-permute-start | bytes 393224 | tf_op jit(solution)/shard_map/ppermute | solution.py:273
  10.5 11.6 %collective-permute-start = (f32[16,16,128]{2,1,0:T(8,128)S(1)}, f32[16,16,128]{2,1,0:T(8,128)S(1)}, u32[]{:S(2)}, u32[]{:S(2)}) collective-permute-start(f32[16,16,128]{2,1,0:T(8,128)S(1)} %multiply_add_fusion.b00.rhs_ref), channel_id=1, source_target_pairs={{16,0},{17,1},{18,2},{19,3},{20,4},{21,5},{22,6},{23,7},{24,8},{25... | collective-permute-start | bytes 393224 | tf_op jit(solution)/shard_map/ppermute | solution.py:273
  13.2 0.9 %copy-start.1 = (f32[6,32,256]{2,1,0:T(8,128)S(1)}, f32[6,32,256]{2,1,0:T(8,128)}, u32[]{:S(2)}) copy-start(f32[6,32,256]{2,1,0:T(8,128)} %constant.4.clone.pick_ref) | copy-start | bytes 589828
  14.1 0.7 %copy-start.2 = (s32[1,1,6]{2,1,0:T(1,128)S(1)}, s32[1,1,6]{2,1,0:T(1,128)}, u32[]{:S(2)}) copy-start(s32[1,1,6]{2,1,0:T(1,128)} %param.12) | copy-start | bytes 76
  27.6 30.9 %all-to-all-start = ((f32[256,1,128]{2,1,0:T(1,128)}), f32[256,1,128]{2,1,0:T(1,128)S(1)}, u32[]{:S(2)}, u32[]{:S(2)}) async-start(f32[256,1,128]{2,1,0:T(1,128)} %get-tuple-element.7), calls=%async_computation | async-start | bytes 262144 | tf_op jit(solution)/shard_map/all_to_all | solution.py:281
  38.6 12.8 %collective-permute-start.3 = (f32[16,16,128]{2,1,0:T(8,128)S(1)}, f32[16,16,128]{2,1,0:T(8,128)S(1)}, u32[]{:S(2)}, u32[]{:S(2)}) collective-permute-start(f32[16,16,128]{2,1,0:T(8,128)S(1)} %get-tuple-element.9), channel_id=1, source_target_pairs={{0,16},{1,17},{2,18},{3,19},{4,20},{5,21},{6,22},{7,23},{8,24},{9,... | collective-permute-start | bytes 393224 | tf_op jit(solution)/shard_map/ppermute | solution.py:273
  42.0 9.5 %collective-permute-start.4 = (f32[16,16,128]{2,1,0:T(8,128)S(1)}, f32[16,16,128]{2,1,0:T(8,128)S(1)}, u32[]{:S(2)}, u32[]{:S(2)}) collective-permute-start(f32[16,16,128]{2,1,0:T(8,128)S(1)} %get-tuple-element.10), channel_id=1, source_target_pairs={{0,1},{1,2},{2,3},{3,4},{4,5},{5,6},{6,7},{7,8},{8,9},{9,10},{10,1... | collective-permute-start | bytes 393224 | tf_op jit(solution)/shard_map/ppermute | solution.py:273
  49.5 9.0 %collective-permute-start.5 = (f32[16,16,128]{2,1,0:T(8,128)S(1)}, f32[16,16,128]{2,1,0:T(8,128)S(1)}, u32[]{:S(2)}, u32[]{:S(2)}) collective-permute-start(f32[16,16,128]{2,1,0:T(8,128)S(1)} %get-tuple-element.11), channel_id=1, source_target_pairs={{0,17},{1,18},{2,19},{3,20},{4,21},{5,22},{6,23},{7,24},{8,25},{9,... | collective-permute-start | bytes 393224 | tf_op jit(solution)/shard_map/ppermute | solution.py:273
where the time goes:
time: 59.9 us; the launch traced here: 59.5 us
  starting transfers between devices  34.6 us (58%)
  Pallas kernels  11.7 us (20%)
  waiting for transfers between devices  9.23 us (15%)
  local copies, waits for them, and re-layouts  1.59 us (3%)
  between operations  1.4 us (2%)
  other arithmetic  1.1 us (2%)
    ppermute x6, starting transfers between devices, moved(): return lax.ppermute(x, ('gx', 'gy'), pairs)  23.5 us
    all_to_all x1, starting transfers between devices, body(): sums = lax.all_to_all(sums, ('gx', 'gy'), 0, 0)  11 us
    ppermute x6, waiting for transfers between devices, moved(): return lax.ppermute(x, ('gx', 'gy'), pairs)  9.23 us
    pallas_call x1, Pallas kernels, patches(): pl.pallas_call(patches_kernel, out_shape=[block] * 4 + [jax.ShapeDtypeStr...  5.46 us
    pallas_call x1, Pallas kernels, spectra_of(): pl.pallas_call(spectra_kernel, out_shape=jax.ShapeDtypeStruct((PATCH * PA...  5.13 us
    unnamed x8, local copies, waits for them, and re-layouts  1.59 us
  transfers between devices with their start and end apart: 7, of which 2 were waited for; matrix products, arithmetic and copies ran while one was open for 0% of the time, Pallas kernels for 9%

commit v1 on v0

v1 whole, which is shorter than its diff:
```python
import math

import numpy as np
import jax
import jax.numpy as jnp
from jax import lax
from jax.experimental import pallas as pl
from jax.experimental.pallas import tpu as pltpu
from jax.sharding import PartitionSpec as P

PATCH = 32
HALF = 16
NPZ = 6
KZ = 17
LANES = 128
SUB = 8
VMEM = pltpu.VMEM


def z_table():
    table = np.zeros((160, 2 * LANES))
    taper = np.sin(math.pi * (np.arange(PATCH) + 0.5) / PATCH)
    for p in range(NPZ):
        for cell in range(PATCH):
            for kz in range(KZ):
                phase = 2.0 * math.pi * (kz * cell % PATCH) / PATCH
                row = 16 + 16 * p + cell
                table[row, KZ * p + kz] = taper[cell] * math.cos(phase)
                if 0 < kz < HALF:
                    table[row, LANES + KZ * p + kz] = -taper[cell] * math.sin(phase)
    return table.astype(np.float32)


TAPER = [math.sin(math.pi * (i + 0.5) / PATCH) for i in range(PATCH)]


def twiddle(value, k, n, sign):
    k %= n
    re, im = value
    if k == 0:
        return value
    if 4 * k == n:
        return (-im, re) if sign > 0 else (im, -re)
    if 2 * k == n:
        return (-re, -im)
    if 4 * k == 3 * n:
        return (im, -re) if sign > 0 else (-im, re)
    c = math.cos(2.0 * math.pi * k / n)
    s = sign * math.sin(2.0 * math.pi * k / n)
    if 8 * k % n == 0:
        h = abs(c)
        cs, ss = (1 if c > 0 else -1), (1 if s > 0 else -1)
        if cs == ss:
            a, b = re - im, re + im
            return (a * (h * cs), b * (h * cs))
        a, b = re + im, im - re
        return (a * (h * cs), b * (h * cs))
    return (re * c - im * s, re * s + im * c)


def add(a, b):
    return (a[0] + b[0], a[1] + b[1])


def sub(a, b):
    return (a[0] - b[0], a[1] - b[1])


def dft4(x, sign):
    a, b = add(x[0], x[2]), sub(x[0], x[2])
    c, d = add(x[1], x[3]), twiddle(sub(x[1], x[3]), 1, 4, sign)
    return [add(a, c), add(b, d), sub(a, c), sub(b, d)]


def dft8(x, sign):
    even = dft4(x[0::2], sign)
    odd = [twiddle(v, k, 8, sign) for k, v in enumerate(dft4(x[1::2], sign))]
    return [add(even[k], odd[k]) for k in range(4)] + [sub(even[k], odd[k]) for k in range(4)]


def dft32(load, sign):
    first = []
    for n2 in range(8):
        part = dft4([load(8 * n1 + n2) for n1 in range(4)], sign)
        first.append([twiddle(v, n2 * k1, 32, sign) for k1, v in enumerate(part)])
    out = [None] * 32
    for k1 in range(4):
        part = dft8([first[n2][k1] for n2 in range(8)], sign)
        for k2 in range(8):
            out[k1 + 4 * k2] = part[k2]
    return out


def halves(value):
    high = value.astype(jnp.bfloat16)
    return high, (value - high.astype(jnp.float32)).astype(jnp.bfloat16)


def dot(a, b, contract_b):
    return lax.dot_general(a, b, (((1,), (contract_b,)), ((), ())), preferred_element_type=jnp.float32)


def dot3(a, b, contract_b):
    return dot(a[0], b[0], contract_b) + (dot(a[1], b[0], contract_b) + dot(a[0], b[1], contract_b))


def prepare_kernel(index_ref, shift_ref, bank_ref, table_ref, block_ref,
                   spectra_ref, window_ref, own_ref, cubes, back, sems):
    copies = [
        pltpu.make_async_copy(bank_ref.at[index_ref[p]], cubes.at[p], sems.at[p]) for p in range(NPZ)
    ]
    for copy in copies:
        copy.start()

    window = pltpu.roll(table_ref[...], shift_ref[0] + 144, 0)[:LANES]
    window_ref[...] = window
    own_ref[...] = dot3(halves(block_ref[...].reshape(HALF * HALF, LANES)), halves(window), 0)

    source = lax.broadcasted_iota(jnp.int32, (NPZ * PATCH, 2 * LANES), 0)
    lane = lax.broadcasted_iota(jnp.int32, (NPZ * PATCH, 2 * LANES), 1)
    p, kz = source // PATCH, source % PATCH
    target = jnp.where(kz < KZ, KZ * p + kz, LANES + KZ * p + PATCH - kz)
    pick = jnp.where(lane == target, 1.0, 0.0).astype(jnp.bfloat16)

    for copy in copies:
        copy.wait()
    total = None
    for first, last in ((0, 4), (4, NPZ)):
        joined = jnp.concatenate(
            [cubes[q].reshape(PATCH * PATCH, PATCH) for q in range(first, last)], axis=1
        )
        high, low = halves(joined)
        rows = pick[PATCH * first : PATCH * last]
        part = dot(high, rows, 0) + dot(low, rows, 0)
        total = part if total is None else total + part
    spectra_ref[...] = total[:, :LANES]
    back[...] = total[:, LANES:]
    row = lax.broadcasted_iota(jnp.int32, (SUB, LANES), 0)
    mirror = (SUB - row) % SUB
    for kx in range(PATCH):
        other = (PATCH - kx) % PATCH
        turned = [
            jnp.take_along_axis(
                back[pl.ds(other * PATCH + SUB * g, SUB), :], mirror, axis=0, mode="promise_in_bounds"
            )
            for g in range(4)
        ]
        for g in range(4):
            rows = pl.ds(kx * PATCH + SUB * g, SUB)
            mirrored = jnp.where(row == 0, turned[(4 - g) % 4], turned[3 - g])
            spectra_ref[rows, :] = spectra_ref[rows, :] + mirrored


def prepare(index, shift, bank, rhs):
    smem = pl.BlockSpec(memory_space=pltpu.SMEM)
    vmem = pl.BlockSpec(memory_space=VMEM)
    return pl.pallas_call(
        prepare_kernel,
        out_shape=[
            jax.ShapeDtypeStruct((PATCH * PATCH, LANES), jnp.float32),
            jax.ShapeDtypeStruct((LANES, 2 * LANES), jnp.float32),
            jax.ShapeDtypeStruct((HALF * HALF, 2 * LANES), jnp.float32),
        ],
        in_specs=[smem, smem, pl.BlockSpec(memory_space=pltpu.HBM), vmem, vmem],
        out_specs=[vmem] * 3,
        scratch_shapes=[
            VMEM((NPZ, PATCH, PATCH, PATCH), jnp.float32),
            VMEM((PATCH * PATCH, LANES), jnp.float32),
            pltpu.SemaphoreType.DMA((NPZ,)),
        ],
        compiler_params=pltpu.CompilerParams(vmem_limit_bytes=50 * 2**20),
        cost_estimate=pl.CostEstimate(flops=400_000_000, bytes_accessed=8_000_000, transcendentals=0),
        name="prepare",
    )(index, shift, bank, z_table(), rhs)


PITCH = 40


def patches_kernel(window_ref, spectra_ref, own_ref, b10, b01, b11,
                   o10, o01, o11, near_ref, energy_ref, real, imag):
    window = halves(window_ref[...])

    for xq, yq, block in ((0, 0, None), (1, 0, b10), (0, 1, b01), (1, 1, b11)):
        if block is None:
            result = own_ref[...]
        else:
            result = dot3(halves(block[...].reshape(HALF * HALF, LANES)), window, 0)
        for i in range(HALF):
            rows = pl.ds((HALF * xq + i) * PITCH + HALF * yq, HALF)
            real[rows, :] = result[HALF * i : HALF * (i + 1), :LANES]
            imag[rows, :] = result[HALF * i : HALF * (i + 1), LANES:]

    def strided(h, y):
        return pl.ds(SUB * PITCH * h + y, SUB, stride=PITCH)

    for h in range(4):
        out = dft32(lambda y: (real[strided(h, y), :] * TAPER[y], imag[strided(h, y), :] * TAPER[y]), -1)
        for k, (re, im) in enumerate(out):
            real[strided(h, k), :] = re
            imag[strided(h, k), :] = im

    energy = jnp.zeros((SUB, LANES), jnp.float32)
    for g in range(4):
        def rows(x):
            return pl.ds(x * PITCH + SUB * g, SUB)

        out = dft32(lambda x: (real[rows(x), :] * TAPER[x], imag[rows(x), :] * TAPER[x]), -1)
        scaled = []
        for k, (re, im) in enumerate(out):
            s = spectra_ref[pl.ds(k * PATCH + SUB * g, SUB), :]
            sre, sim = s * re, s * im
            energy = energy + (sre * re + sim * im)
            scaled.append((sre, sim))
        out = dft32(lambda k: scaled[k], 1)
        for x, (re, im) in enumerate(out):
            real[rows(x), :] = re * (TAPER[x] / PATCH**3)
            imag[rows(x), :] = im * (TAPER[x] / PATCH**3)
    energy_ref[...] = energy

    for h in range(4):
        out = dft32(lambda k: (real[strided(h, k), :], imag[strided(h, k), :]), 1)
        for y, (re, im) in enumerate(out):
            real[strided(h, y), :] = re * TAPER[y]
            imag[strided(h, y), :] = im * TAPER[y]

    for xq, yq, out in ((0, 0, near_ref), (1, 1, o11), (0, 1, o01), (1, 0, o10)):
        pieces = []
        for i in range(HALF):
            rows = pl.ds((HALF * xq + i) * PITCH + HALF * yq, HALF)
            pieces.append(jnp.concatenate([real[rows, :], imag[rows, :]], axis=1))
        both = jnp.concatenate(pieces, axis=0)
        if out is near_ref:
            near_ref[...] = both
        else:
            out[...] = dot3(halves(both), window, 1).reshape(HALF, HALF, LANES)


def patches(window, spectra, own, blocks):
    block = jax.ShapeDtypeStruct(blocks[0].shape, jnp.float32)
    vmem = pl.BlockSpec(memory_space=VMEM)
    return pl.pallas_call(
        patches_kernel,
        out_shape=[block] * 3
        + [jax.ShapeDtypeStruct(own.shape, jnp.float32), jax.ShapeDtypeStruct((SUB, LANES), jnp.float32)],
        in_specs=[vmem] * 6,
        out_specs=[vmem] * 5,
        scratch_shapes=[VMEM((PATCH * PITCH, LANES), jnp.float32)] * 2,
        compiler_params=pltpu.CompilerParams(vmem_limit_bytes=32 * 2**20),
        cost_estimate=pl.CostEstimate(flops=800_000_000, bytes_accessed=4_000_000, transcendentals=0),
        name="patches",
    )(window, spectra, own, *blocks)


def near_kernel(window_ref, near_ref, energy_ref, rhs_ref, damping_ref, image_ref, sums_ref):
    field = rhs_ref[...]
    square = field * field
    damped = damping_ref[...]
    rr = jnp.sum(square)
    dd = jnp.sum(square * damped) + jnp.sum(energy_ref[...]) * (1.0 / PATCH**3)
    lane = lax.broadcasted_iota(jnp.int32, sums_ref.shape, len(sums_ref.shape) - 1)
    sums_ref[...] = jnp.where(lane == 0, rr, jnp.where(lane == 1, dd, 0.0))
    own = dot3(halves(near_ref[...]), halves(window_ref[...]), 1)
    image_ref[...] = own.reshape(field.shape) + damped * field


def near(window, inner, energy, rhs, damping):
    vmem = pl.BlockSpec(memory_space=VMEM)
    return pl.pallas_call(
        near_kernel,
        out_shape=[
            jax.ShapeDtypeStruct(rhs.shape, jnp.float32),
            jax.ShapeDtypeStruct((256, 1, 2), jnp.float32),
        ],
        in_specs=[vmem] * 5,
        out_specs=[vmem] * 2,
        compiler_params=pltpu.CompilerParams(vmem_limit_bytes=32 * 2**20),
        cost_estimate=pl.CostEstimate(flops=20_000_000_000, bytes_accessed=40_000_000, transcendentals=0),
        name="near",
    )(window, inner, energy, rhs, damping)


def finish_kernel(sums_ref, rhs_ref, own, r10, r01, r11, solution_ref, residual_ref):
    totals = jnp.sum(sums_ref[...], axis=(0, 1), keepdims=True)[0]
    lane = lax.broadcasted_iota(jnp.int32, totals.shape, 1)
    rr = jnp.sum(jnp.where(lane == 0, totals, 0.0), axis=1, keepdims=True)
    dd = jnp.sum(jnp.where(lane == 1, totals, 0.0), axis=1, keepdims=True)
    alpha = (rr / dd)[None]
    rhs = rhs_ref[...]
    image = (own[...] + r10[...]) + (r01[...] + r11[...])
    solution_ref[...] = alpha * rhs
    residual_ref[...] = rhs - alpha * image


def finish(sums, rhs, parts):
    block = jax.ShapeDtypeStruct(rhs.shape, jnp.float32)
    vmem = pl.BlockSpec(memory_space=VMEM)
    return pl.pallas_call(
        finish_kernel,
        out_shape=[block, block],
        in_specs=[vmem] * 6,
        out_specs=[vmem] * 2,
        compiler_params=pltpu.CompilerParams(vmem_limit_bytes=8 * 2**20),
        cost_estimate=pl.CostEstimate(flops=1_000_000, bytes_accessed=1_000_000, transcendentals=0),
        name="finish",
    )(sums, rhs, *parts)


def moved(x, by_x, by_y):
    nx, ny = lax.axis_size("gx"), lax.axis_size("gy")
    pairs = [
        (i * ny + j, (i + by_x) * ny + j + by_y)
        for i in range(nx)
        for j in range(ny)
        if 0 <= i + by_x < nx and 0 <= j + by_y < ny
    ]
    return lax.ppermute(x, ("gx", "gy"), pairs)


def body(migrated, prior_sample, damping, psf_bank, psf_index, z_shift):
    rhs = migrated + damping * prior_sample
    halo = [moved(rhs, -1, 0), moved(rhs, 0, -1), moved(rhs, -1, -1)]
    spectra, window, own = prepare(psf_index.reshape(NPZ), z_shift.reshape(1), psf_bank, rhs)
    o10, o01, o11, inner, energy = patches(window, spectra, own, halo)
    back = [moved(o10, 1, 0), moved(o01, 0, 1), moved(o11, 1, 1)]
    image, sums = near(window, inner, energy, rhs, damping)
    sums = lax.all_to_all(sums, ("gx", "gy"), 0, 0)
    return tuple(finish(sums, rhs, [image] + back))


def solution(mesh):
    block = P("gx", "gy", None)
    return jax.shard_map(
        body,
        mesh=mesh,
        in_specs=(block, block, block, P(), block, P("gx", "gy")),
        out_specs=(block, block),
        check_vma=False,
    )
```

time: 59.9 us -> 63.5 us (1.060)
  the two profiles are of different devices: /device:TPU:27 before, /device:TPU:1 now
where the time goes in v1:
time: 63.5 us; the launch traced here: 63.2 us
  blocking collectives  31.8 us (50%)
  starting transfers between devices  19.5 us (31%)
  Pallas kernels  7.71 us (12%)
  local copies, waits for them, and re-layouts  1.57 us (2%)
  between operations  1.4 us (2%)
  other arithmetic  1.09 us (2%)
    all_to_all x1, blocking collectives, body(): sums = lax.all_to_all(sums, ('gx', 'gy'), 0, 0)  31.8 us
    ppermute x6, starting transfers between devices, moved(): return lax.ppermute(x, ('gx', 'gy'), pairs)  19.5 us
    pallas_call x1, Pallas kernels, prepare(): pl.pallas_call(prepare_kernel, out_shape=[jax.ShapeDtypeStruct((PATCH * P...  3.58 us
    pallas_call x1, Pallas kernels, patches(): pl.pallas_call(patches_kernel, out_shape=[block] * 3 + [jax.ShapeDtypeStr...  2.73 us
    unnamed x6, local copies, waits for them, and re-layouts  1.57 us
  transfers between devices with their start and end apart: 6, of which 0 were waited for; matrix products, arithmetic and copies ran while one was open for 0% of the time, Pallas kernels for 6%

profile of v1, /device:TPU:1, one launch (start us, length us, event | category | flops | bytes accessed | tf_op | source)
XLA Modules:
  0.0 63.2 jit_solution(12940514057250503695)
XLA Ops:
  0.6 0.0 copy-start.1
  0.6 1.1 %multiply_add_fusion.block_ref.rhs_ref = f32[16,16,128]{2,1,0:T(8,128)S(1)} fusion(f32[16,16,128]{2,1,0:T(8,128)} %param.7, f32[16,16,128]{2,1,0:T(8,128)} %damping_ref.1, f32[16,16,128]{2,1,0:T(8,128)} %param.8), kind=kLoop, calls=%fused_computation | loop fusion | flops 65536 | bytes 524288 | tf_op jit(solution)/shard_map/add | solution.py:321
  1.7 1.3 %collective-permute-start.2 = (f32[16,16,128]{2,1,0:T(8,128)S(1)}, f32[16,16,128]{2,1,0:T(8,128)S(1)}, u32[]{:S(2)}, u32[]{:S(2)}) collective-permute-start(f32[16,16,128]{2,1,0:T(8,128)S(1)} %multiply_add_fusion.block_ref.rhs_ref), channel_id=1, source_target_pairs={{17,0},{18,1},{19,2},{20,3},{21,4},{22,5},{23,6},{24,7},{25,8},{26... | collective-permute-start | bytes 393224 | tf_op jit(solution)/shard_map/ppermute | solution.py:317
  3.0 5.1 %collective-permute-start.1 = (f32[16,16,128]{2,1,0:T(8,128)S(1)}, f32[16,16,128]{2,1,0:T(8,128)S(1)}, u32[]{:S(2)}, u32[]{:S(2)}) collective-permute-start(f32[16,16,128]{2,1,0:T(8,128)S(1)} %multiply_add_fusion.block_ref.rhs_ref), channel_id=1, source_target_pairs={{1,0},{2,1},{3,2},{4,3},{5,4},{6,5},{7,6},{8,7},{9,8},{10,9},{11,1... | collective-permute-start | bytes 393224 | tf_op jit(solution)/shard_map/ppermute | solution.py:317
  8.2 1.3 %collective-permute-start = (f32[16,16,128]{2,1,0:T(8,128)S(1)}, f32[16,16,128]{2,1,0:T(8,128)S(1)}, u32[]{:S(2)}, u32[]{:S(2)}) collective-permute-start(f32[16,16,128]{2,1,0:T(8,128)S(1)} %multiply_add_fusion.block_ref.rhs_ref), channel_id=1, source_target_pairs={{16,0},{17,1},{18,2},{19,3},{20,4},{21,5},{22,6},{23,7},{24,8},{25... | collective-permute-start | bytes 393224 | tf_op jit(solution)/shard_map/ppermute | solution.py:317
  10.1 0.0 copy-start
  10.2 0.9 %copy-done = f32[160,256]{1,0:T(8,128)S(1)} copy-done((f32[160,256]{1,0:T(8,128)S(1)}, f32[160,256]{1,0:T(8,128)}, u32[]{:S(2)}) %copy-start) | copy-done | bytes 163864
  11.1 0.0 copy-start.2
  11.1 0.7 %copy-done.2 = s32[1,1,6]{2,1,0:T(1,128)S(1)} copy-done((s32[1,1,6]{2,1,0:T(1,128)S(1)}, s32[1,1,6]{2,1,0:T(1,128)}, u32[]{:S(2)}) %copy-start.2) | copy-done | bytes 48
  11.7 3.6 %prepare.1 = (f32[1024,128]{1,0:T(8,128)S(1)}, f32[128,256]{1,0:T(8,128)S(1)}, f32[256,256]{1,0:T(8,128)S(1)}) custom-call(s32[6]{0:T(128)S(1)} %bitcast.3, s32[1]{0:T(128)} %bitcast.2.shift_ref, f32[32,32,32,32]{3,2,1,0:T(8,128)} %bank_ref.1, f32[160,256]{1,0:T(8,128)S(1)} %copy-done, f32[16,16,128]{2,1,0:T(8,128)S(1)} %multiply_add_fusion.block_ref.rhs_ref), custom_call_target="tpu_custom_call" | custom-call | flops 400000000 | bytes 8000000 | tf_op jit(solution)/shard_map/prepare/pallas_call | solution.py:157
  15.3 0.0 collective-permute-done.2.b11
  15.3 0.0 collective-permute-done.1.b01
  15.3 0.0 collective-permute-done.b10
  15.3 2.7 %patches.1 = (f32[16,16,128]{2,1,0:T(8,128)S(1)}, f32[16,16,128]{2,1,0:T(8,128)S(1)}, f32[16,16,128]{2,1,0:T(8,128)S(1)}, f32[256,256]{1,0:T(8,128)S(1)}, f32[8,128]{1,0:T(8,128)S(1)}) custom-call(f32[128,256]{1,0:T(8,128)S(1)} %get-tuple-element.12.window_ref, f32[1024,128]{1,0:T(8,128)S(1)} %get-tuple-element.13.spectra_ref, ...), custom_call_target="tpu_custom_call" | custom-call | flops 800000000 | bytes 4000000 | tf_op jit(solution)/shard_map/patches/pallas_call | solution.py:242
  18.1 4.5 %collective-permute-start.3 = (f32[16,16,128]{2,1,0:T(8,128)S(1)}, f32[16,16,128]{2,1,0:T(8,128)S(1)}, u32[]{:S(2)}, u32[]{:S(2)}) collective-permute-start(f32[16,16,128]{2,1,0:T(8,128)S(1)} %get-tuple-element.19), channel_id=1, source_target_pairs={{0,16},{1,17},{2,18},{3,19},{4,20},{5,21},{6,22},{7,23},{8,24},{9,... | collective-permute-start | bytes 393224 | tf_op jit(solution)/shard_map/ppermute | solution.py:317
  22.6 3.9 %collective-permute-start.4 = (f32[16,16,128]{2,1,0:T(8,128)S(1)}, f32[16,16,128]{2,1,0:T(8,128)S(1)}, u32[]{:S(2)}, u32[]{:S(2)}) collective-permute-start(f32[16,16,128]{2,1,0:T(8,128)S(1)} %get-tuple-element.20), channel_id=1, source_target_pairs={{0,1},{1,2},{2,3},{3,4},{4,5},{5,6},{6,7},{7,8},{8,9},{9,10},{10,1... | collective-permute-start | bytes 393224 | tf_op jit(solution)/shard_map/ppermute | solution.py:317
  26.5 3.4 %collective-permute-start.5 = (f32[16,16,128]{2,1,0:T(8,128)S(1)}, f32[16,16,128]{2,1,0:T(8,128)S(1)}, u32[]{:S(2)}, u32[]{:S(2)}) collective-permute-start(f32[16,16,128]{2,1,0:T(8,128)S(1)} %get-tuple-element.21), channel_id=1, source_target_pairs={{0,17},{1,18},{2,19},{3,20},{4,21},{5,22},{6,23},{7,24},{8,25},{9,... | collective-permute-start | bytes 393224 | tf_op jit(solution)/shard_map/ppermute | solution.py:317
  29.9 0.0 copy-done.1
  29.9 0.3 near.1
  30.2 31.8 %all_to_all.5.sums_ref = f32[256,1,2]{2,1,0:T(1,128)S(1)} all-to-all(f32[256,1,2]{2,1,0:T(1,128)S(1)} %get-tuple-element.17), channel_id=1, replica_groups=mesh['gx'=16,'gy'=16] {'gx','gy'}, dimensions={0} | all-to-all | bytes 4096 | tf_op jit(solution)/shard_map/all_to_all | solution.py:327
  62.1 0.0 collective-permute-done.3.r10
  62.1 0.0 collective-permute-done.4.r01
  62.1 0.0 collective-permute-done.5.r11
  62.1 1.1 %finish.1 = (f32[16,16,128]{2,1,0:T(8,128)}, f32[16,16,128]{2,1,0:T(8,128)}) custom-call(f32[256,1,2]{2,1,0:T(1,128)S(1)} %all_to_all.5.sums_ref, f32[16,16,128]{2,1,0:T(8,128)S(1)} %multiply_add_fusion.block_ref.rhs_ref, f32[16,16,128]{2,1,0:T(8,128)S(1)} %get-tuple-element.18.own, f32[16,16,128]{2,1,0:T(8,128)S(1)} %collective-permute-done.3.r10, ...), custom_call_target="tpu_custom_call" | custom-call | flops 1000000 | bytes 1000000 | tf_op jit(solution)/shard_map/finish/pallas_call | solution.py:298
Async XLA Ops:
  0.6 29.3 %copy-start.1 = (f32[16,16,128]{2,1,0:T(8,128)S(1)}, f32[16,16,128]{2,1,0:T(8,128)}, u32[]{:S(2)}) copy-start(f32[16,16,128]{2,1,0:T(8,128)} %damping_ref.1) | copy-start | bytes 393220
  1.7 13.6 %collective-permute-start.2 = (f32[16,16,128]{2,1,0:T(8,128)S(1)}, f32[16,16,128]{2,1,0:T(8,128)S(1)}, u32[]{:S(2)}, u32[]{:S(2)}) collective-permute-start(f32[16,16,128]{2,1,0:T(8,128)S(1)} %multiply_add_fusion.block_ref.rhs_ref), channel_id=1, source_target_pairs={{17,0},{18,1},{19,2},{20,3},{21,4},{22,5},{23,6},{24,7},{25,8},{26... | collective-permute-start | bytes 393224 | tf_op jit(solution)/shard_map/ppermute | solution.py:317
  3.0 12.3 %collective-permute-start.1 = (f32[16,16,128]{2,1,0:T(8,128)S(1)}, f32[16,16,128]{2,1,0:T(8,128)S(1)}, u32[]{:S(2)}, u32[]{:S(2)}) collective-permute-start(f32[16,16,128]{2,1,0:T(8,128)S(1)} %multiply_add_fusion.block_ref.rhs_ref), channel_id=1, source_target_pairs={{1,0},{2,1},{3,2},{4,3},{5,4},{6,5},{7,6},{8,7},{9,8},{10,9},{11,1... | collective-permute-start | bytes 393224 | tf_op jit(solution)/shard_map/ppermute | solution.py:317
  8.2 7.1 %collective-permute-start = (f32[16,16,128]{2,1,0:T(8,128)S(1)}, f32[16,16,128]{2,1,0:T(8,128)S(1)}, u32[]{:S(2)}, u32[]{:S(2)}) collective-permute-start(f32[16,16,128]{2,1,0:T(8,128)S(1)} %multiply_add_fusion.block_ref.rhs_ref), channel_id=1, source_target_pairs={{16,0},{17,1},{18,2},{19,3},{20,4},{21,5},{22,6},{23,7},{24,8},{25... | collective-permute-start | bytes 393224 | tf_op jit(solution)/shard_map/ppermute | solution.py:317
  10.1 0.9 %copy-start = (f32[160,256]{1,0:T(8,128)S(1)}, f32[160,256]{1,0:T(8,128)}, u32[]{:S(2)}) copy-start(f32[160,256]{1,0:T(8,128)} %constant.2.clone.table_ref) | copy-start | bytes 491524
  11.1 0.7 %copy-start.2 = (s32[1,1,6]{2,1,0:T(1,128)S(1)}, s32[1,1,6]{2,1,0:T(1,128)}, u32[]{:S(2)}) copy-start(s32[1,1,6]{2,1,0:T(1,128)} %param.11) | copy-start | bytes 76
  18.1 44.0 %collective-permute-start.3 = (f32[16,16,128]{2,1,0:T(8,128)S(1)}, f32[16,16,128]{2,1,0:T(8,128)S(1)}, u32[]{:S(2)}, u32[]{:S(2)}) collective-permute-start(f32[16,16,128]{2,1,0:T(8,128)S(1)} %get-tuple-element.19), channel_id=1, source_target_pairs={{0,16},{1,17},{2,18},{3,19},{4,20},{5,21},{6,22},{7,23},{8,24},{9,... | collective-permute-start | bytes 393224 | tf_op jit(solution)/shard_map/ppermute | solution.py:317
  22.6 39.5 %collective-permute-start.4 = (f32[16,16,128]{2,1,0:T(8,128)S(1)}, f32[16,16,128]{2,1,0:T(8,128)S(1)}, u32[]{:S(2)}, u32[]{:S(2)}) collective-permute-start(f32[16,16,128]{2,1,0:T(8,128)S(1)} %get-tuple-element.20), channel_id=1, source_target_pairs={{0,1},{1,2},{2,3},{3,4},{4,5},{5,6},{6,7},{7,8},{8,9},{9,10},{10,1... | collective-permute-start | bytes 393224 | tf_op jit(solution)/shard_map/ppermute | solution.py:317
  26.5 35.6 %collective-permute-start.5 = (f32[16,16,128]{2,1,0:T(8,128)S(1)}, f32[16,16,128]{2,1,0:T(8,128)S(1)}, u32[]{:S(2)}, u32[]{:S(2)}) collective-permute-start(f32[16,16,128]{2,1,0:T(8,128)S(1)} %get-tuple-element.21), channel_id=1, source_target_pairs={{0,17},{1,18},{2,19},{3,20},{4,21},{5,22},{6,23},{7,24},{8,25},{9,... | collective-permute-start | bytes 393224 | tf_op jit(solution)/shard_map/ppermute | solution.py:317

commit v2 on v1

--- a/solution.py
+++ b/solution.py
@@ -178,7 +178,7 @@
 
 
 def patches_kernel(window_ref, spectra_ref, own_ref, b10, b01, b11,
-                   o10, o01, o11, near_ref, energy_ref, real, imag):
+                   o10, upper, near_ref, energy_ref, real, imag):
     window = halves(window_ref[...])
 
     for xq, yq, block in ((0, 0, None), (1, 0, b10), (0, 1, b01), (1, 1, b11)):
@@ -224,16 +224,20 @@
             real[strided(h, y), :] = re * TAPER[y]
             imag[strided(h, y), :] = im * TAPER[y]
 
-    for xq, yq, out in ((0, 0, near_ref), (1, 1, o11), (0, 1, o01), (1, 0, o10)):
+    for xq, yq in ((0, 0), (0, 1), (1, 1), (1, 0)):
         pieces = []
         for i in range(HALF):
             rows = pl.ds((HALF * xq + i) * PITCH + HALF * yq, HALF)
             pieces.append(jnp.concatenate([real[rows, :], imag[rows, :]], axis=1))
         both = jnp.concatenate(pieces, axis=0)
-        if out is near_ref:
+        if xq == 0 and yq == 0:
             near_ref[...] = both
+            continue
+        image = dot3(halves(both), window, 1).reshape(HALF, HALF, LANES)
+        if yq == 0:
+            o10[...] = image
         else:
-            out[...] = dot3(halves(both), window, 1).reshape(HALF, HALF, LANES)
+            upper[pl.ds(HALF * xq, HALF)] = image
 
 
 def patches(window, spectra, own, blocks):
@@ -241,10 +245,10 @@
     vmem = pl.BlockSpec(memory_space=VMEM)
     return pl.pallas_call(
         patches_kernel,
-        out_shape=[block] * 3
+        out_shape=[block, jax.ShapeDtypeStruct((PATCH, HALF, LANES), jnp.float32)]
         + [jax.ShapeDtypeStruct(own.shape, jnp.float32), jax.ShapeDtypeStruct((SUB, LANES), jnp.float32)],
         in_specs=[vmem] * 6,
-        out_specs=[vmem] * 5,
+        out_specs=[vmem] * 4,
         scratch_shapes=[VMEM((PATCH * PITCH, LANES), jnp.float32)] * 2,
         compiler_params=pltpu.CompilerParams(vmem_limit_bytes=32 * 2**20),
         cost_estimate=pl.CostEstimate(flops=800_000_000, bytes_accessed=4_000_000, transcendentals=0),
@@ -270,7 +274,7 @@
         near_kernel,
         out_shape=[
             jax.ShapeDtypeStruct(rhs.shape, jnp.float32),
-            jax.ShapeDtypeStruct((256, 1, 2), jnp.float32),
+            jax.ShapeDtypeStruct((256, 1, LANES), jnp.float32),
         ],
         in_specs=[vmem] * 5,
         out_specs=[vmem] * 2,
@@ -280,14 +284,14 @@
     )(window, inner, energy, rhs, damping)
 
 
-def finish_kernel(sums_ref, rhs_ref, own, r10, r01, r11, solution_ref, residual_ref):
+def finish_kernel(sums_ref, rhs_ref, own, from_y, from_x, solution_ref, residual_ref):
     totals = jnp.sum(sums_ref[...], axis=(0, 1), keepdims=True)[0]
     lane = lax.broadcasted_iota(jnp.int32, totals.shape, 1)
     rr = jnp.sum(jnp.where(lane == 0, totals, 0.0), axis=1, keepdims=True)
     dd = jnp.sum(jnp.where(lane == 1, totals, 0.0), axis=1, keepdims=True)
     alpha = (rr / dd)[None]
     rhs = rhs_ref[...]
-    image = (own[...] + r10[...]) + (r01[...] + r11[...])
+    image = (own[...] + from_y[:HALF]) + from_x[...]
     solution_ref[...] = alpha * rhs
     residual_ref[...] = rhs - alpha * image
 
@@ -298,7 +302,7 @@
     return pl.pallas_call(
         finish_kernel,
         out_shape=[block, block],
-        in_specs=[vmem] * 6,
+        in_specs=[vmem] * 5,
         out_specs=[vmem] * 2,
         compiler_params=pltpu.CompilerParams(vmem_limit_bytes=8 * 2**20),
         cost_estimate=pl.CostEstimate(flops=1_000_000, bytes_accessed=1_000_000, transcendentals=0),
@@ -321,11 +325,12 @@
     rhs = migrated + damping * prior_sample
     halo = [moved(rhs, -1, 0), moved(rhs, 0, -1), moved(rhs, -1, -1)]
     spectra, window, own = prepare(psf_index.reshape(NPZ), z_shift.reshape(1), psf_bank, rhs)
-    o10, o01, o11, inner, energy = patches(window, spectra, own, halo)
-    back = [moved(o10, 1, 0), moved(o01, 0, 1), moved(o11, 1, 1)]
+    o10, upper, inner, energy = patches(window, spectra, own, halo)
+    from_y = moved(upper, 0, 1)
     image, sums = near(window, inner, energy, rhs, damping)
     sums = lax.all_to_all(sums, ("gx", "gy"), 0, 0)
-    return tuple(finish(sums, rhs, [image] + back))
+    from_x = moved(o10 + from_y[HALF:], 1, 0)
+    return tuple(finish(sums, rhs, [image, from_y, from_x]))
 
 
 def solution(mesh):

time: 63.5 us -> 56.2 us (0.89)
  blocking collectives: 31.8 us -> 0 us
  starting transfers between devices: 19.5 us -> 34 us
  waiting for transfers between devices: 0.02 us -> 9.46 us
    all_to_all x1 -> x0, blocking collectives: 31.8 us -> none  [body(): sums = lax.all_to_all(sums, ('gx', 'gy'), 0, 0)]
    all_to_all x0 -> x1, starting transfers between devices: none -> 19.2 us  [body(): sums = lax.all_to_all(sums, ('gx', 'gy'), 0, 0)]
    all_to_all x0 -> x1, waiting for transfers between devices: none -> 9.45 us  [body(): sums = lax.all_to_all(sums, ('gx', 'gy'), 0, 0)]
    ppermute x6 -> x5, starting transfers between devices: 19.5 us -> 14.8 us  [moved(): return lax.ppermute(x, ('gx', 'gy'), pairs)]
  transfers between devices with their start and end apart: 6 -> 6, of which waited for: 0 -> 1; matrix products, arithmetic and copies ran while one was open for 0% -> 0% of each run, Pallas kernels for 6% -> 8%
where the time goes in v2:
time: 56.2 us; the launch traced here: 55.8 us
  starting transfers between devices  34 us (60%)
  waiting for transfers between devices  9.46 us (17%)
  Pallas kernels  8.32 us (15%)
  local copies, waits for them, and re-layouts  1.57 us (3%)
  between operations  1.41 us (3%)
  other arithmetic  1.11 us (2%)
    all_to_all x1, starting transfers between devices, body(): sums = lax.all_to_all(sums, ('gx', 'gy'), 0, 0)  19.2 us
    ppermute x5, starting transfers between devices, moved(): return lax.ppermute(x, ('gx', 'gy'), pairs)  14.8 us
    all_to_all x1, waiting for transfers between devices, body(): sums = lax.all_to_all(sums, ('gx', 'gy'), 0, 0)  9.45 us
    pallas_call x1, Pallas kernels, prepare(): pl.pallas_call(prepare_kernel, out_shape=[jax.ShapeDtypeStruct((PATCH * P...  3.58 us
    pallas_call x1, Pallas kernels, patches(): pl.pallas_call(patches_kernel, out_shape=[block, jax.ShapeDtypeStruct((PA...  2.73 us
    unnamed x6, local copies, waits for them, and re-layouts  1.57 us
  transfers between devices with their start and end apart: 6, of which 1 were waited for; matrix products, arithmetic and copies ran while one was open for 0% of the time, Pallas kernels for 8%

profile of v2, /device:TPU:1, one launch (start us, length us, event | category | flops | bytes accessed | tf_op | source)
XLA Modules:
  0.0 55.8 jit_solution(17269530293383665566)
XLA Ops:
  0.6 0.0 copy-start.1
  0.6 1.1 %multiply_add_fusion.block_ref.rhs_ref = f32[16,16,128]{2,1,0:T(8,128)S(1)} fusion(f32[16,16,128]{2,1,0:T(8,128)} %param.7, f32[16,16,128]{2,1,0:T(8,128)} %damping_ref.1, f32[16,16,128]{2,1,0:T(8,128)} %param.8), kind=kLoop, calls=%fused_computation.1 | loop fusion | flops 65536 | bytes 524288 | tf_op jit(solution)/shard_map/add | solution.py:325
  1.7 1.3 %collective-permute-start.2 = (f32[16,16,128]{2,1,0:T(8,128)S(1)}, f32[16,16,128]{2,1,0:T(8,128)S(1)}, u32[]{:S(2)}, u32[]{:S(2)}) collective-permute-start(f32[16,16,128]{2,1,0:T(8,128)S(1)} %multiply_add_fusion.block_ref.rhs_ref), channel_id=1, source_target_pairs={{17,0},{18,1},{19,2},{20,3},{21,4},{22,5},{23,6},{24,7},{25,8},{26... | collective-permute-start | bytes 393224 | tf_op jit(solution)/shard_map/ppermute | solution.py:321
  3.0 5.1 %collective-permute-start.1 = (f32[16,16,128]{2,1,0:T(8,128)S(1)}, f32[16,16,128]{2,1,0:T(8,128)S(1)}, u32[]{:S(2)}, u32[]{:S(2)}) collective-permute-start(f32[16,16,128]{2,1,0:T(8,128)S(1)} %multiply_add_fusion.block_ref.rhs_ref), channel_id=1, source_target_pairs={{1,0},{2,1},{3,2},{4,3},{5,4},{6,5},{7,6},{8,7},{9,8},{10,9},{11,1... | collective-permute-start | bytes 393224 | tf_op jit(solution)/shard_map/ppermute | solution.py:321
  8.2 1.3 %collective-permute-start = (f32[16,16,128]{2,1,0:T(8,128)S(1)}, f32[16,16,128]{2,1,0:T(8,128)S(1)}, u32[]{:S(2)}, u32[]{:S(2)}) collective-permute-start(f32[16,16,128]{2,1,0:T(8,128)S(1)} %multiply_add_fusion.block_ref.rhs_ref), channel_id=1, source_target_pairs={{16,0},{17,1},{18,2},{19,3},{20,4},{21,5},{22,6},{23,7},{24,8},{25... | collective-permute-start | bytes 393224 | tf_op jit(solution)/shard_map/ppermute | solution.py:321
  10.1 0.0 copy-start
  10.2 0.9 %copy-done = f32[160,256]{1,0:T(8,128)S(1)} copy-done((f32[160,256]{1,0:T(8,128)S(1)}, f32[160,256]{1,0:T(8,128)}, u32[]{:S(2)}) %copy-start) | copy-done | bytes 163864
  11.1 0.0 copy-start.2
  11.1 0.7 %copy-done.2 = s32[1,1,6]{2,1,0:T(1,128)S(1)} copy-done((s32[1,1,6]{2,1,0:T(1,128)S(1)}, s32[1,1,6]{2,1,0:T(1,128)}, u32[]{:S(2)}) %copy-start.2) | copy-done | bytes 48
  11.7 3.6 %prepare.1 = (f32[1024,128]{1,0:T(8,128)S(1)}, f32[128,256]{1,0:T(8,128)S(1)}, f32[256,256]{1,0:T(8,128)S(1)}) custom-call(s32[6]{0:T(128)S(1)} %bitcast.3, s32[1]{0:T(128)} %bitcast.2.shift_ref, f32[32,32,32,32]{3,2,1,0:T(8,128)} %bank_ref.1, f32[160,256]{1,0:T(8,128)S(1)} %copy-done, f32[16,16,128]{2,1,0:T(8,128)S(1)} %multiply_add_fusion.block_ref.rhs_ref), custom_call_target="tpu_custom_call" | custom-call | flops 400000000 | bytes 8000000 | tf_op jit(solution)/shard_map/prepare/pallas_call | solution.py:157
  15.3 0.0 collective-permute-done.2.b11
  15.3 0.0 collective-permute-done.1.b01
  15.3 0.0 collective-permute-done.b10
  15.3 2.7 %patches.1 = (f32[16,16,128]{2,1,0:T(8,128)S(1)}, f32[32,16,128]{2,1,0:T(8,128)S(1)}, f32[256,256]{1,0:T(8,128)S(1)}, f32[8,128]{1,0:T(8,128)S(1)}) custom-call(f32[128,256]{1,0:T(8,128)S(1)} %get-tuple-element.11.window_ref, f32[1024,128]{1,0:T(8,128)S(1)} %get-tuple-element.12.spectra_ref, f32[256,256]{1,0:T(8,128)S(1)} %get-tuple-element.13.own_ref, ...), custom_call_target="tpu_custom_call" | custom-call | flops 800000000 | bytes 4000000 | tf_op jit(solution)/shard_map/patches/pallas_call | solution.py:246
  18.1 3.6 %collective-permute-start.3 = (f32[32,16,128]{2,1,0:T(8,128)S(1)}, f32[32,16,128]{2,1,0:T(8,128)S(1)}, u32[]{:S(2)}, u32[]{:S(2)}) collective-permute-start(f32[32,16,128]{2,1,0:T(8,128)S(1)} %get-tuple-element.18), channel_id=1, source_target_pairs={{0,1},{1,2},{2,3},{3,4},{4,5},{5,6},{6,7},{7,8},{8,9},{9,10},{10,1... | collective-permute-start | bytes 786440 | tf_op jit(solution)/shard_map/ppermute | solution.py:321
  21.7 0.0 copy-done.1
  21.7 0.9 %near.1 = (f32[16,16,128]{2,1,0:T(8,128)S(1)}, f32[256,1,128]{2,1,0:T(1,128)}) custom-call(f32[128,256]{1,0:T(8,128)S(1)} %get-tuple-element.11.window_ref, f32[256,256]{1,0:T(8,128)S(1)} %get-tuple-element.14.near_ref, f32[8,128]{1,0:T(8,128)S(1)} %get-tuple-element.15.energy_ref, f32[16,16,128]{2,1,0:T(8,128)S(1)} %multiply_add_fusion.block_ref.rhs_ref, ...), custom_call_target="tpu_custom_call" | custom-call | flops 20000000000 | bytes 40000000 | tf_op jit(solution)/shard_map/near/pallas_call | solution.py:273
  22.6 19.2 %all-to-all-start = ((f32[256,1,128]{2,1,0:T(1,128)}), f32[256,1,128]{2,1,0:T(1,128)S(1)}, u32[]{:S(2)}, u32[]{:S(2)}) async-start(f32[256,1,128]{2,1,0:T(1,128)} %get-tuple-element.16), calls=%async_computation | async-start | bytes 262144 | tf_op jit(solution)/shard_map/all_to_all | solution.py:331
  41.8 0.0 collective-permute-done.3.from_y
  41.9 3.4 %collective-permute-start.4 = (f32[16,16,128]{2,1,0:T(8,128)S(1)}, f32[16,16,128]{2,1,0:T(8,128)S(1)}, u32[]{:S(2)}, u32[]{:S(2)}) collective-permute-start(f32[16,16,128]{2,1,0:T(8,128)S(1)} %slice_add_fusion), channel_id=1, source_target_pairs={{0,16},{1,17},{2,18},{3,19},{4,20},{5,21},{6,22},{7,23},{8,24},{9,... | collective-permute-start | bytes 393224 | tf_op jit(solution)/shard_map/ppermute | solution.py:321
  45.3 9.4 %all-to-all-done.sums_ref = f32[256,1,128]{2,1,0:T(1,128)S(1)} async-done(((f32[256,1,128]{2,1,0:T(1,128)}), f32[256,1,128]{2,1,0:T(1,128)S(1)}, u32[]{:S(2)}, u32[]{:S(2)}) %all-to-all-start) | async-done | bytes 131104 | tf_op jit(solution)/shard_map/all_to_all | solution.py:331
  54.8 0.0 collective-permute-done.4.from_x
  54.8 1.1 %finish.1 = (f32[16,16,128]{2,1,0:T(8,128)}, f32[16,16,128]{2,1,0:T(8,128)}) custom-call(f32[256,1,128]{2,1,0:T(1,128)S(1)} %all-to-all-done.sums_ref, f32[16,16,128]{2,1,0:T(8,128)S(1)} %multiply_add_fusion.block_ref.rhs_ref, f32[16,16,128]{2,1,0:T(8,128)S(1)} %get-tuple-element.17.own, f32[32,16,128]{2,1,0:T(8,128)S(1)} %collective-permute-done.3.from_y, ...), custom_call_target="tpu_custom_call" | custom-call | flops 1000000 | bytes 1000000 | tf_op jit(solution)/shard_map/finish/pallas_call | solution.py:302
  (1 shorter events, 0.0 us)
Async XLA Ops:
  0.6 21.1 %copy-start.1 = (f32[16,16,128]{2,1,0:T(8,128)S(1)}, f32[16,16,128]{2,1,0:T(8,128)}, u32[]{:S(2)}) copy-start(f32[16,16,128]{2,1,0:T(8,128)} %damping_ref.1) | copy-start | bytes 393220
  1.7 13.6 %collective-permute-start.2 = (f32[16,16,128]{2,1,0:T(8,128)S(1)}, f32[16,16,128]{2,1,0:T(8,128)S(1)}, u32[]{:S(2)}, u32[]{:S(2)}) collective-permute-start(f32[16,16,128]{2,1,0:T(8,128)S(1)} %multiply_add_fusion.block_ref.rhs_ref), channel_id=1, source_target_pairs={{17,0},{18,1},{19,2},{20,3},{21,4},{22,5},{23,6},{24,7},{25,8},{26... | collective-permute-start | bytes 393224 | tf_op jit(solution)/shard_map/ppermute | solution.py:321
  3.0 12.3 %collective-permute-start.1 = (f32[16,16,128]{2,1,0:T(8,128)S(1)}, f32[16,16,128]{2,1,0:T(8,128)S(1)}, u32[]{:S(2)}, u32[]{:S(2)}) collective-permute-start(f32[16,16,128]{2,1,0:T(8,128)S(1)} %multiply_add_fusion.block_ref.rhs_ref), channel_id=1, source_target_pairs={{1,0},{2,1},{3,2},{4,3},{5,4},{6,5},{7,6},{8,7},{9,8},{10,9},{11,1... | collective-permute-start | bytes 393224 | tf_op jit(solution)/shard_map/ppermute | solution.py:321
  8.2 7.1 %collective-permute-start = (f32[16,16,128]{2,1,0:T(8,128)S(1)}, f32[16,16,128]{2,1,0:T(8,128)S(1)}, u32[]{:S(2)}, u32[]{:S(2)}) collective-permute-start(f32[16,16,128]{2,1,0:T(8,128)S(1)} %multiply_add_fusion.block_ref.rhs_ref), channel_id=1, source_target_pairs={{16,0},{17,1},{18,2},{19,3},{20,4},{21,5},{22,6},{23,7},{24,8},{25... | collective-permute-start | bytes 393224 | tf_op jit(solution)/shard_map/ppermute | solution.py:321
  10.1 0.9 %copy-start = (f32[160,256]{1,0:T(8,128)S(1)}, f32[160,256]{1,0:T(8,128)}, u32[]{:S(2)}) copy-start(f32[160,256]{1,0:T(8,128)} %constant.2.clone.table_ref) | copy-start | bytes 491524
  11.1 0.7 %copy-start.2 = (s32[1,1,6]{2,1,0:T(1,128)S(1)}, s32[1,1,6]{2,1,0:T(1,128)}, u32[]{:S(2)}) copy-start(s32[1,1,6]{2,1,0:T(1,128)} %param.11) | copy-start | bytes 76
  18.1 23.8 %collective-permute-start.3 = (f32[32,16,128]{2,1,0:T(8,128)S(1)}, f32[32,16,128]{2,1,0:T(8,128)S(1)}, u32[]{:S(2)}, u32[]{:S(2)}) collective-permute-start(f32[32,16,128]{2,1,0:T(8,128)S(1)} %get-tuple-element.18), channel_id=1, source_target_pairs={{0,1},{1,2},{2,3},{3,4},{4,5},{5,6},{6,7},{7,8},{8,9},{9,10},{10,1... | collective-permute-start | bytes 786440 | tf_op jit(solution)/shard_map/ppermute | solution.py:321
  22.6 32.1 %all-to-all-start = ((f32[256,1,128]{2,1,0:T(1,128)}), f32[256,1,128]{2,1,0:T(1,128)S(1)}, u32[]{:S(2)}, u32[]{:S(2)}) async-start(f32[256,1,128]{2,1,0:T(1,128)} %get-tuple-element.16), calls=%async_computation | async-start | bytes 262144 | tf_op jit(solution)/shard_map/all_to_all | solution.py:331
  41.9 12.9 %collective-permute-start.4 = (f32[16,16,128]{2,1,0:T(8,128)S(1)}, f32[16,16,128]{2,1,0:T(8,128)S(1)}, u32[]{:S(2)}, u32[]{:S(2)}) collective-permute-start(f32[16,16,128]{2,1,0:T(8,128)S(1)} %slice_add_fusion), channel_id=1, source_target_pairs={{0,16},{1,17},{2,18},{3,19},{4,20},{5,21},{6,22},{7,23},{8,24},{9,... | collective-permute-start | bytes 393224 | tf_op jit(solution)/shard_map/ppermute | solution.py:321

commit v3 on v2

--- a/solution.py
+++ b/solution.py
@@ -1,6 +1,5 @@
 import math
 
-import numpy as np
 import jax
 import jax.numpy as jnp
 from jax import lax
@@ -15,20 +14,6 @@
 LANES = 128
 SUB = 8
 VMEM = pltpu.VMEM
-
-
-def z_table():
-    table = np.zeros((160, 2 * LANES))
-    taper = np.sin(math.pi * (np.arange(PATCH) + 0.5) / PATCH)
-    for p in range(NPZ):
-        for cell in range(PATCH):
-            for kz in range(KZ):
-                phase = 2.0 * math.pi * (kz * cell % PATCH) / PATCH
-                row = 16 + 16 * p + cell
-                table[row, KZ * p + kz] = taper[cell] * math.cos(phase)
-                if 0 < kz < HALF:
-                    table[row, LANES + KZ * p + kz] = -taper[cell] * math.sin(phase)
-    return table.astype(np.float32)
 
 
 TAPER = [math.sin(math.pi * (i + 0.5) / PATCH) for i in range(PATCH)]
@@ -104,17 +89,47 @@
     return dot(a[0], b[0], contract_b) + (dot(a[1], b[0], contract_b) + dot(a[0], b[1], contract_b))
 
 
-def prepare_kernel(index_ref, shift_ref, bank_ref, table_ref, block_ref,
+def lookup(values, places):
+    lane = lax.broadcasted_iota(jnp.int32, (SUB, LANES), 1)
+    table = jnp.zeros((SUB, LANES), jnp.float32)
+    for i, value in enumerate(values):
+        table = jnp.where(lane == i, value, table)
+    return jnp.take_along_axis(table, places, axis=1, mode="promise_in_bounds")
+
+
+COSINES = [math.cos(2.0 * math.pi * i / PATCH) for i in range(PATCH)]
+COSINES[8] = COSINES[24] = 0.0
+
+
+def window_of(shift, window_ref):
+    lane = lax.broadcasted_iota(jnp.int32, (SUB, LANES), 1)
+    p = jnp.zeros_like(lane)
+    for q in range(1, NPZ):
+        p = jnp.where(lane >= KZ * q, q, p)
+    kz = lane - KZ * p
+    first = lax.broadcasted_iota(jnp.int32, (SUB, LANES), 0) - shift - HALF * p
+    for g in range(LANES // SUB):
+        cell = first + SUB * g
+        inside = (cell >= 0) & (cell < PATCH) & (lane < KZ * NPZ)
+        cell = cell & (PATCH - 1)
+        taper = jnp.where(inside, lookup(TAPER, cell), 0.0)
+        phase = (kz * cell) & (PATCH - 1)
+        rows = pl.ds(SUB * g, SUB)
+        window_ref[rows, :LANES] = taper * lookup(COSINES, phase)
+        sine = taper * lookup(COSINES, (phase + PATCH // 4) & (PATCH - 1))
+        window_ref[rows, LANES:] = jnp.where((kz == 0) | (kz == HALF), 0.0, sine)
+
+
+def prepare_kernel(index_ref, shift_ref, bank_ref, block_ref,
                    spectra_ref, window_ref, own_ref, cubes, back, sems):
     copies = [
-        pltpu.make_async_copy(bank_ref.at[index_ref[p]], cubes.at[p], sems.at[p]) for p in range(NPZ)
+        pltpu.make_async_copy(bank_ref.at[index_ref[0, 0, p]], cubes.at[p], sems.at[p]) for p in range(NPZ)
     ]
     for copy in copies:
         copy.start()
 
-    window = pltpu.roll(table_ref[...], shift_ref[0] + 144, 0)[:LANES]
-    window_ref[...] = window
-    own_ref[...] = dot3(halves(block_ref[...].reshape(HALF * HALF, LANES)), halves(window), 0)
+    window_of(shift_ref[0, 0], window_ref)
+    own_ref[...] = dot3(halves(block_ref[...].reshape(HALF * HALF, LANES)), halves(window_ref[...]), 0)
 
     source = lax.broadcasted_iota(jnp.int32, (NPZ * PATCH, 2 * LANES), 0)
     lane = lax.broadcasted_iota(jnp.int32, (NPZ * PATCH, 2 * LANES), 1)
@@ -161,7 +176,7 @@
             jax.ShapeDtypeStruct((LANES, 2 * LANES), jnp.float32),
             jax.ShapeDtypeStruct((HALF * HALF, 2 * LANES), jnp.float32),
         ],
-        in_specs=[smem, smem, pl.BlockSpec(memory_space=pltpu.HBM), vmem, vmem],
+        in_specs=[smem, smem, pl.BlockSpec(memory_space=pltpu.HBM), vmem],
         out_specs=[vmem] * 3,
         scratch_shapes=[
             VMEM((NPZ, PATCH, PATCH, PATCH), jnp.float32),
@@ -171,7 +186,7 @@
         compiler_params=pltpu.CompilerParams(vmem_limit_bytes=50 * 2**20),
         cost_estimate=pl.CostEstimate(flops=400_000_000, bytes_accessed=8_000_000, transcendentals=0),
         name="prepare",
-    )(index, shift, bank, z_table(), rhs)
+    )(index, shift, bank, rhs)
 
 
 PITCH = 40
@@ -268,13 +283,13 @@
     image_ref[...] = own.reshape(field.shape) + damped * field
 
 
-def near(window, inner, energy, rhs, damping):
+def near(window, inner, energy, rhs, damping, copies):
     vmem = pl.BlockSpec(memory_space=VMEM)
     return pl.pallas_call(
         near_kernel,
         out_shape=[
             jax.ShapeDtypeStruct(rhs.shape, jnp.float32),
-            jax.ShapeDtypeStruct((256, 1, LANES), jnp.float32),
+            jax.ShapeDtypeStruct((copies, 1, LANES), jnp.float32),
         ],
         in_specs=[vmem] * 5,
         out_specs=[vmem] * 2,
@@ -284,8 +299,9 @@
     )(window, inner, energy, rhs, damping)
 
 
-def finish_kernel(sums_ref, rhs_ref, own, from_y, from_x, solution_ref, residual_ref):
-    totals = jnp.sum(sums_ref[...], axis=(0, 1), keepdims=True)[0]
+def finish_kernel(sums_ref, others_ref, rhs_ref, own, from_y, from_x, solution_ref, residual_ref):
+    totals = [jnp.sum(ref[...], axis=(0, 1), keepdims=True)[0] for ref in (sums_ref, others_ref)]
+    totals = totals[0] + totals[1]
     lane = lax.broadcasted_iota(jnp.int32, totals.shape, 1)
     rr = jnp.sum(jnp.where(lane == 0, totals, 0.0), axis=1, keepdims=True)
     dd = jnp.sum(jnp.where(lane == 1, totals, 0.0), axis=1, keepdims=True)
@@ -296,18 +312,18 @@
     residual_ref[...] = rhs - alpha * image
 
 
-def finish(sums, rhs, parts):
+def finish(sums, others, rhs, parts):
     block = jax.ShapeDtypeStruct(rhs.shape, jnp.float32)
     vmem = pl.BlockSpec(memory_space=VMEM)
     return pl.pallas_call(
         finish_kernel,
         out_shape=[block, block],
-        in_specs=[vmem] * 5,
+        in_specs=[vmem] * 6,
         out_specs=[vmem] * 2,
         compiler_params=pltpu.CompilerParams(vmem_limit_bytes=8 * 2**20),
         cost_estimate=pl.CostEstimate(flops=1_000_000, bytes_accessed=1_000_000, transcendentals=0),
         name="finish",
-    )(sums, rhs, *parts)
+    )(sums, others, rhs, *parts)
 
 
 def moved(x, by_x, by_y):
@@ -323,14 +339,17 @@
 
 def body(migrated, prior_sample, damping, psf_bank, psf_index, z_shift):
     rhs = migrated + damping * prior_sample
+    nx, ny = lax.axis_size("gx"), lax.axis_size("gy")
     halo = [moved(rhs, -1, 0), moved(rhs, 0, -1), moved(rhs, -1, -1)]
-    spectra, window, own = prepare(psf_index.reshape(NPZ), z_shift.reshape(1), psf_bank, rhs)
+    spectra, window, own = prepare(psf_index, z_shift, psf_bank, rhs)
     o10, upper, inner, energy = patches(window, spectra, own, halo)
     from_y = moved(upper, 0, 1)
-    image, sums = near(window, inner, energy, rhs, damping)
-    sums = lax.all_to_all(sums, ("gx", "gy"), 0, 0)
+    image, sums = near(window, inner, energy, rhs, damping, nx * ny // 2)
+    groups = [[i * ny + j for i in range(nx) for j in range(k, ny, 2)] for k in range(2)]
+    sums = lax.all_to_all(sums, ("gx", "gy"), 0, 0, axis_index_groups=groups)
+    others = lax.ppermute(sums, "gy", [(j, j ^ 1) for j in range(ny)])
     from_x = moved(o10 + from_y[HALF:], 1, 0)
-    return tuple(finish(sums, rhs, [image, from_y, from_x]))
+    return tuple(finish(sums, others, rhs, [image, from_y, from_x]))
 
 
 def solution(mesh):

time: 56.2 us -> 55.9 us (level)
  local copies, waits for them, and re-layouts: 1.57 us -> 0.65 us
    all_to_all x1, waiting for transfers between devices: 9.45 us -> 7.84 us  [body(): sums = lax.all_to_all(sums, ('gx', 'gy'), 0, 0, axis_index_groups=groups)]
    ppermute x0 -> x1, waiting for transfers between devices: none -> 1.25 us  [body(): others = lax.ppermute(sums, 'gy', [(j, j ^ 1) for j in range(ny)])]
    all_to_all x1, starting transfers between devices: 19.2 us -> 20.4 us  [body(): sums = lax.all_to_all(sums, ('gx', 'gy'), 0, 0, axis_index_groups=groups)]
    unnamed x6 -> x4, local copies, waits for them, and re-layouts: 1.57 us -> 0.65 us
    ppermute x5, starting transfers between devices: 14.8 us -> 14 us  [moved(): return lax.ppermute(x, ('gx', 'gy'), pairs)]
    ppermute x5, waiting for transfers between devices: 0.01 us -> 0.63 us  [moved(): return lax.ppermute(x, ('gx', 'gy'), pairs)]
  transfers between devices with their start and end apart: 6 -> 7, of which waited for: 1 -> 3; matrix products, arithmetic and copies ran while one was open for 0% -> 0% of each run, Pallas kernels for 8% -> 8%
where the time goes in v3:
time: 55.9 us; the launch traced here: 55.6 us
  starting transfers between devices  34.5 us (62%)
  waiting for transfers between devices  9.72 us (17%)
  Pallas kernels  8.26 us (15%)
  between operations  1.4 us (3%)
  other arithmetic  1.11 us (2%)
  local copies, waits for them, and re-layouts  0.65 us (1%)
    all_to_all x1, starting transfers between devices, body(): sums = lax.all_to_all(sums, ('gx', 'gy'), 0, 0, axis_index_groups=groups)  20.4 us
    ppermute x5, starting transfers between devices, moved(): return lax.ppermute(x, ('gx', 'gy'), pairs)  14 us
    all_to_all x1, waiting for transfers between devices, body(): sums = lax.all_to_all(sums, ('gx', 'gy'), 0, 0, axis_index_groups=groups)  7.84 us
    pallas_call x1, Pallas kernels, prepare(): pl.pallas_call(prepare_kernel, out_shape=[jax.ShapeDtypeStruct((PATCH * P...  3.71 us
    pallas_call x1, Pallas kernels, patches(): pl.pallas_call(patches_kernel, out_shape=[block, jax.ShapeDtypeStruct((PA...  2.73 us
    ppermute x1, waiting for transfers between devices, body(): others = lax.ppermute(sums, 'gy', [(j, j ^ 1) for j in range(ny)])  1.25 us
  transfers between devices with their start and end apart: 7, of which 3 were waited for; matrix products, arithmetic and copies ran while one was open for 0% of the time, Pallas kernels for 8%

profile of v3, /device:TPU:1, one launch (start us, length us, event | category | flops | bytes accessed | tf_op | source)
XLA Modules:
  0.0 55.6 jit_solution(7705002939778378224)
XLA Ops:
  0.6 0.0 copy-start
  0.6 1.1 %multiply_add_fusion.block_ref.rhs_ref = f32[16,16,128]{2,1,0:T(8,128)S(1)} fusion(f32[16,16,128]{2,1,0:T(8,128)} %param.6, f32[16,16,128]{2,1,0:T(8,128)} %damping_ref.1, f32[16,16,128]{2,1,0:T(8,128)} %param.7), kind=kLoop, calls=%fused_computation.1 | loop fusion | flops 65536 | bytes 524288 | tf_op jit(solution)/shard_map/add | solution.py:341
  1.7 1.3 %collective-permute-start.2 = (f32[16,16,128]{2,1,0:T(8,128)S(1)}, f32[16,16,128]{2,1,0:T(8,128)S(1)}, u32[]{:S(2)}, u32[]{:S(2)}) collective-permute-start(f32[16,16,128]{2,1,0:T(8,128)S(1)} %multiply_add_fusion.block_ref.rhs_ref), channel_id=1, source_target_pairs={{17,0},{18,1},{19,2},{20,3},{21,4},{22,5},{23,6},{24,7},{25,8},{26... | collective-permute-start | bytes 393224 | tf_op jit(solution)/shard_map/ppermute | solution.py:337
  3.0 5.1 %collective-permute-start.1 = (f32[16,16,128]{2,1,0:T(8,128)S(1)}, f32[16,16,128]{2,1,0:T(8,128)S(1)}, u32[]{:S(2)}, u32[]{:S(2)}) collective-permute-start(f32[16,16,128]{2,1,0:T(8,128)S(1)} %multiply_add_fusion.block_ref.rhs_ref), channel_id=1, source_target_pairs={{1,0},{2,1},{3,2},{4,3},{5,4},{6,5},{7,6},{8,7},{9,8},{10,9},{11,1... | collective-permute-start | bytes 393224 | tf_op jit(solution)/shard_map/ppermute | solution.py:337
  8.2 1.3 %collective-permute-start = (f32[16,16,128]{2,1,0:T(8,128)S(1)}, f32[16,16,128]{2,1,0:T(8,128)S(1)}, u32[]{:S(2)}, u32[]{:S(2)}) collective-permute-start(f32[16,16,128]{2,1,0:T(8,128)S(1)} %multiply_add_fusion.block_ref.rhs_ref), channel_id=1, source_target_pairs={{16,0},{17,1},{18,2},{19,3},{20,4},{21,5},{22,6},{23,7},{24,8},{25... | collective-permute-start | bytes 393224 | tf_op jit(solution)/shard_map/ppermute | solution.py:337
  10.1 0.0 copy-start.1
  10.1 0.6 %copy-done.1 = s32[1,1,6]{2,1,0:T(1,128)S(1)} copy-done((s32[1,1,6]{2,1,0:T(1,128)S(1)}, s32[1,1,6]{2,1,0:T(1,128)}, u32[]{:S(2)}) %copy-start.1) | copy-done | bytes 48
  10.8 3.7 %prepare.1 = (f32[1024,128]{1,0:T(8,128)S(1)}, f32[128,256]{1,0:T(8,128)S(1)}, f32[256,256]{1,0:T(8,128)S(1)}) custom-call(s32[1,1,6]{2,1,0:T(1,128)S(1)} %copy-done.1, s32[1,1]{1,0:T(1,128)S(6)} %copy.8.shift_ref, f32[32,32,32,32]{3,2,1,0:T(8,128)} %bank_ref.1, f32[16,16,128]{2,1,0:T(8,128)S(1)} %multiply_add_fusion.block_ref.rhs_ref), custom_call_target="tpu_custom_call" | custom-call | flops 400000000 | bytes 8000000 | tf_op jit(solution)/shard_map/prepare/pallas_call | solution.py:172
  14.5 0.0 collective-permute-done.2.b11
  14.5 0.0 collective-permute-done.1.b01
  14.5 0.6 %collective-permute-done.b10 = f32[16,16,128]{2,1,0:T(8,128)S(1)} collective-permute-done((f32[16,16,128]{2,1,0:T(8,128)S(1)}, f32[16,16,128]{2,1,0:T(8,128)S(1)}, u32[]{:S(2)}, u32[]{:S(2)}) %collective-permute-start) | collective-permute-done | bytes 131104 | tf_op jit(solution)/shard_map/ppermute | solution.py:337
  15.2 2.7 %patches.1 = (f32[16,16,128]{2,1,0:T(8,128)S(1)}, f32[32,16,128]{2,1,0:T(8,128)S(1)}, f32[256,256]{1,0:T(8,128)S(1)}, f32[8,128]{1,0:T(8,128)S(1)}) custom-call(f32[128,256]{1,0:T(8,128)S(1)} %get-tuple-element.11.window_ref, f32[1024,128]{1,0:T(8,128)S(1)} %get-tuple-element.12.spectra_ref, f32[256,256]{1,0:T(8,128)S(1)} %get-tuple-element.13.own_ref, ...), custom_call_target="tpu_custom_call" | custom-call | flops 800000000 | bytes 4000000 | tf_op jit(solution)/shard_map/patches/pallas_call | solution.py:261
  17.9 3.8 %collective-permute-start.4 = (f32[32,16,128]{2,1,0:T(8,128)S(1)}, f32[32,16,128]{2,1,0:T(8,128)S(1)}, u32[]{:S(2)}, u32[]{:S(2)}) collective-permute-start(f32[32,16,128]{2,1,0:T(8,128)S(1)} %get-tuple-element.18), channel_id=1, source_target_pairs={{0,1},{1,2},{2,3},{3,4},{4,5},{5,6},{6,7},{7,8},{8,9},{9,10},{10,1... | collective-permute-start | bytes 786440 | tf_op jit(solution)/shard_map/ppermute | solution.py:337
  21.7 0.0 copy-done
  21.7 0.9 %near.1 = (f32[16,16,128]{2,1,0:T(8,128)S(1)}, f32[128,1,128]{2,1,0:T(1,128)}) custom-call(f32[128,256]{1,0:T(8,128)S(1)} %get-tuple-element.11.window_ref, f32[256,256]{1,0:T(8,128)S(1)} %get-tuple-element.14.near_ref, f32[8,128]{1,0:T(8,128)S(1)} %get-tuple-element.15.energy_ref, f32[16,16,128]{2,1,0:T(8,128)S(1)} %multiply_add_fusion.block_ref.rhs_ref, ...), custom_call_target="tpu_custom_call" | custom-call | flops 20000000000 | bytes 40000000 | tf_op jit(solution)/shard_map/near/pallas_call | solution.py:288
  22.6 20.4 %all-to-all-start = ((f32[128,1,128]{2,1,0:T(1,128)}), f32[128,1,128]{2,1,0:T(1,128)S(1)}, u32[]{:S(2)}, u32[]{:S(2)}) async-start(f32[128,1,128]{2,1,0:T(1,128)} %get-tuple-element.16), calls=%async_computation | async-start | bytes 131072 | tf_op jit(solution)/shard_map/all_to_all | solution.py:349
  43.0 0.0 collective-permute-done.4.from_y
  43.1 2.5 %collective-permute-start.5 = (f32[16,16,128]{2,1,0:T(8,128)S(1)}, f32[16,16,128]{2,1,0:T(8,128)S(1)}, u32[]{:S(2)}, u32[]{:S(2)}) collective-permute-start(f32[16,16,128]{2,1,0:T(8,128)S(1)} %slice_add_fusion), channel_id=1, source_target_pairs={{0,16},{1,17},{2,18},{3,19},{4,20},{5,21},{6,22},{7,23},{8,24},{9,... | collective-permute-start | bytes 393224 | tf_op jit(solution)/shard_map/ppermute | solution.py:337
  45.6 7.8 %all-to-all-done.sums_ref = f32[128,1,128]{2,1,0:T(1,128)S(1)} async-done(((f32[128,1,128]{2,1,0:T(1,128)}), f32[128,1,128]{2,1,0:T(1,128)S(1)}, u32[]{:S(2)}, u32[]{:S(2)}) %all-to-all-start) | async-done | bytes 65568 | tf_op jit(solution)/shard_map/all_to_all | solution.py:349
  53.4 0.0 collective-permute-start.3
  53.4 1.3 %collective-permute-done.3.others_ref = f32[128,1,128]{2,1,0:T(1,128)S(1)} collective-permute-done((f32[128,1,128]{2,1,0:T(1,128)S(1)}, f32[128,1,128]{2,1,0:T(1,128)S(1)}, u32[]{:S(2)}, u32[]{:S(2)}) %collective-permute-start.3) | collective-permute-done | bytes 65568 | tf_op jit(solution)/shard_map/ppermute | solution.py:350
  54.6 0.0 collective-permute-done.5.from_x
  54.7 0.9 %finish.1 = (f32[16,16,128]{2,1,0:T(8,128)}, f32[16,16,128]{2,1,0:T(8,128)}) custom-call(f32[128,1,128]{2,1,0:T(1,128)S(1)} %all-to-all-done.sums_ref, f32[128,1,128]{2,1,0:T(1,128)S(1)} %collective-permute-done.3.others_ref, f32[16,16,128]{2,1,0:T(8,128)S(1)} %multiply_add_fusion.block_ref.rhs_ref, f32[16,16,128]{2,1,0:T(8,128)S(1)} %get-tuple-element.17.own, ...), custom_call_target="tpu_custom_call" | custom-call | flops 1000000 | bytes 1000000 | tf_op jit(solution)/shard_map/finish/pallas_call | solution.py:318
  (1 shorter events, 0.0 us)
Async XLA Ops:
  0.6 21.1 %copy-start = (f32[16,16,128]{2,1,0:T(8,128)S(1)}, f32[16,16,128]{2,1,0:T(8,128)}, u32[]{:S(2)}) copy-start(f32[16,16,128]{2,1,0:T(8,128)} %damping_ref.1) | copy-start | bytes 393220
  1.7 12.8 %collective-permute-start.2 = (f32[16,16,128]{2,1,0:T(8,128)S(1)}, f32[16,16,128]{2,1,0:T(8,128)S(1)}, u32[]{:S(2)}, u32[]{:S(2)}) collective-permute-start(f32[16,16,128]{2,1,0:T(8,128)S(1)} %multiply_add_fusion.block_ref.rhs_ref), channel_id=1, source_target_pairs={{17,0},{18,1},{19,2},{20,3},{21,4},{22,5},{23,6},{24,7},{25,8},{26... | collective-permute-start | bytes 393224 | tf_op jit(solution)/shard_map/ppermute | solution.py:337
  3.0 11.5 %collective-permute-start.1 = (f32[16,16,128]{2,1,0:T(8,128)S(1)}, f32[16,16,128]{2,1,0:T(8,128)S(1)}, u32[]{:S(2)}, u32[]{:S(2)}) collective-permute-start(f32[16,16,128]{2,1,0:T(8,128)S(1)} %multiply_add_fusion.block_ref.rhs_ref), channel_id=1, source_target_pairs={{1,0},{2,1},{3,2},{4,3},{5,4},{6,5},{7,6},{8,7},{9,8},{10,9},{11,1... | collective-permute-start | bytes 393224 | tf_op jit(solution)/shard_map/ppermute | solution.py:337
  8.2 7.0 %collective-permute-start = (f32[16,16,128]{2,1,0:T(8,128)S(1)}, f32[16,16,128]{2,1,0:T(8,128)S(1)}, u32[]{:S(2)}, u32[]{:S(2)}) collective-permute-start(f32[16,16,128]{2,1,0:T(8,128)S(1)} %multiply_add_fusion.block_ref.rhs_ref), channel_id=1, source_target_pairs={{16,0},{17,1},{18,2},{19,3},{20,4},{21,5},{22,6},{23,7},{24,8},{25... | collective-permute-start | bytes 393224 | tf_op jit(solution)/shard_map/ppermute | solution.py:337
  10.1 0.7 %copy-start.1 = (s32[1,1,6]{2,1,0:T(1,128)S(1)}, s32[1,1,6]{2,1,0:T(1,128)}, u32[]{:S(2)}) copy-start(s32[1,1,6]{2,1,0:T(1,128)} %index_ref.1) | copy-start | bytes 76
  17.9 25.1 %collective-permute-start.4 = (f32[32,16,128]{2,1,0:T(8,128)S(1)}, f32[32,16,128]{2,1,0:T(8,128)S(1)}, u32[]{:S(2)}, u32[]{:S(2)}) collective-permute-start(f32[32,16,128]{2,1,0:T(8,128)S(1)} %get-tuple-element.18), channel_id=1, source_target_pairs={{0,1},{1,2},{2,3},{3,4},{4,5},{5,6},{6,7},{7,8},{8,9},{9,10},{10,1... | collective-permute-start | bytes 786440 | tf_op jit(solution)/shard_map/ppermute | solution.py:337
  22.6 30.8 %all-to-all-start = ((f32[128,1,128]{2,1,0:T(1,128)}), f32[128,1,128]{2,1,0:T(1,128)S(1)}, u32[]{:S(2)}, u32[]{:S(2)}) async-start(f32[128,1,128]{2,1,0:T(1,128)} %get-tuple-element.16), calls=%async_computation | async-start | bytes 131072 | tf_op jit(solution)/shard_map/all_to_all | solution.py:349
  43.1 11.6 %collective-permute-start.5 = (f32[16,16,128]{2,1,0:T(8,128)S(1)}, f32[16,16,128]{2,1,0:T(8,128)S(1)}, u32[]{:S(2)}, u32[]{:S(2)}) collective-permute-start(f32[16,16,128]{2,1,0:T(8,128)S(1)} %slice_add_fusion), channel_id=1, source_target_pairs={{0,16},{1,17},{2,18},{3,19},{4,20},{5,21},{6,22},{7,23},{8,24},{9,... | collective-permute-start | bytes 393224 | tf_op jit(solution)/shard_map/ppermute | solution.py:337
  53.4 1.3 %collective-permute-start.3 = (f32[128,1,128]{2,1,0:T(1,128)S(1)}, f32[128,1,128]{2,1,0:T(1,128)S(1)}, u32[]{:S(2)}, u32[]{:S(2)}) collective-permute-start(f32[128,1,128]{2,1,0:T(1,128)S(1)} %all-to-all-done.sums_ref), channel_id=1, source_target_pairs={{0,1},{1,0},{2,3},{3,2},{4,5},{5,4},{6,7},{7,6},{8,9},{9,8},{10,11... | collective-permute-start | bytes 196616 | tf_op jit(solution)/shard_map/ppermute | solution.py:350

commit v4 on v3

--- a/solution.py
+++ b/solution.py
@@ -192,8 +192,8 @@
 PITCH = 40
 
 
-def patches_kernel(window_ref, spectra_ref, own_ref, b10, b01, b11,
-                   o10, upper, near_ref, energy_ref, real, imag):
+def patches_kernel(window_ref, spectra_ref, own_ref, rhs_ref, damping_ref, b10, b01, b11,
+                   o10, upper, near_ref, sums_ref, real, imag, sums, sem):
     window = halves(window_ref[...])
 
     for xq, yq, block in ((0, 0, None), (1, 0, b10), (0, 1, b01), (1, 1, b11)):
@@ -231,7 +231,14 @@
         for x, (re, im) in enumerate(out):
             real[rows(x), :] = re * (TAPER[x] / PATCH**3)
             imag[rows(x), :] = im * (TAPER[x] / PATCH**3)
-    energy_ref[...] = energy
+
+    square = rhs_ref[...] * rhs_ref[...]
+    rr = jnp.sum(square)
+    dd = jnp.sum(square * damping_ref[...]) + jnp.sum(energy) * (1.0 / PATCH**3)
+    lane = lax.broadcasted_iota(jnp.int32, sums.shape, len(sums.shape) - 1)
+    sums[...] = jnp.where(lane == 0, rr, jnp.where(lane == 1, dd, 0.0))
+    leaving = pltpu.make_async_copy(sums, sums_ref, sem)
+    leaving.start()
 
     for h in range(4):
         out = dft32(lambda k: (real[strided(h, k), :], imag[strided(h, k), :]), 1)
@@ -253,50 +260,42 @@
             o10[...] = image
         else:
             upper[pl.ds(HALF * xq, HALF)] = image
-
-
-def patches(window, spectra, own, blocks):
+    leaving.wait()
+
+
+def patches(window, spectra, own, rhs, damping, blocks, copies):
     block = jax.ShapeDtypeStruct(blocks[0].shape, jnp.float32)
     vmem = pl.BlockSpec(memory_space=VMEM)
     return pl.pallas_call(
         patches_kernel,
         out_shape=[block, jax.ShapeDtypeStruct((PATCH, HALF, LANES), jnp.float32)]
-        + [jax.ShapeDtypeStruct(own.shape, jnp.float32), jax.ShapeDtypeStruct((SUB, LANES), jnp.float32)],
-        in_specs=[vmem] * 6,
-        out_specs=[vmem] * 4,
-        scratch_shapes=[VMEM((PATCH * PITCH, LANES), jnp.float32)] * 2,
+        + [jax.ShapeDtypeStruct(own.shape, jnp.float32), jax.ShapeDtypeStruct((copies, 1, LANES), jnp.float32)],
+        in_specs=[vmem] * 8,
+        out_specs=[vmem] * 3 + [pl.BlockSpec(memory_space=pltpu.HBM)],
+        scratch_shapes=[VMEM((PATCH * PITCH, LANES), jnp.float32)] * 2
+        + [VMEM((copies, 1, LANES), jnp.float32), pltpu.SemaphoreType.DMA],
         compiler_params=pltpu.CompilerParams(vmem_limit_bytes=32 * 2**20),
         cost_estimate=pl.CostEstimate(flops=800_000_000, bytes_accessed=4_000_000, transcendentals=0),
         name="patches",
-    )(window, spectra, own, *blocks)
-
-
-def near_kernel(window_ref, near_ref, energy_ref, rhs_ref, damping_ref, image_ref, sums_ref):
-    field = rhs_ref[...]
-    square = field * field
-    damped = damping_ref[...]
-    rr = jnp.sum(square)
-    dd = jnp.sum(square * damped) + jnp.sum(energy_ref[...]) * (1.0 / PATCH**3)
-    lane = lax.broadcasted_iota(jnp.int32, sums_ref.shape, len(sums_ref.shape) - 1)
-    sums_ref[...] = jnp.where(lane == 0, rr, jnp.where(lane == 1, dd, 0.0))
+    )(window, spectra, own, rhs, damping, *blocks)
+
+
+def near_kernel(window_ref, near_ref, rhs_ref, damping_ref, image_ref):
     own = dot3(halves(near_ref[...]), halves(window_ref[...]), 1)
-    image_ref[...] = own.reshape(field.shape) + damped * field
-
-
-def near(window, inner, energy, rhs, damping, copies):
+    image_ref[...] = own.reshape(image_ref.shape) + damping_ref[...] * rhs_ref[...]
+
+
+def near(window, inner, rhs, damping):
     vmem = pl.BlockSpec(memory_space=VMEM)
     return pl.pallas_call(
         near_kernel,
-        out_shape=[
-            jax.ShapeDtypeStruct(rhs.shape, jnp.float32),
-            jax.ShapeDtypeStruct((copies, 1, LANES), jnp.float32),
-        ],
-        in_specs=[vmem] * 5,
-        out_specs=[vmem] * 2,
+        out_shape=jax.ShapeDtypeStruct(rhs.shape, jnp.float32),
+        in_specs=[vmem] * 4,
+        out_specs=vmem,
         compiler_params=pltpu.CompilerParams(vmem_limit_bytes=32 * 2**20),
-        cost_estimate=pl.CostEstimate(flops=20_000_000_000, bytes_accessed=40_000_000, transcendentals=0),
+        cost_estimate=pl.CostEstimate(flops=20_000_000, bytes_accessed=1_000_000, transcendentals=0),
         name="near",
-    )(window, inner, energy, rhs, damping)
+    )(window, inner, rhs, damping)
 
 
 def finish_kernel(sums_ref, others_ref, rhs_ref, own, from_y, from_x, solution_ref, residual_ref):
@@ -342,9 +341,9 @@
     nx, ny = lax.axis_size("gx"), lax.axis_size("gy")
     halo = [moved(rhs, -1, 0), moved(rhs, 0, -1), moved(rhs, -1, -1)]
     spectra, window, own = prepare(psf_index, z_shift, psf_bank, rhs)
-    o10, upper, inner, energy = patches(window, spectra, own, halo)
+    o10, upper, inner, sums = patches(window, spectra, own, rhs, damping, halo, nx * ny // 2)
     from_y = moved(upper, 0, 1)
-    image, sums = near(window, inner, energy, rhs, damping, nx * ny // 2)
+    image = near(window, inner, rhs, damping)
     groups = [[i * ny + j for i in range(nx) for j in range(k, ny, 2)] for k in range(2)]
     sums = lax.all_to_all(sums, ("gx", "gy"), 0, 0, axis_index_groups=groups)
     others = lax.ppermute(sums, "gy", [(j, j ^ 1) for j in range(ny)])

time: 55.9 us -> 55.5 us (level)
    pallas_call x1, Pallas kernels: 0.88 us -> 0.27 us  [near(): pl.pallas_call(near_kernel, out_shape=jax.ShapeDtypeStruct(rhs.shape, jnp...]
  transfers between devices with their start and end apart: 7 -> 7, of which waited for: 3 -> 3; matrix products, arithmetic and copies ran while one was open for 0% -> 0% of each run, Pallas kernels for 8% -> 7%
where the time goes in v4:
time: 55.5 us; the launch traced here: 55.2 us
  starting transfers between devices  34.5 us (62%)
  waiting for transfers between devices  9.44 us (17%)
  Pallas kernels  8.13 us (15%)
  between operations  1.4 us (3%)
  other arithmetic  1.11 us (2%)
  local copies, waits for them, and re-layouts  0.65 us (1%)
    all_to_all x1, starting transfers between devices, body(): sums = lax.all_to_all(sums, ('gx', 'gy'), 0, 0, axis_index_groups=groups)  20.5 us
    ppermute x5, starting transfers between devices, moved(): return lax.ppermute(x, ('gx', 'gy'), pairs)  14 us
    all_to_all x1, waiting for transfers between devices, body(): sums = lax.all_to_all(sums, ('gx', 'gy'), 0, 0, axis_index_groups=groups)  7.84 us
    pallas_call x1, Pallas kernels, prepare(): pl.pallas_call(prepare_kernel, out_shape=[jax.ShapeDtypeStruct((PATCH * P...  3.71 us
    pallas_call x1, Pallas kernels, patches(): pl.pallas_call(patches_kernel, out_shape=[block, jax.ShapeDtypeStruct((PA...  3.2 us
  transfers between devices with their start and end apart: 7, of which 3 were waited for; matrix products, arithmetic and copies ran while one was open for 0% of the time, Pallas kernels for 7%

profile of v4, /device:TPU:1, one launch (start us, length us, event | category | flops | bytes accessed | tf_op | source)
XLA Modules:
  0.0 55.2 jit_solution(17418709809509289441)
XLA Ops:
  0.6 0.0 copy-start
  0.6 1.1 %multiply_add_fusion.block_ref.rhs_ref = f32[16,16,128]{2,1,0:T(8,128)S(1)} fusion(f32[16,16,128]{2,1,0:T(8,128)} %param.6, f32[16,16,128]{2,1,0:T(8,128)} %damping_ref.3, f32[16,16,128]{2,1,0:T(8,128)} %param.7), kind=kLoop, calls=%fused_computation.1 | loop fusion | flops 65536 | bytes 524288 | tf_op jit(solution)/shard_map/add | solution.py:340
  1.7 1.3 %collective-permute-start.2 = (f32[16,16,128]{2,1,0:T(8,128)S(1)}, f32[16,16,128]{2,1,0:T(8,128)S(1)}, u32[]{:S(2)}, u32[]{:S(2)}) collective-permute-start(f32[16,16,128]{2,1,0:T(8,128)S(1)} %multiply_add_fusion.block_ref.rhs_ref), channel_id=1, source_target_pairs={{17,0},{18,1},{19,2},{20,3},{21,4},{22,5},{23,6},{24,7},{25,8},{26... | collective-permute-start | bytes 393224 | tf_op jit(solution)/shard_map/ppermute | solution.py:336
  3.0 5.1 %collective-permute-start.1 = (f32[16,16,128]{2,1,0:T(8,128)S(1)}, f32[16,16,128]{2,1,0:T(8,128)S(1)}, u32[]{:S(2)}, u32[]{:S(2)}) collective-permute-start(f32[16,16,128]{2,1,0:T(8,128)S(1)} %multiply_add_fusion.block_ref.rhs_ref), channel_id=1, source_target_pairs={{1,0},{2,1},{3,2},{4,3},{5,4},{6,5},{7,6},{8,7},{9,8},{10,9},{11,1... | collective-permute-start | bytes 393224 | tf_op jit(solution)/shard_map/ppermute | solution.py:336
  8.2 1.3 %collective-permute-start = (f32[16,16,128]{2,1,0:T(8,128)S(1)}, f32[16,16,128]{2,1,0:T(8,128)S(1)}, u32[]{:S(2)}, u32[]{:S(2)}) collective-permute-start(f32[16,16,128]{2,1,0:T(8,128)S(1)} %multiply_add_fusion.block_ref.rhs_ref), channel_id=1, source_target_pairs={{16,0},{17,1},{18,2},{19,3},{20,4},{21,5},{22,6},{23,7},{24,8},{25... | collective-permute-start | bytes 393224 | tf_op jit(solution)/shard_map/ppermute | solution.py:336
  10.1 0.0 copy-start.1
  10.1 0.6 %copy-done.1 = s32[1,1,6]{2,1,0:T(1,128)S(1)} copy-done((s32[1,1,6]{2,1,0:T(1,128)S(1)}, s32[1,1,6]{2,1,0:T(1,128)}, u32[]{:S(2)}) %copy-start.1) | copy-done | bytes 48
  10.8 3.7 %prepare.1 = (f32[1024,128]{1,0:T(8,128)S(1)}, f32[128,256]{1,0:T(8,128)S(1)}, f32[256,256]{1,0:T(8,128)S(1)}) custom-call(s32[1,1,6]{2,1,0:T(1,128)S(1)} %copy-done.1, s32[1,1]{1,0:T(1,128)S(6)} %copy.8.shift_ref, f32[32,32,32,32]{3,2,1,0:T(8,128)} %bank_ref.1, f32[16,16,128]{2,1,0:T(8,128)S(1)} %multiply_add_fusion.block_ref.rhs_ref), custom_call_target="tpu_custom_call" | custom-call | flops 400000000 | bytes 8000000 | tf_op jit(solution)/shard_map/prepare/pallas_call | solution.py:172
  14.5 0.0 collective-permute-done.2.b11
  14.5 0.0 collective-permute-done.1.b01
  14.5 0.6 %collective-permute-done.b10 = f32[16,16,128]{2,1,0:T(8,128)S(1)} collective-permute-done((f32[16,16,128]{2,1,0:T(8,128)S(1)}, f32[16,16,128]{2,1,0:T(8,128)S(1)}, u32[]{:S(2)}, u32[]{:S(2)}) %collective-permute-start) | collective-permute-done | bytes 131104 | tf_op jit(solution)/shard_map/ppermute | solution.py:336
  15.2 0.0 copy-done
  15.2 3.2 %patches.1 = (f32[16,16,128]{2,1,0:T(8,128)S(1)}, f32[32,16,128]{2,1,0:T(8,128)S(1)}, f32[256,256]{1,0:T(8,128)S(1)}, f32[128,1,128]{2,1,0:T(1,128)}) custom-call(f32[128,256]{1,0:T(8,128)S(1)} %get-tuple-element.9.window_ref, f32[1024,128]{1,0:T(8,128)S(1)} %get-tuple-element.10.spectra_ref, f32[256,256]{1,0:T(8,128)S(1)} %get-tuple-element.11.own_ref, ...), custom_call_target="tpu_custom_call" | custom-call | flops 800000000 | bytes 4000000 | tf_op jit(solution)/shard_map/patches/pallas_call | solution.py:269
  18.4 3.8 %collective-permute-start.4 = (f32[32,16,128]{2,1,0:T(8,128)S(1)}, f32[32,16,128]{2,1,0:T(8,128)S(1)}, u32[]{:S(2)}, u32[]{:S(2)}) collective-permute-start(f32[32,16,128]{2,1,0:T(8,128)S(1)} %get-tuple-element.14), channel_id=1, source_target_pairs={{0,1},{1,2},{2,3},{3,4},{4,5},{5,6},{6,7},{7,8},{8,9},{9,10},{10,1... | collective-permute-start | bytes 786440 | tf_op jit(solution)/shard_map/ppermute | solution.py:336
  22.2 20.5 %all-to-all-start = ((f32[128,1,128]{2,1,0:T(1,128)}), f32[128,1,128]{2,1,0:T(1,128)S(1)}, u32[]{:S(2)}, u32[]{:S(2)}) async-start(f32[128,1,128]{2,1,0:T(1,128)} %get-tuple-element.12), calls=%async_computation | async-start | bytes 131072 | tf_op jit(solution)/shard_map/all_to_all | solution.py:348
  42.6 0.0 collective-permute-done.4.from_y
  42.7 2.5 %collective-permute-start.5 = (f32[16,16,128]{2,1,0:T(8,128)S(1)}, f32[16,16,128]{2,1,0:T(8,128)S(1)}, u32[]{:S(2)}, u32[]{:S(2)}) collective-permute-start(f32[16,16,128]{2,1,0:T(8,128)S(1)} %slice_add_fusion), channel_id=1, source_target_pairs={{0,16},{1,17},{2,18},{3,19},{4,20},{5,21},{6,22},{7,23},{8,24},{9,... | collective-permute-start | bytes 393224 | tf_op jit(solution)/shard_map/ppermute | solution.py:336
  45.2 7.8 %all-to-all-done.sums_ref = f32[128,1,128]{2,1,0:T(1,128)S(1)} async-done(((f32[128,1,128]{2,1,0:T(1,128)}), f32[128,1,128]{2,1,0:T(1,128)S(1)}, u32[]{:S(2)}, u32[]{:S(2)}) %all-to-all-start) | async-done | bytes 65568 | tf_op jit(solution)/shard_map/all_to_all | solution.py:348
  53.0 0.0 collective-permute-start.3
  53.0 0.3 near.1.own
  53.3 1.0 %collective-permute-done.3.others_ref = f32[128,1,128]{2,1,0:T(1,128)S(1)} collective-permute-done((f32[128,1,128]{2,1,0:T(1,128)S(1)}, f32[128,1,128]{2,1,0:T(1,128)S(1)}, u32[]{:S(2)}, u32[]{:S(2)}) %collective-permute-start.3) | collective-permute-done | bytes 65568 | tf_op jit(solution)/shard_map/ppermute | solution.py:349
  54.3 0.0 collective-permute-done.5.from_x
  54.3 0.9 %finish.1 = (f32[16,16,128]{2,1,0:T(8,128)}, f32[16,16,128]{2,1,0:T(8,128)}) custom-call(f32[128,1,128]{2,1,0:T(1,128)S(1)} %all-to-all-done.sums_ref, f32[128,1,128]{2,1,0:T(1,128)S(1)} %collective-permute-done.3.others_ref, f32[16,16,128]{2,1,0:T(8,128)S(1)} %multiply_add_fusion.block_ref.rhs_ref, f32[16,16,128]{2,1,0:T(8,128)S(1)} %near.1.own, ...), custom_call_target="tpu_custom_call" | custom-call | flops 1000000 | bytes 1000000 | tf_op jit(solution)/shard_map/finish/pallas_call | solution.py:317
  (1 shorter events, 0.0 us)
Async XLA Ops:
  0.6 14.5 %copy-start = (f32[16,16,128]{2,1,0:T(8,128)S(1)}, f32[16,16,128]{2,1,0:T(8,128)}, u32[]{:S(2)}) copy-start(f32[16,16,128]{2,1,0:T(8,128)} %damping_ref.3) | copy-start | bytes 393220
  1.7 12.8 %collective-permute-start.2 = (f32[16,16,128]{2,1,0:T(8,128)S(1)}, f32[16,16,128]{2,1,0:T(8,128)S(1)}, u32[]{:S(2)}, u32[]{:S(2)}) collective-permute-start(f32[16,16,128]{2,1,0:T(8,128)S(1)} %multiply_add_fusion.block_ref.rhs_ref), channel_id=1, source_target_pairs={{17,0},{18,1},{19,2},{20,3},{21,4},{22,5},{23,6},{24,7},{25,8},{26... | collective-permute-start | bytes 393224 | tf_op jit(solution)/shard_map/ppermute | solution.py:336
  3.0 11.5 %collective-permute-start.1 = (f32[16,16,128]{2,1,0:T(8,128)S(1)}, f32[16,16,128]{2,1,0:T(8,128)S(1)}, u32[]{:S(2)}, u32[]{:S(2)}) collective-permute-start(f32[16,16,128]{2,1,0:T(8,128)S(1)} %multiply_add_fusion.block_ref.rhs_ref), channel_id=1, source_target_pairs={{1,0},{2,1},{3,2},{4,3},{5,4},{6,5},{7,6},{8,7},{9,8},{10,9},{11,1... | collective-permute-start | bytes 393224 | tf_op jit(solution)/shard_map/ppermute | solution.py:336
  8.2 7.0 %collective-permute-start = (f32[16,16,128]{2,1,0:T(8,128)S(1)}, f32[16,16,128]{2,1,0:T(8,128)S(1)}, u32[]{:S(2)}, u32[]{:S(2)}) collective-permute-start(f32[16,16,128]{2,1,0:T(8,128)S(1)} %multiply_add_fusion.block_ref.rhs_ref), channel_id=1, source_target_pairs={{16,0},{17,1},{18,2},{19,3},{20,4},{21,5},{22,6},{23,7},{24,8},{25... | collective-permute-start | bytes 393224 | tf_op jit(solution)/shard_map/ppermute | solution.py:336
  10.1 0.7 %copy-start.1 = (s32[1,1,6]{2,1,0:T(1,128)S(1)}, s32[1,1,6]{2,1,0:T(1,128)}, u32[]{:S(2)}) copy-start(s32[1,1,6]{2,1,0:T(1,128)} %index_ref.1) | copy-start | bytes 76
  18.4 24.3 %collective-permute-start.4 = (f32[32,16,128]{2,1,0:T(8,128)S(1)}, f32[32,16,128]{2,1,0:T(8,128)S(1)}, u32[]{:S(2)}, u32[]{:S(2)}) collective-permute-start(f32[32,16,128]{2,1,0:T(8,128)S(1)} %get-tuple-element.14), channel_id=1, source_target_pairs={{0,1},{1,2},{2,3},{3,4},{4,5},{5,6},{6,7},{7,8},{8,9},{9,10},{10,1... | collective-permute-start | bytes 786440 | tf_op jit(solution)/shard_map/ppermute | solution.py:336
  22.2 30.8 %all-to-all-start = ((f32[128,1,128]{2,1,0:T(1,128)}), f32[128,1,128]{2,1,0:T(1,128)S(1)}, u32[]{:S(2)}, u32[]{:S(2)}) async-start(f32[128,1,128]{2,1,0:T(1,128)} %get-tuple-element.12), calls=%async_computation | async-start | bytes 131072 | tf_op jit(solution)/shard_map/all_to_all | solution.py:348
  42.7 11.6 %collective-permute-start.5 = (f32[16,16,128]{2,1,0:T(8,128)S(1)}, f32[16,16,128]{2,1,0:T(8,128)S(1)}, u32[]{:S(2)}, u32[]{:S(2)}) collective-permute-start(f32[16,16,128]{2,1,0:T(8,128)S(1)} %slice_add_fusion), channel_id=1, source_target_pairs={{0,16},{1,17},{2,18},{3,19},{4,20},{5,21},{6,22},{7,23},{8,24},{9,... | collective-permute-start | bytes 393224 | tf_op jit(solution)/shard_map/ppermute | solution.py:336
  53.0 1.3 %collective-permute-start.3 = (f32[128,1,128]{2,1,0:T(1,128)S(1)}, f32[128,1,128]{2,1,0:T(1,128)S(1)}, u32[]{:S(2)}, u32[]{:S(2)}) collective-permute-start(f32[128,1,128]{2,1,0:T(1,128)S(1)} %all-to-all-done.sums_ref), channel_id=1, source_target_pairs={{0,1},{1,0},{2,3},{3,2},{4,5},{5,4},{6,7},{7,6},{8,9},{9,8},{10,11... | collective-permute-start | bytes 196616 | tf_op jit(solution)/shard_map/ppermute | solution.py:349

commit v5 on v4

--- a/solution.py
+++ b/solution.py
@@ -192,8 +192,12 @@
 PITCH = 40
 
 
-def patches_kernel(window_ref, spectra_ref, own_ref, rhs_ref, damping_ref, b10, b01, b11,
-                   o10, upper, near_ref, sums_ref, real, imag, sums, sem):
+def strided(h, y):
+    return pl.ds(SUB * PITCH * h + y, SUB, stride=PITCH)
+
+
+def forward_kernel(window_ref, spectra_ref, own_ref, rhs_ref, damping_ref, b10, b01, b11,
+                   real, imag, sums_ref, sums, sem):
     window = halves(window_ref[...])
 
     for xq, yq, block in ((0, 0, None), (1, 0, b10), (0, 1, b01), (1, 1, b11)):
@@ -206,9 +210,6 @@
             real[rows, :] = result[HALF * i : HALF * (i + 1), :LANES]
             imag[rows, :] = result[HALF * i : HALF * (i + 1), LANES:]
 
-    def strided(h, y):
-        return pl.ds(SUB * PITCH * h + y, SUB, stride=PITCH)
-
     for h in range(4):
         out = dft32(lambda y: (real[strided(h, y), :] * TAPER[y], imag[strided(h, y), :] * TAPER[y]), -1)
         for k, (re, im) in enumerate(out):
@@ -221,16 +222,12 @@
             return pl.ds(x * PITCH + SUB * g, SUB)
 
         out = dft32(lambda x: (real[rows(x), :] * TAPER[x], imag[rows(x), :] * TAPER[x]), -1)
-        scaled = []
         for k, (re, im) in enumerate(out):
             s = spectra_ref[pl.ds(k * PATCH + SUB * g, SUB), :]
             sre, sim = s * re, s * im
             energy = energy + (sre * re + sim * im)
-            scaled.append((sre, sim))
-        out = dft32(lambda k: scaled[k], 1)
-        for x, (re, im) in enumerate(out):
-            real[rows(x), :] = re * (TAPER[x] / PATCH**3)
-            imag[rows(x), :] = im * (TAPER[x] / PATCH**3)
+            real[rows(k), :] = sre
+            imag[rows(k), :] = sim
 
     square = rhs_ref[...] * rhs_ref[...]
     rr = jnp.sum(square)
@@ -239,45 +236,67 @@
     sums[...] = jnp.where(lane == 0, rr, jnp.where(lane == 1, dd, 0.0))
     leaving = pltpu.make_async_copy(sums, sums_ref, sem)
     leaving.start()
+    leaving.wait()
+
+
+def forward(window, spectra, own, rhs, damping, blocks, copies):
+    vmem = pl.BlockSpec(memory_space=VMEM)
+    return pl.pallas_call(
+        forward_kernel,
+        out_shape=[jax.ShapeDtypeStruct((PATCH * PITCH, LANES), jnp.float32)] * 2
+        + [jax.ShapeDtypeStruct((copies, 1, LANES), jnp.float32)],
+        in_specs=[vmem] * 8,
+        out_specs=[vmem] * 2 + [pl.BlockSpec(memory_space=pltpu.HBM)],
+        scratch_shapes=[VMEM((copies, 1, LANES), jnp.float32), pltpu.SemaphoreType.DMA],
+        compiler_params=pltpu.CompilerParams(vmem_limit_bytes=32 * 2**20),
+        cost_estimate=pl.CostEstimate(flops=800_000_000, bytes_accessed=4_000_000, transcendentals=0),
+        name="forward",
+    )(window, spectra, own, rhs, damping, *blocks)
+
+
+def inverse_kernel(window_ref, real, imag, o10, o01, o11, near_ref, back_real, back_imag):
+    window = halves(window_ref[...])
+
+    for g in range(4):
+        def rows(x):
+            return pl.ds(x * PITCH + SUB * g, SUB)
+
+        out = dft32(lambda k: (real[rows(k), :], imag[rows(k), :]), 1)
+        for x, (re, im) in enumerate(out):
+            back_real[rows(x), :] = re * (TAPER[x] / PATCH**3)
+            back_imag[rows(x), :] = im * (TAPER[x] / PATCH**3)
 
     for h in range(4):
-        out = dft32(lambda k: (real[strided(h, k), :], imag[strided(h, k), :]), 1)
+        out = dft32(lambda k: (back_real[strided(h, k), :], back_imag[strided(h, k), :]), 1)
         for y, (re, im) in enumerate(out):
-            real[strided(h, y), :] = re * TAPER[y]
-            imag[strided(h, y), :] = im * TAPER[y]
-
-    for xq, yq in ((0, 0), (0, 1), (1, 1), (1, 0)):
+            back_real[strided(h, y), :] = re * TAPER[y]
+            back_imag[strided(h, y), :] = im * TAPER[y]
+
+    for xq, yq, out in ((0, 0, near_ref), (1, 1, o11), (0, 1, o01), (1, 0, o10)):
         pieces = []
         for i in range(HALF):
             rows = pl.ds((HALF * xq + i) * PITCH + HALF * yq, HALF)
-            pieces.append(jnp.concatenate([real[rows, :], imag[rows, :]], axis=1))
+            pieces.append(jnp.concatenate([back_real[rows, :], back_imag[rows, :]], axis=1))
         both = jnp.concatenate(pieces, axis=0)
-        if xq == 0 and yq == 0:
+        if out is near_ref:
             near_ref[...] = both
-            continue
-        image = dot3(halves(both), window, 1).reshape(HALF, HALF, LANES)
-        if yq == 0:
-            o10[...] = image
         else:
-            upper[pl.ds(HALF * xq, HALF)] = image
-    leaving.wait()
-
-
-def patches(window, spectra, own, rhs, damping, blocks, copies):
-    block = jax.ShapeDtypeStruct(blocks[0].shape, jnp.float32)
-    vmem = pl.BlockSpec(memory_space=VMEM)
-    return pl.pallas_call(
-        patches_kernel,
-        out_shape=[block, jax.ShapeDtypeStruct((PATCH, HALF, LANES), jnp.float32)]
-        + [jax.ShapeDtypeStruct(own.shape, jnp.float32), jax.ShapeDtypeStruct((copies, 1, LANES), jnp.float32)],
-        in_specs=[vmem] * 8,
-        out_specs=[vmem] * 3 + [pl.BlockSpec(memory_space=pltpu.HBM)],
-        scratch_shapes=[VMEM((PATCH * PITCH, LANES), jnp.float32)] * 2
-        + [VMEM((copies, 1, LANES), jnp.float32), pltpu.SemaphoreType.DMA],
+            out[...] = dot3(halves(both), window, 1).reshape(HALF, HALF, LANES)
+
+
+def inverse(window, real, imag):
+    vmem = pl.BlockSpec(memory_space=VMEM)
+    return pl.pallas_call(
+        inverse_kernel,
+        out_shape=[jax.ShapeDtypeStruct((HALF, HALF, LANES), jnp.float32)] * 3
+        + [jax.ShapeDtypeStruct((HALF * HALF, 2 * LANES), jnp.float32)],
+        in_specs=[vmem] * 3,
+        out_specs=[vmem] * 4,
+        scratch_shapes=[VMEM((PATCH * PITCH, LANES), jnp.float32)] * 2,
         compiler_params=pltpu.CompilerParams(vmem_limit_bytes=32 * 2**20),
         cost_estimate=pl.CostEstimate(flops=800_000_000, bytes_accessed=4_000_000, transcendentals=0),
-        name="patches",
-    )(window, spectra, own, rhs, damping, *blocks)
+        name="inverse",
+    )(window, real, imag)
 
 
 def near_kernel(window_ref, near_ref, rhs_ref, damping_ref, image_ref):
@@ -298,7 +317,7 @@
     )(window, inner, rhs, damping)
 
 
-def finish_kernel(sums_ref, others_ref, rhs_ref, own, from_y, from_x, solution_ref, residual_ref):
+def finish_kernel(sums_ref, others_ref, rhs_ref, own, r11, r01, r10, solution_ref, residual_ref):
     totals = [jnp.sum(ref[...], axis=(0, 1), keepdims=True)[0] for ref in (sums_ref, others_ref)]
     totals = totals[0] + totals[1]
     lane = lax.broadcasted_iota(jnp.int32, totals.shape, 1)
@@ -306,7 +325,7 @@
     dd = jnp.sum(jnp.where(lane == 1, totals, 0.0), axis=1, keepdims=True)
     alpha = (rr / dd)[None]
     rhs = rhs_ref[...]
-    image = (own[...] + from_y[:HALF]) + from_x[...]
+    image = (own[...] + r11[...]) + (r01[...] + r10[...])
     solution_ref[...] = alpha * rhs
     residual_ref[...] = rhs - alpha * image
 
@@ -317,7 +336,7 @@
     return pl.pallas_call(
         finish_kernel,
         out_shape=[block, block],
-        in_specs=[vmem] * 6,
+        in_specs=[vmem] * 7,
         out_specs=[vmem] * 2,
         compiler_params=pltpu.CompilerParams(vmem_limit_bytes=8 * 2**20),
         cost_estimate=pl.CostEstimate(flops=1_000_000, bytes_accessed=1_000_000, transcendentals=0),
@@ -341,14 +360,14 @@
     nx, ny = lax.axis_size("gx"), lax.axis_size("gy")
     halo = [moved(rhs, -1, 0), moved(rhs, 0, -1), moved(rhs, -1, -1)]
     spectra, window, own = prepare(psf_index, z_shift, psf_bank, rhs)
-    o10, upper, inner, sums = patches(window, spectra, own, rhs, damping, halo, nx * ny // 2)
-    from_y = moved(upper, 0, 1)
-    image = near(window, inner, rhs, damping)
+    real, imag, sums = forward(window, spectra, own, rhs, damping, halo, nx * ny // 2)
     groups = [[i * ny + j for i in range(nx) for j in range(k, ny, 2)] for k in range(2)]
     sums = lax.all_to_all(sums, ("gx", "gy"), 0, 0, axis_index_groups=groups)
     others = lax.ppermute(sums, "gy", [(j, j ^ 1) for j in range(ny)])
-    from_x = moved(o10 + from_y[HALF:], 1, 0)
-    return tuple(finish(sums, others, rhs, [image, from_y, from_x]))
+    o10, o01, o11, inner = inverse(window, real, imag)
+    back = [moved(o11, 1, 1), moved(o01, 0, 1), moved(o10, 1, 0)]
+    image = near(window, inner, rhs, damping)
+    return tuple(finish(sums, others, rhs, [image] + back))
 
 
 def solution(mesh):

time: 55.5 us -> 56 us (level)
  the two profiles are of different devices: /device:TPU:1 before, /device:TPU:31 now
where the time goes in v5:
time: 56 us; the launch traced here: 55.6 us
  starting transfers between devices  32.1 us (57%)
  waiting for transfers between devices  11.9 us (21%)
  Pallas kernels  8.46 us (15%)
  between operations  1.41 us (3%)
  other arithmetic  1.09 us (2%)
  local copies, waits for them, and re-layouts  0.65 us (1%)
    ppermute x6, starting transfers between devices, moved(): return lax.ppermute(x, ('gx', 'gy'), pairs)  23.8 us
    ppermute x6, waiting for transfers between devices, moved(): return lax.ppermute(x, ('gx', 'gy'), pairs)  11.9 us
    all_to_all x1, starting transfers between devices, body(): sums = lax.all_to_all(sums, ('gx', 'gy'), 0, 0, axis_index_groups=groups)  8.18 us
    pallas_call x1, Pallas kernels, prepare(): pl.pallas_call(prepare_kernel, out_shape=[jax.ShapeDtypeStruct((PATCH * P...  3.71 us
    pallas_call x1, Pallas kernels, forward(): pl.pallas_call(forward_kernel, out_shape=[jax.ShapeDtypeStruct((PATCH * P...  2.19 us
    pallas_call x1, Pallas kernels, inverse(): pl.pallas_call(inverse_kernel, out_shape=[jax.ShapeDtypeStruct((HALF, HAL...  1.35 us
  transfers between devices with their start and end apart: 8, of which 3 were waited for; matrix products, arithmetic and copies ran while one was open for 0% of the time, Pallas kernels for 10%

profile of v5, /device:TPU:31, one launch (start us, length us, event | category | flops | bytes accessed | tf_op | source)
XLA Modules:
  0.0 55.6 jit_solution(5573522991394356784)
XLA Ops:
  0.6 0.0 copy-start
  0.6 1.1 %multiply_add_fusion.block_ref.rhs_ref = f32[16,16,128]{2,1,0:T(8,128)S(1)} fusion(f32[16,16,128]{2,1,0:T(8,128)} %param.6, f32[16,16,128]{2,1,0:T(8,128)} %damping_ref.3, f32[16,16,128]{2,1,0:T(8,128)} %param.7), kind=kLoop, calls=%fused_computation | loop fusion | flops 65536 | bytes 524288 | tf_op jit(solution)/shard_map/add | solution.py:359
  1.7 7.1 %collective-permute-start.2 = (f32[16,16,128]{2,1,0:T(8,128)S(1)}, f32[16,16,128]{2,1,0:T(8,128)S(1)}, u32[]{:S(2)}, u32[]{:S(2)}) collective-permute-start(f32[16,16,128]{2,1,0:T(8,128)S(1)} %multiply_add_fusion.block_ref.rhs_ref), channel_id=1, source_target_pairs={{17,0},{18,1},{19,2},{20,3},{21,4},{22,5},{23,6},{24,7},{25,8},{26... | collective-permute-start | bytes 393224 | tf_op jit(solution)/shard_map/ppermute | solution.py:355
  8.8 1.9 %collective-permute-start.1 = (f32[16,16,128]{2,1,0:T(8,128)S(1)}, f32[16,16,128]{2,1,0:T(8,128)S(1)}, u32[]{:S(2)}, u32[]{:S(2)}) collective-permute-start(f32[16,16,128]{2,1,0:T(8,128)S(1)} %multiply_add_fusion.block_ref.rhs_ref), channel_id=1, source_target_pairs={{1,0},{2,1},{3,2},{4,3},{5,4},{6,5},{7,6},{8,7},{9,8},{10,9},{11,1... | collective-permute-start | bytes 393224 | tf_op jit(solution)/shard_map/ppermute | solution.py:355
  10.8 2.0 %collective-permute-start = (f32[16,16,128]{2,1,0:T(8,128)S(1)}, f32[16,16,128]{2,1,0:T(8,128)S(1)}, u32[]{:S(2)}, u32[]{:S(2)}) collective-permute-start(f32[16,16,128]{2,1,0:T(8,128)S(1)} %multiply_add_fusion.block_ref.rhs_ref), channel_id=1, source_target_pairs={{16,0},{17,1},{18,2},{19,3},{20,4},{21,5},{22,6},{23,7},{24,8},{25... | collective-permute-start | bytes 393224 | tf_op jit(solution)/shard_map/ppermute | solution.py:355
  13.4 0.0 copy-start.1
  13.4 0.6 %copy-done.1 = s32[1,1,6]{2,1,0:T(1,128)S(1)} copy-done((s32[1,1,6]{2,1,0:T(1,128)S(1)}, s32[1,1,6]{2,1,0:T(1,128)}, u32[]{:S(2)}) %copy-start.1) | copy-done | bytes 48
  14.1 3.7 %prepare.1 = (f32[1024,128]{1,0:T(8,128)S(1)}, f32[128,256]{1,0:T(8,128)S(1)}, f32[256,256]{1,0:T(8,128)S(1)}) custom-call(s32[1,1,6]{2,1,0:T(1,128)S(1)} %copy-done.1, s32[1,1]{1,0:T(1,128)S(6)} %copy.8.shift_ref, f32[32,32,32,32]{3,2,1,0:T(8,128)} %bank_ref.1, f32[16,16,128]{2,1,0:T(8,128)S(1)} %multiply_add_fusion.block_ref.rhs_ref), custom_call_target="tpu_custom_call" | custom-call | flops 400000000 | bytes 8000000 | tf_op jit(solution)/shard_map/prepare/pallas_call | solution.py:172
  17.8 0.0 collective-permute-done.2.b11
  17.8 4.5 %collective-permute-done.1.b01 = f32[16,16,128]{2,1,0:T(8,128)S(1)} collective-permute-done((f32[16,16,128]{2,1,0:T(8,128)S(1)}, f32[16,16,128]{2,1,0:T(8,128)S(1)}, u32[]{:S(2)}, u32[]{:S(2)}) %collective-permute-start.1) | collective-permute-done | bytes 131104 | tf_op jit(solution)/shard_map/ppermute | solution.py:355
  22.4 0.0 collective-permute-done.b10
  22.4 0.0 copy-done
  22.4 2.2 %forward.1 = (f32[1280,128]{1,0:T(8,128)S(1)}, f32[1280,128]{1,0:T(8,128)S(1)}, f32[128,1,128]{2,1,0:T(1,128)}) custom-call(f32[128,256]{1,0:T(8,128)S(1)} %get-tuple-element.12.window_ref, f32[1024,128]{1,0:T(8,128)S(1)} %get-tuple-element.13.spectra_ref, f32[256,256]{1,0:T(8,128)S(1)} %get-tuple-element.14.own_ref, ...), custom_call_target="tpu_custom_call" | custom-call | flops 800000000 | bytes 4000000 | tf_op jit(solution)/shard_map/forward/pallas_call | solution.py:244
  24.6 8.2 %all-to-all-start = ((f32[128,1,128]{2,1,0:T(1,128)}), f32[128,1,128]{2,1,0:T(1,128)S(1)}, u32[]{:S(2)}, u32[]{:S(2)}) async-start(f32[128,1,128]{2,1,0:T(1,128)} %get-tuple-element.15), calls=%async_computation | async-start | bytes 131072 | tf_op jit(solution)/shard_map/all_to_all | solution.py:365
  32.7 1.3 %inverse.1 = (f32[16,16,128]{2,1,0:T(8,128)S(1)}, f32[16,16,128]{2,1,0:T(8,128)S(1)}, f32[16,16,128]{2,1,0:T(8,128)S(1)}, f32[256,256]{1,0:T(8,128)S(1)}) custom-call(f32[128,256]{1,0:T(8,128)S(1)} %get-tuple-element.12.window_ref, f32[1280,128]{1,0:T(8,128)S(1)} %get-tuple-element.16.real, f32[1280,128]{1,0:T(8,128)S(1)} %get-tuple-element.17.imag), custom_call_target="tpu_custom_call" | custom-call | flops 800000000 | bytes 4000000 | tf_op jit(solution)/shard_map/inverse/pallas_call | solution.py:289
  34.1 7.8 %collective-permute-start.4 = (f32[16,16,128]{2,1,0:T(8,128)S(1)}, f32[16,16,128]{2,1,0:T(8,128)S(1)}, u32[]{:S(2)}, u32[]{:S(2)}) collective-permute-start(f32[16,16,128]{2,1,0:T(8,128)S(1)} %get-tuple-element.19), channel_id=1, source_target_pairs={{0,17},{1,18},{2,19},{3,20},{4,21},{5,22},{6,23},{7,24},{8,25},{9,... | collective-permute-start | bytes 393224 | tf_op jit(solution)/shard_map/ppermute | solution.py:355
  41.9 2.8 %collective-permute-start.5 = (f32[16,16,128]{2,1,0:T(8,128)S(1)}, f32[16,16,128]{2,1,0:T(8,128)S(1)}, u32[]{:S(2)}, u32[]{:S(2)}) collective-permute-start(f32[16,16,128]{2,1,0:T(8,128)S(1)} %get-tuple-element.20), channel_id=1, source_target_pairs={{0,1},{1,2},{2,3},{3,4},{4,5},{5,6},{6,7},{7,8},{8,9},{9,10},{10,1... | collective-permute-start | bytes 393224 | tf_op jit(solution)/shard_map/ppermute | solution.py:355
  44.7 2.3 %collective-permute-start.6 = (f32[16,16,128]{2,1,0:T(8,128)S(1)}, f32[16,16,128]{2,1,0:T(8,128)S(1)}, u32[]{:S(2)}, u32[]{:S(2)}) collective-permute-start(f32[16,16,128]{2,1,0:T(8,128)S(1)} %get-tuple-element.21), channel_id=1, source_target_pairs={{0,16},{1,17},{2,18},{3,19},{4,20},{5,21},{6,22},{7,23},{8,24},{9,... | collective-permute-start | bytes 393224 | tf_op jit(solution)/shard_map/ppermute | solution.py:355
  46.9 0.0 all-to-all-done.sums_ref
  47.0 0.1 collective-permute-start.3
  47.1 0.3 near.1.own
  47.3 2.1 %collective-permute-done.4.r11 = f32[16,16,128]{2,1,0:T(8,128)S(1)} collective-permute-done((f32[16,16,128]{2,1,0:T(8,128)S(1)}, f32[16,16,128]{2,1,0:T(8,128)S(1)}, u32[]{:S(2)}, u32[]{:S(2)}) %collective-permute-start.4) | collective-permute-done | bytes 131104 | tf_op jit(solution)/shard_map/ppermute | solution.py:355
  49.4 0.0 collective-permute-done.5.r01
  49.4 5.2 %collective-permute-done.6.r10 = f32[16,16,128]{2,1,0:T(8,128)S(1)} collective-permute-done((f32[16,16,128]{2,1,0:T(8,128)S(1)}, f32[16,16,128]{2,1,0:T(8,128)S(1)}, u32[]{:S(2)}, u32[]{:S(2)}) %collective-permute-start.6) | collective-permute-done | bytes 131104 | tf_op jit(solution)/shard_map/ppermute | solution.py:355
  54.7 0.0 collective-permute-done.3.others_ref
  54.7 0.9 %finish.1 = (f32[16,16,128]{2,1,0:T(8,128)}, f32[16,16,128]{2,1,0:T(8,128)}) custom-call(f32[128,1,128]{2,1,0:T(1,128)S(1)} %all-to-all-done.sums_ref, f32[128,1,128]{2,1,0:T(1,128)S(1)} %collective-permute-done.3.others_ref, f32[16,16,128]{2,1,0:T(8,128)S(1)} %multiply_add_fusion.block_ref.rhs_ref, f32[16,16,128]{2,1,0:T(8,128)S(1)} %near.1.own, ...), custom_call_target="tpu_custom_call" | custom-call | flops 1000000 | bytes 1000000 | tf_op jit(solution)/shard_map/finish/pallas_call | solution.py:336
Async XLA Ops:
  0.6 21.7 %copy-start = (f32[16,16,128]{2,1,0:T(8,128)S(1)}, f32[16,16,128]{2,1,0:T(8,128)}, u32[]{:S(2)}) copy-start(f32[16,16,128]{2,1,0:T(8,128)} %damping_ref.3) | copy-start | bytes 393220
  1.7 16.1 %collective-permute-start.2 = (f32[16,16,128]{2,1,0:T(8,128)S(1)}, f32[16,16,128]{2,1,0:T(8,128)S(1)}, u32[]{:S(2)}, u32[]{:S(2)}) collective-permute-start(f32[16,16,128]{2,1,0:T(8,128)S(1)} %multiply_add_fusion.block_ref.rhs_ref), channel_id=1, source_target_pairs={{17,0},{18,1},{19,2},{20,3},{21,4},{22,5},{23,6},{24,7},{25,8},{26... | collective-permute-start | bytes 393224 | tf_op jit(solution)/shard_map/ppermute | solution.py:355
  8.8 13.5 %collective-permute-start.1 = (f32[16,16,128]{2,1,0:T(8,128)S(1)}, f32[16,16,128]{2,1,0:T(8,128)S(1)}, u32[]{:S(2)}, u32[]{:S(2)}) collective-permute-start(f32[16,16,128]{2,1,0:T(8,128)S(1)} %multiply_add_fusion.block_ref.rhs_ref), channel_id=1, source_target_pairs={{1,0},{2,1},{3,2},{4,3},{5,4},{6,5},{7,6},{8,7},{9,8},{10,9},{11,1... | collective-permute-start | bytes 393224 | tf_op jit(solution)/shard_map/ppermute | solution.py:355
  10.8 11.6 %collective-permute-start = (f32[16,16,128]{2,1,0:T(8,128)S(1)}, f32[16,16,128]{2,1,0:T(8,128)S(1)}, u32[]{:S(2)}, u32[]{:S(2)}) collective-permute-start(f32[16,16,128]{2,1,0:T(8,128)S(1)} %multiply_add_fusion.block_ref.rhs_ref), channel_id=1, source_target_pairs={{16,0},{17,1},{18,2},{19,3},{20,4},{21,5},{22,6},{23,7},{24,8},{25... | collective-permute-start | bytes 393224 | tf_op jit(solution)/shard_map/ppermute | solution.py:355
  13.4 0.7 %copy-start.1 = (s32[1,1,6]{2,1,0:T(1,128)S(1)}, s32[1,1,6]{2,1,0:T(1,128)}, u32[]{:S(2)}) copy-start(s32[1,1,6]{2,1,0:T(1,128)} %index_ref.1) | copy-start | bytes 76
  24.6 22.4 %all-to-all-start = ((f32[128,1,128]{2,1,0:T(1,128)}), f32[128,1,128]{2,1,0:T(1,128)S(1)}, u32[]{:S(2)}, u32[]{:S(2)}) async-start(f32[128,1,128]{2,1,0:T(1,128)} %get-tuple-element.15), calls=%async_computation | async-start | bytes 131072 | tf_op jit(solution)/shard_map/all_to_all | solution.py:365
  34.1 15.3 %collective-permute-start.4 = (f32[16,16,128]{2,1,0:T(8,128)S(1)}, f32[16,16,128]{2,1,0:T(8,128)S(1)}, u32[]{:S(2)}, u32[]{:S(2)}) collective-permute-start(f32[16,16,128]{2,1,0:T(8,128)S(1)} %get-tuple-element.19), channel_id=1, source_target_pairs={{0,17},{1,18},{2,19},{3,20},{4,21},{5,22},{6,23},{7,24},{8,25},{9,... | collective-permute-start | bytes 393224 | tf_op jit(solution)/shard_map/ppermute | solution.py:355
  41.9 7.5 %collective-permute-start.5 = (f32[16,16,128]{2,1,0:T(8,128)S(1)}, f32[16,16,128]{2,1,0:T(8,128)S(1)}, u32[]{:S(2)}, u32[]{:S(2)}) collective-permute-start(f32[16,16,128]{2,1,0:T(8,128)S(1)} %get-tuple-element.20), channel_id=1, source_target_pairs={{0,1},{1,2},{2,3},{3,4},{4,5},{5,6},{6,7},{7,8},{8,9},{9,10},{10,1... | collective-permute-start | bytes 393224 | tf_op jit(solution)/shard_map/ppermute | solution.py:355
  44.7 10.0 %collective-permute-start.6 = (f32[16,16,128]{2,1,0:T(8,128)S(1)}, f32[16,16,128]{2,1,0:T(8,128)S(1)}, u32[]{:S(2)}, u32[]{:S(2)}) collective-permute-start(f32[16,16,128]{2,1,0:T(8,128)S(1)} %get-tuple-element.21), channel_id=1, source_target_pairs={{0,16},{1,17},{2,18},{3,19},{4,20},{5,21},{6,22},{7,23},{8,24},{9,... | collective-permute-start | bytes 393224 | tf_op jit(solution)/shard_map/ppermute | solution.py:355
  47.0 7.7 %collective-permute-start.3 = (f32[128,1,128]{2,1,0:T(1,128)S(1)}, f32[128,1,128]{2,1,0:T(1,128)S(1)}, u32[]{:S(2)}, u32[]{:S(2)}) collective-permute-start(f32[128,1,128]{2,1,0:T(1,128)S(1)} %all-to-all-done.sums_ref), channel_id=1, source_target_pairs={{0,1},{1,0},{2,3},{3,2},{4,5},{5,4},{6,7},{7,6},{8,9},{9,8},{10,11... | collective-permute-start | bytes 196616 | tf_op jit(solution)/shard_map/ppermute | solution.py:366

commit v6 on v4

--- a/solution.py
+++ b/solution.py
@@ -193,7 +193,7 @@
 
 
 def patches_kernel(window_ref, spectra_ref, own_ref, rhs_ref, damping_ref, b10, b01, b11,
-                   o10, upper, near_ref, sums_ref, real, imag, sums, sem):
+                   upper, inner, sums_ref, real, imag, held, sums, sem):
     window = halves(window_ref[...])
 
     for xq, yq, block in ((0, 0, None), (1, 0, b10), (0, 1, b01), (1, 1, b11)):
@@ -246,59 +246,59 @@
             real[strided(h, y), :] = re * TAPER[y]
             imag[strided(h, y), :] = im * TAPER[y]
 
-    for xq, yq in ((0, 0), (0, 1), (1, 1), (1, 0)):
-        pieces = []
+    for xq in range(2):
         for i in range(HALF):
-            rows = pl.ds((HALF * xq + i) * PITCH + HALF * yq, HALF)
-            pieces.append(jnp.concatenate([real[rows, :], imag[rows, :]], axis=1))
-        both = jnp.concatenate(pieces, axis=0)
-        if xq == 0 and yq == 0:
-            near_ref[...] = both
-            continue
-        image = dot3(halves(both), window, 1).reshape(HALF, HALF, LANES)
-        if yq == 0:
-            o10[...] = image
-        else:
-            upper[pl.ds(HALF * xq, HALF)] = image
+            rows = pl.ds((HALF * xq + i) * PITCH, PATCH)
+            target = pl.ds(i * PATCH, PATCH)
+            both = jnp.concatenate([real[rows, :], imag[rows, :]], axis=1)
+            if xq == 0:
+                inner[target, :] = both
+            else:
+                held[target, :] = both
+    upper[...] = dot3(halves(held[...]), window, 1).reshape(upper.shape)
     leaving.wait()
 
 
 def patches(window, spectra, own, rhs, damping, blocks, copies):
-    block = jax.ShapeDtypeStruct(blocks[0].shape, jnp.float32)
     vmem = pl.BlockSpec(memory_space=VMEM)
     return pl.pallas_call(
         patches_kernel,
-        out_shape=[block, jax.ShapeDtypeStruct((PATCH, HALF, LANES), jnp.float32)]
-        + [jax.ShapeDtypeStruct(own.shape, jnp.float32), jax.ShapeDtypeStruct((copies, 1, LANES), jnp.float32)],
+        out_shape=[jax.ShapeDtypeStruct((HALF, PATCH, LANES), jnp.float32)]
+        + [jax.ShapeDtypeStruct((HALF * PATCH, 2 * LANES), jnp.float32), jax.ShapeDtypeStruct((copies, 1, LANES), jnp.float32)],
         in_specs=[vmem] * 8,
-        out_specs=[vmem] * 3 + [pl.BlockSpec(memory_space=pltpu.HBM)],
+        out_specs=[vmem] * 2 + [pl.BlockSpec(memory_space=pltpu.HBM)],
         scratch_shapes=[VMEM((PATCH * PITCH, LANES), jnp.float32)] * 2
-        + [VMEM((copies, 1, LANES), jnp.float32), pltpu.SemaphoreType.DMA],
+        + [
+            VMEM((HALF * PATCH, 2 * LANES), jnp.float32),
+            VMEM((copies, 1, LANES), jnp.float32),
+            pltpu.SemaphoreType.DMA,
+        ],
         compiler_params=pltpu.CompilerParams(vmem_limit_bytes=32 * 2**20),
         cost_estimate=pl.CostEstimate(flops=800_000_000, bytes_accessed=4_000_000, transcendentals=0),
         name="patches",
     )(window, spectra, own, rhs, damping, *blocks)
 
 
-def near_kernel(window_ref, near_ref, rhs_ref, damping_ref, image_ref):
-    own = dot3(halves(near_ref[...]), halves(window_ref[...]), 1)
-    image_ref[...] = own.reshape(image_ref.shape) + damping_ref[...] * rhs_ref[...]
-
-
-def near(window, inner, rhs, damping):
+def near_kernel(window_ref, inner, rhs_ref, damping_ref, arrived, image_ref, leaving_ref):
+    lower = dot3(halves(inner[...]), halves(window_ref[...]), 1).reshape(arrived.shape) + arrived[...]
+    image_ref[...] = lower[:, :HALF] + damping_ref[...] * rhs_ref[...]
+    leaving_ref[...] = lower[:, HALF:]
+
+
+def near(window, inner, rhs, damping, arrived):
     vmem = pl.BlockSpec(memory_space=VMEM)
     return pl.pallas_call(
         near_kernel,
-        out_shape=jax.ShapeDtypeStruct(rhs.shape, jnp.float32),
-        in_specs=[vmem] * 4,
-        out_specs=vmem,
+        out_shape=[jax.ShapeDtypeStruct(rhs.shape, jnp.float32)] * 2,
+        in_specs=[vmem] * 5,
+        out_specs=[vmem] * 2,
         compiler_params=pltpu.CompilerParams(vmem_limit_bytes=32 * 2**20),
         cost_estimate=pl.CostEstimate(flops=20_000_000, bytes_accessed=1_000_000, transcendentals=0),
         name="near",
-    )(window, inner, rhs, damping)
-
-
-def finish_kernel(sums_ref, others_ref, rhs_ref, own, from_y, from_x, solution_ref, residual_ref):
+    )(window, inner, rhs, damping, arrived)
+
+
+def finish_kernel(sums_ref, others_ref, rhs_ref, own, from_y, solution_ref, residual_ref):
     totals = [jnp.sum(ref[...], axis=(0, 1), keepdims=True)[0] for ref in (sums_ref, others_ref)]
     totals = totals[0] + totals[1]
     lane = lax.broadcasted_iota(jnp.int32, totals.shape, 1)
@@ -306,7 +306,7 @@
     dd = jnp.sum(jnp.where(lane == 1, totals, 0.0), axis=1, keepdims=True)
     alpha = (rr / dd)[None]
     rhs = rhs_ref[...]
-    image = (own[...] + from_y[:HALF]) + from_x[...]
+    image = own[...] + from_y[...]
     solution_ref[...] = alpha * rhs
     residual_ref[...] = rhs - alpha * image
 
@@ -317,7 +317,7 @@
     return pl.pallas_call(
         finish_kernel,
         out_shape=[block, block],
-        in_specs=[vmem] * 6,
+        in_specs=[vmem] * 5,
         out_specs=[vmem] * 2,
         compiler_params=pltpu.CompilerParams(vmem_limit_bytes=8 * 2**20),
         cost_estimate=pl.CostEstimate(flops=1_000_000, bytes_accessed=1_000_000, transcendentals=0),
@@ -341,14 +341,14 @@
     nx, ny = lax.axis_size("gx"), lax.axis_size("gy")
     halo = [moved(rhs, -1, 0), moved(rhs, 0, -1), moved(rhs, -1, -1)]
     spectra, window, own = prepare(psf_index, z_shift, psf_bank, rhs)
-    o10, upper, inner, sums = patches(window, spectra, own, rhs, damping, halo, nx * ny // 2)
-    from_y = moved(upper, 0, 1)
-    image = near(window, inner, rhs, damping)
+    upper, inner, sums = patches(window, spectra, own, rhs, damping, halo, nx * ny // 2)
+    from_x = moved(upper, 1, 0)
     groups = [[i * ny + j for i in range(nx) for j in range(k, ny, 2)] for k in range(2)]
     sums = lax.all_to_all(sums, ("gx", "gy"), 0, 0, axis_index_groups=groups)
     others = lax.ppermute(sums, "gy", [(j, j ^ 1) for j in range(ny)])
-    from_x = moved(o10 + from_y[HALF:], 1, 0)
-    return tuple(finish(sums, others, rhs, [image, from_y, from_x]))
+    image, leaving = near(window, inner, rhs, damping, from_x)
+    from_y = moved(leaving, 0, 1)
+    return tuple(finish(sums, others, rhs, [image, from_y]))
 
 
 def solution(mesh):

time: 55.5 us -> 53.7 us (0.968)
  starting transfers between devices: 34.5 us -> 32.2 us
    all_to_all x1, starting transfers between devices: 20.5 us -> 18.3 us  [body(): sums = lax.all_to_all(sums, ('gx', 'gy'), 0, 0, axis_index_groups=groups)]
  transfers between devices with their start and end apart: 7 -> 7, of which waited for: 3 -> 3; matrix products, arithmetic and copies ran while one was open for 0% -> 0% of each run, Pallas kernels for 7% -> 8%
where the time goes in v6:
time: 53.7 us; the launch traced here: 53.4 us
  starting transfers between devices  32.2 us (60%)
  waiting for transfers between devices  9.87 us (18%)
  Pallas kernels  8.18 us (15%)
  between operations  1.39 us (3%)
  other arithmetic  1.09 us (2%)
  local copies, waits for them, and re-layouts  0.65 us (1%)
    all_to_all x1, starting transfers between devices, body(): sums = lax.all_to_all(sums, ('gx', 'gy'), 0, 0, axis_index_groups=groups)  18.3 us
    ppermute x5, starting transfers between devices, moved(): return lax.ppermute(x, ('gx', 'gy'), pairs)  13.6 us
    all_to_all x1, waiting for transfers between devices, body(): sums = lax.all_to_all(sums, ('gx', 'gy'), 0, 0, axis_index_groups=groups)  8.25 us
    pallas_call x1, Pallas kernels, prepare(): pl.pallas_call(prepare_kernel, out_shape=[jax.ShapeDtypeStruct((PATCH * P...  3.71 us
    pallas_call x1, Pallas kernels, patches(): pl.pallas_call(patches_kernel, out_shape=[jax.ShapeDtypeStruct((HALF, PAT...  3.15 us
    add x1, other arithmetic, body(): rhs = migrated + damping * prior_sample  1.09 us
  transfers between devices with their start and end apart: 7, of which 3 were waited for; matrix products, arithmetic and copies ran while one was open for 0% of the time, Pallas kernels for 8%

profile of v6, /device:TPU:1, one launch (start us, length us, event | category | flops | bytes accessed | tf_op | source)
XLA Modules:
  0.0 53.4 jit_solution(2256143439306231117)
XLA Ops:
  0.6 0.0 copy-start
  0.6 1.1 %multiply_add_fusion.block_ref.rhs_ref = f32[16,16,128]{2,1,0:T(8,128)S(1)} fusion(f32[16,16,128]{2,1,0:T(8,128)} %param.6, f32[16,16,128]{2,1,0:T(8,128)} %damping_ref.3, f32[16,16,128]{2,1,0:T(8,128)} %param.7), kind=kLoop, calls=%fused_computation | loop fusion | flops 65536 | bytes 524288 | tf_op jit(solution)/shard_map/add | solution.py:340
  1.7 1.3 %collective-permute-start.2 = (f32[16,16,128]{2,1,0:T(8,128)S(1)}, f32[16,16,128]{2,1,0:T(8,128)S(1)}, u32[]{:S(2)}, u32[]{:S(2)}) collective-permute-start(f32[16,16,128]{2,1,0:T(8,128)S(1)} %multiply_add_fusion.block_ref.rhs_ref), channel_id=1, source_target_pairs={{17,0},{18,1},{19,2},{20,3},{21,4},{22,5},{23,6},{24,7},{25,8},{26... | collective-permute-start | bytes 393224 | tf_op jit(solution)/shard_map/ppermute | solution.py:336
  3.0 5.1 %collective-permute-start.1 = (f32[16,16,128]{2,1,0:T(8,128)S(1)}, f32[16,16,128]{2,1,0:T(8,128)S(1)}, u32[]{:S(2)}, u32[]{:S(2)}) collective-permute-start(f32[16,16,128]{2,1,0:T(8,128)S(1)} %multiply_add_fusion.block_ref.rhs_ref), channel_id=1, source_target_pairs={{1,0},{2,1},{3,2},{4,3},{5,4},{6,5},{7,6},{8,7},{9,8},{10,9},{11,1... | collective-permute-start | bytes 393224 | tf_op jit(solution)/shard_map/ppermute | solution.py:336
  8.2 1.3 %collective-permute-start = (f32[16,16,128]{2,1,0:T(8,128)S(1)}, f32[16,16,128]{2,1,0:T(8,128)S(1)}, u32[]{:S(2)}, u32[]{:S(2)}) collective-permute-start(f32[16,16,128]{2,1,0:T(8,128)S(1)} %multiply_add_fusion.block_ref.rhs_ref), channel_id=1, source_target_pairs={{16,0},{17,1},{18,2},{19,3},{20,4},{21,5},{22,6},{23,7},{24,8},{25... | collective-permute-start | bytes 393224 | tf_op jit(solution)/shard_map/ppermute | solution.py:336
  10.1 0.0 copy-start.1
  10.1 0.6 %copy-done.1 = s32[1,1,6]{2,1,0:T(1,128)S(1)} copy-done((s32[1,1,6]{2,1,0:T(1,128)S(1)}, s32[1,1,6]{2,1,0:T(1,128)}, u32[]{:S(2)}) %copy-start.1) | copy-done | bytes 48
  10.8 3.7 %prepare.1 = (f32[1024,128]{1,0:T(8,128)S(1)}, f32[128,256]{1,0:T(8,128)S(1)}, f32[256,256]{1,0:T(8,128)S(1)}) custom-call(s32[1,1,6]{2,1,0:T(1,128)S(1)} %copy-done.1, s32[1,1]{1,0:T(1,128)S(6)} %copy.8.shift_ref, f32[32,32,32,32]{3,2,1,0:T(8,128)} %bank_ref.1, f32[16,16,128]{2,1,0:T(8,128)S(1)} %multiply_add_fusion.block_ref.rhs_ref), custom_call_target="tpu_custom_call" | custom-call | flops 400000000 | bytes 8000000 | tf_op jit(solution)/shard_map/prepare/pallas_call | solution.py:172
  14.5 0.0 collective-permute-done.2.b11
  14.5 0.0 collective-permute-done.1.b01
  14.5 0.6 %collective-permute-done.b10 = f32[16,16,128]{2,1,0:T(8,128)S(1)} collective-permute-done((f32[16,16,128]{2,1,0:T(8,128)S(1)}, f32[16,16,128]{2,1,0:T(8,128)S(1)}, u32[]{:S(2)}, u32[]{:S(2)}) %collective-permute-start) | collective-permute-done | bytes 131104 | tf_op jit(solution)/shard_map/ppermute | solution.py:336
  15.2 0.0 copy-done
  15.2 3.1 %patches.1 = (f32[16,32,128]{2,1,0:T(8,128)S(1)}, f32[512,256]{1,0:T(8,128)S(1)}, f32[128,1,128]{2,1,0:T(1,128)}) custom-call(f32[128,256]{1,0:T(8,128)S(1)} %get-tuple-element.10.window_ref, f32[1024,128]{1,0:T(8,128)S(1)} %get-tuple-element.11.spectra_ref, f32[256,256]{1,0:T(8,128)S(1)} %get-tuple-element.12.own_ref, ...), custom_call_target="tpu_custom_call" | custom-call | flops 800000000 | bytes 4000000 | tf_op jit(solution)/shard_map/patches/pallas_call | solution.py:264
  18.3 3.9 %collective-permute-start.4 = (f32[16,32,128]{2,1,0:T(8,128)S(1)}, f32[16,32,128]{2,1,0:T(8,128)S(1)}, u32[]{:S(2)}, u32[]{:S(2)}) collective-permute-start(f32[16,32,128]{2,1,0:T(8,128)S(1)} %get-tuple-element.15), channel_id=1, source_target_pairs={{0,16},{1,17},{2,18},{3,19},{4,20},{5,21},{6,22},{7,23},{8,24},{9,... | collective-permute-start | bytes 786440 | tf_op jit(solution)/shard_map/ppermute | solution.py:336
  22.3 18.3 %all-to-all-start = ((f32[128,1,128]{2,1,0:T(1,128)}), f32[128,1,128]{2,1,0:T(1,128)S(1)}, u32[]{:S(2)}, u32[]{:S(2)}) async-start(f32[128,1,128]{2,1,0:T(1,128)} %get-tuple-element.13), calls=%async_computation | async-start | bytes 131072 | tf_op jit(solution)/shard_map/all_to_all | solution.py:347
  40.6 0.0 collective-permute-done.4.arrived
  40.6 0.4 near.1
  41.0 1.9 %collective-permute-start.5 = (f32[16,16,128]{2,1,0:T(8,128)S(1)}, f32[16,16,128]{2,1,0:T(8,128)S(1)}, u32[]{:S(2)}, u32[]{:S(2)}) collective-permute-start(f32[16,16,128]{2,1,0:T(8,128)S(1)} %get-tuple-element.17), channel_id=1, source_target_pairs={{0,1},{1,2},{2,3},{3,4},{4,5},{5,6},{6,7},{7,8},{8,9},{9,10},{10,1... | collective-permute-start | bytes 393224 | tf_op jit(solution)/shard_map/ppermute | solution.py:336
  42.9 8.3 %all-to-all-done.sums_ref = f32[128,1,128]{2,1,0:T(1,128)S(1)} async-done(((f32[128,1,128]{2,1,0:T(1,128)}), f32[128,1,128]{2,1,0:T(1,128)S(1)}, u32[]{:S(2)}, u32[]{:S(2)}) %all-to-all-start) | async-done | bytes 65568 | tf_op jit(solution)/shard_map/all_to_all | solution.py:347
  51.2 0.3 collective-permute-start.3
  51.4 1.0 %collective-permute-done.3.others_ref = f32[128,1,128]{2,1,0:T(1,128)S(1)} collective-permute-done((f32[128,1,128]{2,1,0:T(1,128)S(1)}, f32[128,1,128]{2,1,0:T(1,128)S(1)}, u32[]{:S(2)}, u32[]{:S(2)}) %collective-permute-start.3) | collective-permute-done | bytes 65568 | tf_op jit(solution)/shard_map/ppermute | solution.py:348
  52.4 0.0 collective-permute-done.5.from_y
  52.4 0.9 %finish.1 = (f32[16,16,128]{2,1,0:T(8,128)}, f32[16,16,128]{2,1,0:T(8,128)}) custom-call(f32[128,1,128]{2,1,0:T(1,128)S(1)} %all-to-all-done.sums_ref, f32[128,1,128]{2,1,0:T(1,128)S(1)} %collective-permute-done.3.others_ref, f32[16,16,128]{2,1,0:T(8,128)S(1)} %multiply_add_fusion.block_ref.rhs_ref, f32[16,16,128]{2,1,0:T(8,128)S(1)} %get-tuple-element.16.own, ...), custom_call_target="tpu_custom_call" | custom-call | flops 1000000 | bytes 1000000 | tf_op jit(solution)/shard_map/finish/pallas_call | solution.py:317
Async XLA Ops:
  0.6 14.5 %copy-start = (f32[16,16,128]{2,1,0:T(8,128)S(1)}, f32[16,16,128]{2,1,0:T(8,128)}, u32[]{:S(2)}) copy-start(f32[16,16,128]{2,1,0:T(8,128)} %damping_ref.3) | copy-start | bytes 393220
  1.7 12.8 %collective-permute-start.2 = (f32[16,16,128]{2,1,0:T(8,128)S(1)}, f32[16,16,128]{2,1,0:T(8,128)S(1)}, u32[]{:S(2)}, u32[]{:S(2)}) collective-permute-start(f32[16,16,128]{2,1,0:T(8,128)S(1)} %multiply_add_fusion.block_ref.rhs_ref), channel_id=1, source_target_pairs={{17,0},{18,1},{19,2},{20,3},{21,4},{22,5},{23,6},{24,7},{25,8},{26... | collective-permute-start | bytes 393224 | tf_op jit(solution)/shard_map/ppermute | solution.py:336
  3.0 11.5 %collective-permute-start.1 = (f32[16,16,128]{2,1,0:T(8,128)S(1)}, f32[16,16,128]{2,1,0:T(8,128)S(1)}, u32[]{:S(2)}, u32[]{:S(2)}) collective-permute-start(f32[16,16,128]{2,1,0:T(8,128)S(1)} %multiply_add_fusion.block_ref.rhs_ref), channel_id=1, source_target_pairs={{1,0},{2,1},{3,2},{4,3},{5,4},{6,5},{7,6},{8,7},{9,8},{10,9},{11,1... | collective-permute-start | bytes 393224 | tf_op jit(solution)/shard_map/ppermute | solution.py:336
  8.2 7.0 %collective-permute-start = (f32[16,16,128]{2,1,0:T(8,128)S(1)}, f32[16,16,128]{2,1,0:T(8,128)S(1)}, u32[]{:S(2)}, u32[]{:S(2)}) collective-permute-start(f32[16,16,128]{2,1,0:T(8,128)S(1)} %multiply_add_fusion.block_ref.rhs_ref), channel_id=1, source_target_pairs={{16,0},{17,1},{18,2},{19,3},{20,4},{21,5},{22,6},{23,7},{24,8},{25... | collective-permute-start | bytes 393224 | tf_op jit(solution)/shard_map/ppermute | solution.py:336
  10.1 0.7 %copy-start.1 = (s32[1,1,6]{2,1,0:T(1,128)S(1)}, s32[1,1,6]{2,1,0:T(1,128)}, u32[]{:S(2)}) copy-start(s32[1,1,6]{2,1,0:T(1,128)} %index_ref.1) | copy-start | bytes 76
  18.3 22.3 %collective-permute-start.4 = (f32[16,32,128]{2,1,0:T(8,128)S(1)}, f32[16,32,128]{2,1,0:T(8,128)S(1)}, u32[]{:S(2)}, u32[]{:S(2)}) collective-permute-start(f32[16,32,128]{2,1,0:T(8,128)S(1)} %get-tuple-element.15), channel_id=1, source_target_pairs={{0,16},{1,17},{2,18},{3,19},{4,20},{5,21},{6,22},{7,23},{8,24},{9,... | collective-permute-start | bytes 786440 | tf_op jit(solution)/shard_map/ppermute | solution.py:336
  22.3 28.9 %all-to-all-start = ((f32[128,1,128]{2,1,0:T(1,128)}), f32[128,1,128]{2,1,0:T(1,128)S(1)}, u32[]{:S(2)}, u32[]{:S(2)}) async-start(f32[128,1,128]{2,1,0:T(1,128)} %get-tuple-element.13), calls=%async_computation | async-start | bytes 131072 | tf_op jit(solution)/shard_map/all_to_all | solution.py:347
  41.0 11.4 %collective-permute-start.5 = (f32[16,16,128]{2,1,0:T(8,128)S(1)}, f32[16,16,128]{2,1,0:T(8,128)S(1)}, u32[]{:S(2)}, u32[]{:S(2)}) collective-permute-start(f32[16,16,128]{2,1,0:T(8,128)S(1)} %get-tuple-element.17), channel_id=1, source_target_pairs={{0,1},{1,2},{2,3},{3,4},{4,5},{5,6},{6,7},{7,8},{8,9},{9,10},{10,1... | collective-permute-start | bytes 393224 | tf_op jit(solution)/shard_map/ppermute | solution.py:336
  51.2 1.3 %collective-permute-start.3 = (f32[128,1,128]{2,1,0:T(1,128)S(1)}, f32[128,1,128]{2,1,0:T(1,128)S(1)}, u32[]{:S(2)}, u32[]{:S(2)}) collective-permute-start(f32[128,1,128]{2,1,0:T(1,128)S(1)} %all-to-all-done.sums_ref), channel_id=1, source_target_pairs={{0,1},{1,0},{2,3},{3,2},{4,5},{5,4},{6,7},{7,6},{8,9},{9,8},{10,11... | collective-permute-start | bytes 196616 | tf_op jit(solution)/shard_map/ppermute | solution.py:348

commit v7 on v6

--- a/solution.py
+++ b/solution.py
@@ -192,8 +192,12 @@
 PITCH = 40
 
 
-def patches_kernel(window_ref, spectra_ref, own_ref, rhs_ref, damping_ref, b10, b01, b11,
-                   upper, inner, sums_ref, real, imag, held, sums, sem):
+def strided(h, y):
+    return pl.ds(SUB * PITCH * h + y, SUB, stride=PITCH)
+
+
+def patches_kernel(window_ref, spectra_ref, own_ref, rhs_ref, damping_ref, b10, b11, b01,
+                   upper, real, imag, sums_ref, held, sums, sem):
     window = halves(window_ref[...])
 
     for xq, yq, block in ((0, 0, None), (1, 0, b10), (0, 1, b01), (1, 1, b11)):
@@ -205,9 +209,6 @@
             rows = pl.ds((HALF * xq + i) * PITCH + HALF * yq, HALF)
             real[rows, :] = result[HALF * i : HALF * (i + 1), :LANES]
             imag[rows, :] = result[HALF * i : HALF * (i + 1), LANES:]
-
-    def strided(h, y):
-        return pl.ds(SUB * PITCH * h + y, SUB, stride=PITCH)
 
     for h in range(4):
         out = dft32(lambda y: (real[strided(h, y), :] * TAPER[y], imag[strided(h, y), :] * TAPER[y]), -1)
@@ -240,21 +241,14 @@
     leaving = pltpu.make_async_copy(sums, sums_ref, sem)
     leaving.start()
 
-    for h in range(4):
+    for h in range(2, 4):
         out = dft32(lambda k: (real[strided(h, k), :], imag[strided(h, k), :]), 1)
         for y, (re, im) in enumerate(out):
             real[strided(h, y), :] = re * TAPER[y]
             imag[strided(h, y), :] = im * TAPER[y]
-
-    for xq in range(2):
-        for i in range(HALF):
-            rows = pl.ds((HALF * xq + i) * PITCH, PATCH)
-            target = pl.ds(i * PATCH, PATCH)
-            both = jnp.concatenate([real[rows, :], imag[rows, :]], axis=1)
-            if xq == 0:
-                inner[target, :] = both
-            else:
-                held[target, :] = both
+    for i in range(HALF):
+        rows = pl.ds((HALF + i) * PITCH, PATCH)
+        held[pl.ds(i * PATCH, PATCH), :] = jnp.concatenate([real[rows, :], imag[rows, :]], axis=1)
     upper[...] = dot3(halves(held[...]), window, 1).reshape(upper.shape)
     leaving.wait()
 
@@ -264,11 +258,11 @@
     return pl.pallas_call(
         patches_kernel,
         out_shape=[jax.ShapeDtypeStruct((HALF, PATCH, LANES), jnp.float32)]
-        + [jax.ShapeDtypeStruct((HALF * PATCH, 2 * LANES), jnp.float32), jax.ShapeDtypeStruct((copies, 1, LANES), jnp.float32)],
+        + [jax.ShapeDtypeStruct((PATCH * PITCH, LANES), jnp.float32)] * 2
+        + [jax.ShapeDtypeStruct((copies, 1, LANES), jnp.float32)],
         in_specs=[vmem] * 8,
-        out_specs=[vmem] * 2 + [pl.BlockSpec(memory_space=pltpu.HBM)],
-        scratch_shapes=[VMEM((PATCH * PITCH, LANES), jnp.float32)] * 2
-        + [
+        out_specs=[vmem] * 3 + [pl.BlockSpec(memory_space=pltpu.HBM)],
+        scratch_shapes=[
             VMEM((HALF * PATCH, 2 * LANES), jnp.float32),
             VMEM((copies, 1, LANES), jnp.float32),
             pltpu.SemaphoreType.DMA,
@@ -279,23 +273,34 @@
     )(window, spectra, own, rhs, damping, *blocks)
 
 
-def near_kernel(window_ref, inner, rhs_ref, damping_ref, arrived, image_ref, leaving_ref):
-    lower = dot3(halves(inner[...]), halves(window_ref[...]), 1).reshape(arrived.shape) + arrived[...]
+def near_kernel(window_ref, real, imag, rhs_ref, damping_ref, arrived, image_ref, leaving_ref, held):
+    for h in range(2):
+        out = dft32(lambda k: (real[strided(h, k), :], imag[strided(h, k), :]), 1)
+        for y, (re, im) in enumerate(out):
+            held[0, strided(h, y), :] = re * TAPER[y]
+            held[1, strided(h, y), :] = im * TAPER[y]
+    both = [
+        jnp.concatenate([held[part, pl.ds(i * PITCH, PATCH), :] for i in range(HALF)], axis=0)
+        for part in range(2)
+    ]
+    both = jnp.concatenate(both, axis=1)
+    lower = dot3(halves(both), halves(window_ref[...]), 1).reshape(arrived.shape) + arrived[...]
     image_ref[...] = lower[:, :HALF] + damping_ref[...] * rhs_ref[...]
     leaving_ref[...] = lower[:, HALF:]
 
 
-def near(window, inner, rhs, damping, arrived):
+def near(window, real, imag, rhs, damping, arrived):
     vmem = pl.BlockSpec(memory_space=VMEM)
     return pl.pallas_call(
         near_kernel,
         out_shape=[jax.ShapeDtypeStruct(rhs.shape, jnp.float32)] * 2,
-        in_specs=[vmem] * 5,
+        in_specs=[vmem] * 6,
         out_specs=[vmem] * 2,
+        scratch_shapes=[VMEM((2, HALF * PITCH, LANES), jnp.float32)],
         compiler_params=pltpu.CompilerParams(vmem_limit_bytes=32 * 2**20),
         cost_estimate=pl.CostEstimate(flops=20_000_000, bytes_accessed=1_000_000, transcendentals=0),
         name="near",
-    )(window, inner, rhs, damping, arrived)
+    )(window, real, imag, rhs, damping, arrived)
 
 
 def finish_kernel(sums_ref, others_ref, rhs_ref, own, from_y, solution_ref, residual_ref):
@@ -339,14 +344,16 @@
 def body(migrated, prior_sample, damping, psf_bank, psf_index, z_shift):
     rhs = migrated + damping * prior_sample
     nx, ny = lax.axis_size("gx"), lax.axis_size("gy")
-    halo = [moved(rhs, -1, 0), moved(rhs, 0, -1), moved(rhs, -1, -1)]
+    from_x, from_xy, from_y = moved(rhs, -1, 0), moved(rhs, -1, -1), moved(rhs, 0, -1)
     spectra, window, own = prepare(psf_index, z_shift, psf_bank, rhs)
-    upper, inner, sums = patches(window, spectra, own, rhs, damping, halo, nx * ny // 2)
+    upper, real, imag, sums = patches(
+        window, spectra, own, rhs, damping, [from_x, from_xy, from_y], nx * ny // 2
+    )
     from_x = moved(upper, 1, 0)
     groups = [[i * ny + j for i in range(nx) for j in range(k, ny, 2)] for k in range(2)]
     sums = lax.all_to_all(sums, ("gx", "gy"), 0, 0, axis_index_groups=groups)
     others = lax.ppermute(sums, "gy", [(j, j ^ 1) for j in range(ny)])
-    image, leaving = near(window, inner, rhs, damping, from_x)
+    image, leaving = near(window, real, imag, rhs, damping, from_x)
     from_y = moved(leaving, 0, 1)
     return tuple(finish(sums, others, rhs, [image, from_y]))
 

time: 53.7 us -> 52.8 us (0.983)
  waiting for transfers between devices: 9.87 us -> 7.75 us
  starting transfers between devices: 32.2 us -> 33.5 us
    all_to_all x1, waiting for transfers between devices: 8.25 us -> 5.96 us  [body(): sums = lax.all_to_all(sums, ('gx', 'gy'), 0, 0, axis_index_groups=groups)]
    ppermute x1, starting transfers between devices: 0.26 us -> 2.24 us  [body(): others = lax.ppermute(sums, 'gy', [(j, j ^ 1) for j in range(ny)])]
    all_to_all x1, starting transfers between devices: 18.3 us -> 16.6 us  [body(): sums = lax.all_to_all(sums, ('gx', 'gy'), 0, 0, axis_index_groups=groups)]
    ppermute x5, starting transfers between devices: 13.6 us -> 14.6 us  [moved(): return lax.ppermute(x, ('gx', 'gy'), pairs)]
where the time goes in v7:
time: 52.8 us; the launch traced here: 52.5 us
  starting transfers between devices  33.5 us (63%)
  Pallas kernels  8.16 us (15%)
  waiting for transfers between devices  7.75 us (15%)
  between operations  1.38 us (3%)
  other arithmetic  1.09 us (2%)
  local copies, waits for them, and re-layouts  0.65 us (1%)
    all_to_all x1, starting transfers between devices, body(): sums = lax.all_to_all(sums, ('gx', 'gy'), 0, 0, axis_index_groups=groups)  16.6 us
    ppermute x5, starting transfers between devices, moved(): return lax.ppermute(x, ('gx', 'gy'), pairs)  14.6 us
    all_to_all x1, waiting for transfers between devices, body(): sums = lax.all_to_all(sums, ('gx', 'gy'), 0, 0, axis_index_groups=groups)  5.96 us
    pallas_call x1, Pallas kernels, prepare(): pl.pallas_call(prepare_kernel, out_shape=[jax.ShapeDtypeStruct((PATCH * P...  3.71 us
    pallas_call x1, Pallas kernels, patches(): pl.pallas_call(patches_kernel, out_shape=[jax.ShapeDtypeStruct((HALF, PAT...  2.87 us
    ppermute x1, starting transfers between devices, body(): others = lax.ppermute(sums, 'gy', [(j, j ^ 1) for j in range(ny)])  2.24 us
    add x1, other arithmetic, body(): rhs = migrated + damping * prior_sample  1.09 us
  transfers between devices with their start and end apart: 7, of which 3 were waited for; matrix products, arithmetic and copies ran while one was open for 0% of the time, Pallas kernels for 8%

profile of v7, /device:TPU:1, one launch (start us, length us, event | category | flops | bytes accessed | tf_op | source)
XLA Modules:
  0.0 52.5 jit_solution(8687085193072964890)
XLA Ops:
  0.6 0.0 copy-start
  0.6 1.1 %multiply_add_fusion.block_ref.rhs_ref = f32[16,16,128]{2,1,0:T(8,128)S(1)} fusion(f32[16,16,128]{2,1,0:T(8,128)} %param.6, f32[16,16,128]{2,1,0:T(8,128)} %damping_ref.3, f32[16,16,128]{2,1,0:T(8,128)} %param.7), kind=kLoop, calls=%fused_computation | loop fusion | flops 65536 | bytes 524288 | tf_op jit(solution)/shard_map/add | solution.py:345
  1.7 5.1 %collective-permute-start.2 = (f32[16,16,128]{2,1,0:T(8,128)S(1)}, f32[16,16,128]{2,1,0:T(8,128)S(1)}, u32[]{:S(2)}, u32[]{:S(2)}) collective-permute-start(f32[16,16,128]{2,1,0:T(8,128)S(1)} %multiply_add_fusion.block_ref.rhs_ref), channel_id=1, source_target_pairs={{1,0},{2,1},{3,2},{4,3},{5,4},{6,5},{7,6},{8,7},{9,8},{10,9},{11,1... | collective-permute-start | bytes 393224 | tf_op jit(solution)/shard_map/ppermute | solution.py:341
  6.9 1.3 %collective-permute-start.1 = (f32[16,16,128]{2,1,0:T(8,128)S(1)}, f32[16,16,128]{2,1,0:T(8,128)S(1)}, u32[]{:S(2)}, u32[]{:S(2)}) collective-permute-start(f32[16,16,128]{2,1,0:T(8,128)S(1)} %multiply_add_fusion.block_ref.rhs_ref), channel_id=1, source_target_pairs={{17,0},{18,1},{19,2},{20,3},{21,4},{22,5},{23,6},{24,7},{25,8},{26... | collective-permute-start | bytes 393224 | tf_op jit(solution)/shard_map/ppermute | solution.py:341
  8.2 1.3 %collective-permute-start = (f32[16,16,128]{2,1,0:T(8,128)S(1)}, f32[16,16,128]{2,1,0:T(8,128)S(1)}, u32[]{:S(2)}, u32[]{:S(2)}) collective-permute-start(f32[16,16,128]{2,1,0:T(8,128)S(1)} %multiply_add_fusion.block_ref.rhs_ref), channel_id=1, source_target_pairs={{16,0},{17,1},{18,2},{19,3},{20,4},{21,5},{22,6},{23,7},{24,8},{25... | collective-permute-start | bytes 393224 | tf_op jit(solution)/shard_map/ppermute | solution.py:341
  10.1 0.0 copy-start.1
  10.1 0.6 %copy-done.1 = s32[1,1,6]{2,1,0:T(1,128)S(1)} copy-done((s32[1,1,6]{2,1,0:T(1,128)S(1)}, s32[1,1,6]{2,1,0:T(1,128)}, u32[]{:S(2)}) %copy-start.1) | copy-done | bytes 48
  10.8 3.7 %prepare.1 = (f32[1024,128]{1,0:T(8,128)S(1)}, f32[128,256]{1,0:T(8,128)S(1)}, f32[256,256]{1,0:T(8,128)S(1)}) custom-call(s32[1,1,6]{2,1,0:T(1,128)S(1)} %copy-done.1, s32[1,1]{1,0:T(1,128)S(6)} %copy.8.shift_ref, f32[32,32,32,32]{3,2,1,0:T(8,128)} %bank_ref.1, f32[16,16,128]{2,1,0:T(8,128)S(1)} %multiply_add_fusion.block_ref.rhs_ref), custom_call_target="tpu_custom_call" | custom-call | flops 400000000 | bytes 8000000 | tf_op jit(solution)/shard_map/prepare/pallas_call | solution.py:172
  14.5 0.0 collective-permute-done.2.b01
  14.5 0.9 %collective-permute-done.1.b11 = f32[16,16,128]{2,1,0:T(8,128)S(1)} collective-permute-done((f32[16,16,128]{2,1,0:T(8,128)S(1)}, f32[16,16,128]{2,1,0:T(8,128)S(1)}, u32[]{:S(2)}, u32[]{:S(2)}) %collective-permute-start.1) | collective-permute-done | bytes 131104 | tf_op jit(solution)/shard_map/ppermute | solution.py:341
  15.4 0.0 collective-permute-done.b10
  15.4 0.0 copy-done
  15.4 2.9 %patches.1 = (f32[16,32,128]{2,1,0:T(8,128)S(1)}, f32[1280,128]{1,0:T(8,128)S(1)}, f32[1280,128]{1,0:T(8,128)S(1)}, f32[128,1,128]{2,1,0:T(1,128)}) custom-call(f32[128,256]{1,0:T(8,128)S(1)} %get-tuple-element.11.window_ref, f32[1024,128]{1,0:T(8,128)S(1)} %get-tuple-element.12.spectra_ref, f32[256,256]{1,0:T(8,128)S(1)} %get-tuple-element.13.own_ref, ...), custom_call_target="tpu_custom_call" | custom-call | flops 800000000 | bytes 4000000 | tf_op jit(solution)/shard_map/patches/pallas_call | solution.py:258
  18.3 3.2 %collective-permute-start.4 = (f32[16,32,128]{2,1,0:T(8,128)S(1)}, f32[16,32,128]{2,1,0:T(8,128)S(1)}, u32[]{:S(2)}, u32[]{:S(2)}) collective-permute-start(f32[16,32,128]{2,1,0:T(8,128)S(1)} %get-tuple-element.17), channel_id=1, source_target_pairs={{0,16},{1,17},{2,18},{3,19},{4,20},{5,21},{6,22},{7,23},{8,24},{9,... | collective-permute-start | bytes 786440 | tf_op jit(solution)/shard_map/ppermute | solution.py:341
  21.4 16.6 %all-to-all-start = ((f32[128,1,128]{2,1,0:T(1,128)}), f32[128,1,128]{2,1,0:T(1,128)S(1)}, u32[]{:S(2)}, u32[]{:S(2)}) async-start(f32[128,1,128]{2,1,0:T(1,128)} %get-tuple-element.14), calls=%async_computation | async-start | bytes 131072 | tf_op jit(solution)/shard_map/all_to_all | solution.py:354
  38.1 0.0 collective-permute-done.4.arrived
  38.1 0.6 %near.1 = (f32[16,16,128]{2,1,0:T(8,128)S(1)}, f32[16,16,128]{2,1,0:T(8,128)S(1)}) custom-call(f32[128,256]{1,0:T(8,128)S(1)} %get-tuple-element.11.window_ref, f32[1280,128]{1,0:T(8,128)S(1)} %get-tuple-element.15.real, f32[1280,128]{1,0:T(8,128)S(1)} %get-tuple-element.16.imag, f32[16,16,128]{2,1,0:T(8,128)S(1)} %multiply_add_fusion.block_ref.rhs_ref, ...), custom_call_target="tpu_custom_call" | custom-call | flops 20000000 | bytes 1000000 | tf_op jit(solution)/shard_map/near/pallas_call | solution.py:294
  38.7 3.7 %collective-permute-start.5 = (f32[16,16,128]{2,1,0:T(8,128)S(1)}, f32[16,16,128]{2,1,0:T(8,128)S(1)}, u32[]{:S(2)}, u32[]{:S(2)}) collective-permute-start(f32[16,16,128]{2,1,0:T(8,128)S(1)} %get-tuple-element.19), channel_id=1, source_target_pairs={{0,1},{1,2},{2,3},{3,4},{4,5},{5,6},{6,7},{7,8},{8,9},{9,10},{10,1... | collective-permute-start | bytes 393224 | tf_op jit(solution)/shard_map/ppermute | solution.py:341
  42.5 6.0 %all-to-all-done.sums_ref = f32[128,1,128]{2,1,0:T(1,128)S(1)} async-done(((f32[128,1,128]{2,1,0:T(1,128)}), f32[128,1,128]{2,1,0:T(1,128)S(1)}, u32[]{:S(2)}, u32[]{:S(2)}) %all-to-all-start) | async-done | bytes 65568 | tf_op jit(solution)/shard_map/all_to_all | solution.py:354
  48.4 2.2 %collective-permute-start.3 = (f32[128,1,128]{2,1,0:T(1,128)S(1)}, f32[128,1,128]{2,1,0:T(1,128)S(1)}, u32[]{:S(2)}, u32[]{:S(2)}) collective-permute-start(f32[128,1,128]{2,1,0:T(1,128)S(1)} %all-to-all-done.sums_ref), channel_id=1, source_target_pairs={{0,1},{1,0},{2,3},{3,2},{4,5},{5,4},{6,7},{7,6},{8,9},{9,8},{10,11... | collective-permute-start | bytes 196616 | tf_op jit(solution)/shard_map/ppermute | solution.py:355
  50.7 0.9 %collective-permute-done.3.others_ref = f32[128,1,128]{2,1,0:T(1,128)S(1)} collective-permute-done((f32[128,1,128]{2,1,0:T(1,128)S(1)}, f32[128,1,128]{2,1,0:T(1,128)S(1)}, u32[]{:S(2)}, u32[]{:S(2)}) %collective-permute-start.3) | collective-permute-done | bytes 65568 | tf_op jit(solution)/shard_map/ppermute | solution.py:355
  51.6 0.0 collective-permute-done.5.from_y
  51.6 0.9 %finish.1 = (f32[16,16,128]{2,1,0:T(8,128)}, f32[16,16,128]{2,1,0:T(8,128)}) custom-call(f32[128,1,128]{2,1,0:T(1,128)S(1)} %all-to-all-done.sums_ref, f32[128,1,128]{2,1,0:T(1,128)S(1)} %collective-permute-done.3.others_ref, f32[16,16,128]{2,1,0:T(8,128)S(1)} %multiply_add_fusion.block_ref.rhs_ref, f32[16,16,128]{2,1,0:T(8,128)S(1)} %get-tuple-element.18.own, ...), custom_call_target="tpu_custom_call" | custom-call | flops 1000000 | bytes 1000000 | tf_op jit(solution)/shard_map/finish/pallas_call | solution.py:322
Async XLA Ops:
  0.6 14.8 %copy-start = (f32[16,16,128]{2,1,0:T(8,128)S(1)}, f32[16,16,128]{2,1,0:T(8,128)}, u32[]{:S(2)}) copy-start(f32[16,16,128]{2,1,0:T(8,128)} %damping_ref.3) | copy-start | bytes 393220
  1.7 12.8 %collective-permute-start.2 = (f32[16,16,128]{2,1,0:T(8,128)S(1)}, f32[16,16,128]{2,1,0:T(8,128)S(1)}, u32[]{:S(2)}, u32[]{:S(2)}) collective-permute-start(f32[16,16,128]{2,1,0:T(8,128)S(1)} %multiply_add_fusion.block_ref.rhs_ref), channel_id=1, source_target_pairs={{1,0},{2,1},{3,2},{4,3},{5,4},{6,5},{7,6},{8,7},{9,8},{10,9},{11,1... | collective-permute-start | bytes 393224 | tf_op jit(solution)/shard_map/ppermute | solution.py:341
  6.9 8.5 %collective-permute-start.1 = (f32[16,16,128]{2,1,0:T(8,128)S(1)}, f32[16,16,128]{2,1,0:T(8,128)S(1)}, u32[]{:S(2)}, u32[]{:S(2)}) collective-permute-start(f32[16,16,128]{2,1,0:T(8,128)S(1)} %multiply_add_fusion.block_ref.rhs_ref), channel_id=1, source_target_pairs={{17,0},{18,1},{19,2},{20,3},{21,4},{22,5},{23,6},{24,7},{25,8},{26... | collective-permute-start | bytes 393224 | tf_op jit(solution)/shard_map/ppermute | solution.py:341
  8.2 7.2 %collective-permute-start = (f32[16,16,128]{2,1,0:T(8,128)S(1)}, f32[16,16,128]{2,1,0:T(8,128)S(1)}, u32[]{:S(2)}, u32[]{:S(2)}) collective-permute-start(f32[16,16,128]{2,1,0:T(8,128)S(1)} %multiply_add_fusion.block_ref.rhs_ref), channel_id=1, source_target_pairs={{16,0},{17,1},{18,2},{19,3},{20,4},{21,5},{22,6},{23,7},{24,8},{25... | collective-permute-start | bytes 393224 | tf_op jit(solution)/shard_map/ppermute | solution.py:341
  10.1 0.7 %copy-start.1 = (s32[1,1,6]{2,1,0:T(1,128)S(1)}, s32[1,1,6]{2,1,0:T(1,128)}, u32[]{:S(2)}) copy-start(s32[1,1,6]{2,1,0:T(1,128)} %index_ref.1) | copy-start | bytes 76
  18.3 19.8 %collective-permute-start.4 = (f32[16,32,128]{2,1,0:T(8,128)S(1)}, f32[16,32,128]{2,1,0:T(8,128)S(1)}, u32[]{:S(2)}, u32[]{:S(2)}) collective-permute-start(f32[16,32,128]{2,1,0:T(8,128)S(1)} %get-tuple-element.17), channel_id=1, source_target_pairs={{0,16},{1,17},{2,18},{3,19},{4,20},{5,21},{6,22},{7,23},{8,24},{9,... | collective-permute-start | bytes 786440 | tf_op jit(solution)/shard_map/ppermute | solution.py:341
  21.4 27.0 %all-to-all-start = ((f32[128,1,128]{2,1,0:T(1,128)}), f32[128,1,128]{2,1,0:T(1,128)S(1)}, u32[]{:S(2)}, u32[]{:S(2)}) async-start(f32[128,1,128]{2,1,0:T(1,128)} %get-tuple-element.14), calls=%async_computation | async-start | bytes 131072 | tf_op jit(solution)/shard_map/all_to_all | solution.py:354
  38.7 12.9 %collective-permute-start.5 = (f32[16,16,128]{2,1,0:T(8,128)S(1)}, f32[16,16,128]{2,1,0:T(8,128)S(1)}, u32[]{:S(2)}, u32[]{:S(2)}) collective-permute-start(f32[16,16,128]{2,1,0:T(8,128)S(1)} %get-tuple-element.19), channel_id=1, source_target_pairs={{0,1},{1,2},{2,3},{3,4},{4,5},{5,6},{6,7},{7,8},{8,9},{9,10},{10,1... | collective-permute-start | bytes 393224 | tf_op jit(solution)/shard_map/ppermute | solution.py:341
  48.4 3.1 %collective-permute-start.3 = (f32[128,1,128]{2,1,0:T(1,128)S(1)}, f32[128,1,128]{2,1,0:T(1,128)S(1)}, u32[]{:S(2)}, u32[]{:S(2)}) collective-permute-start(f32[128,1,128]{2,1,0:T(1,128)S(1)} %all-to-all-done.sums_ref), channel_id=1, source_target_pairs={{0,1},{1,0},{2,3},{3,2},{4,5},{5,4},{6,7},{7,6},{8,9},{9,8},{10,11... | collective-permute-start | bytes 196616 | tf_op jit(solution)/shard_map/ppermute | solution.py:355

commit v8 on v7

--- a/solution.py
+++ b/solution.py
@@ -303,31 +303,39 @@
     )(window, real, imag, rhs, damping, arrived)
 
 
-def finish_kernel(sums_ref, others_ref, rhs_ref, own, from_y, solution_ref, residual_ref):
-    totals = [jnp.sum(ref[...], axis=(0, 1), keepdims=True)[0] for ref in (sums_ref, others_ref)]
-    totals = totals[0] + totals[1]
+def finish_kernel(sums_ref, rhs_ref, own, from_y, solution_ref, residual_ref, solved, left, sems):
+    totals = jnp.sum(sums_ref[...], axis=(0, 1), keepdims=True)[0]
     lane = lax.broadcasted_iota(jnp.int32, totals.shape, 1)
     rr = jnp.sum(jnp.where(lane == 0, totals, 0.0), axis=1, keepdims=True)
     dd = jnp.sum(jnp.where(lane == 1, totals, 0.0), axis=1, keepdims=True)
     alpha = (rr / dd)[None]
-    rhs = rhs_ref[...]
-    image = own[...] + from_y[...]
-    solution_ref[...] = alpha * rhs
-    residual_ref[...] = rhs - alpha * image
-
-
-def finish(sums, others, rhs, parts):
+    leaving = []
+    for c in range(4):
+        rows = pl.ds(4 * c, 4)
+        rhs = rhs_ref[rows]
+        solved[rows] = alpha * rhs
+        left[rows] = rhs - alpha * (own[rows] + from_y[rows])
+        for k, (source, target) in enumerate(((solved, solution_ref), (left, residual_ref))):
+            copy = pltpu.make_async_copy(source.at[rows], target.at[rows], sems.at[2 * c + k])
+            copy.start()
+            leaving.append(copy)
+    for copy in leaving:
+        copy.wait()
+
+
+def finish(sums, rhs, parts):
     block = jax.ShapeDtypeStruct(rhs.shape, jnp.float32)
     vmem = pl.BlockSpec(memory_space=VMEM)
     return pl.pallas_call(
         finish_kernel,
         out_shape=[block, block],
-        in_specs=[vmem] * 5,
-        out_specs=[vmem] * 2,
+        in_specs=[vmem] * 4,
+        out_specs=[pl.BlockSpec(memory_space=pltpu.HBM)] * 2,
+        scratch_shapes=[VMEM(rhs.shape, jnp.float32)] * 2 + [pltpu.SemaphoreType.DMA((8,))],
         compiler_params=pltpu.CompilerParams(vmem_limit_bytes=8 * 2**20),
         cost_estimate=pl.CostEstimate(flops=1_000_000, bytes_accessed=1_000_000, transcendentals=0),
         name="finish",
-    )(sums, others, rhs, *parts)
+    )(sums, rhs, *parts)
 
 
 def moved(x, by_x, by_y):
@@ -347,15 +355,13 @@
     from_x, from_xy, from_y = moved(rhs, -1, 0), moved(rhs, -1, -1), moved(rhs, 0, -1)
     spectra, window, own = prepare(psf_index, z_shift, psf_bank, rhs)
     upper, real, imag, sums = patches(
-        window, spectra, own, rhs, damping, [from_x, from_xy, from_y], nx * ny // 2
+        window, spectra, own, rhs, damping, [from_x, from_xy, from_y], nx * ny
     )
     from_x = moved(upper, 1, 0)
-    groups = [[i * ny + j for i in range(nx) for j in range(k, ny, 2)] for k in range(2)]
-    sums = lax.all_to_all(sums, ("gx", "gy"), 0, 0, axis_index_groups=groups)
-    others = lax.ppermute(sums, "gy", [(j, j ^ 1) for j in range(ny)])
+    sums = lax.all_to_all(sums, ("gx", "gy"), 0, 0)
     image, leaving = near(window, real, imag, rhs, damping, from_x)
     from_y = moved(leaving, 0, 1)
-    return tuple(finish(sums, others, rhs, [image, from_y]))
+    return tuple(finish(sums, rhs, [image, from_y]))
 
 
 def solution(mesh):

time: 52.8 us -> 51.9 us (0.983)
  starting transfers between devices: 33.5 us -> 30.5 us
  waiting for transfers between devices: 7.75 us -> 9.6 us
    all_to_all x1, waiting for transfers between devices: 5.96 us -> 8.72 us  [body(): sums = lax.all_to_all(sums, ('gx', 'gy'), 0, 0)]
    ppermute x1 -> x0, starting transfers between devices: 2.24 us -> none  [body(): others = lax.ppermute(sums, 'gy', [(j, j ^ 1) for j in range(ny)])]
    ppermute x1 -> x0, waiting for transfers between devices: 0.9 us -> none  [body(): others = lax.ppermute(sums, 'gy', [(j, j ^ 1) for j in range(ny)])]
    all_to_all x1, starting transfers between devices: 16.6 us -> 16.1 us  [body(): sums = lax.all_to_all(sums, ('gx', 'gy'), 0, 0)]
  transfers between devices with their start and end apart: 7 -> 6, of which waited for: 3 -> 2; matrix products, arithmetic and copies ran while one was open for 0% -> 0% of each run, Pallas kernels for 8% -> 8%
where the time goes in v8:
time: 51.9 us; the launch traced here: 51.6 us
  starting transfers between devices  30.5 us (59%)
  waiting for transfers between devices  9.6 us (18%)
  Pallas kernels  8.39 us (16%)
  between operations  1.38 us (3%)
  other arithmetic  1.09 us (2%)
  local copies, waits for them, and re-layouts  0.65 us (1%)
    all_to_all x1, starting transfers between devices, body(): sums = lax.all_to_all(sums, ('gx', 'gy'), 0, 0)  16.1 us
    ppermute x5, starting transfers between devices, moved(): return lax.ppermute(x, ('gx', 'gy'), pairs)  14.4 us
    all_to_all x1, waiting for transfers between devices, body(): sums = lax.all_to_all(sums, ('gx', 'gy'), 0, 0)  8.72 us
    pallas_call x1, Pallas kernels, prepare(): pl.pallas_call(prepare_kernel, out_shape=[jax.ShapeDtypeStruct((PATCH * P...  3.71 us
    pallas_call x1, Pallas kernels, patches(): pl.pallas_call(patches_kernel, out_shape=[jax.ShapeDtypeStruct((HALF, PAT...  2.93 us
    pallas_call x1, Pallas kernels, finish(): pl.pallas_call(finish_kernel, out_shape=[block, block], in_specs=[vmem] *...  1.12 us
    add x1, other arithmetic, body(): rhs = migrated + damping * prior_sample  1.09 us
  transfers between devices with their start and end apart: 6, of which 2 were waited for; matrix products, arithmetic and copies ran while one was open for 0% of the time, Pallas kernels for 8%

profile of v8, /device:TPU:1, one launch (start us, length us, event | category | flops | bytes accessed | tf_op | source)
XLA Modules:
  0.0 51.6 jit_solution(1116619937973199676)
XLA Ops:
  0.6 0.0 copy-start
  0.6 1.1 %multiply_add_fusion.block_ref.rhs_ref = f32[16,16,128]{2,1,0:T(8,128)S(1)} fusion(f32[16,16,128]{2,1,0:T(8,128)} %param.6, f32[16,16,128]{2,1,0:T(8,128)} %damping_ref.3, f32[16,16,128]{2,1,0:T(8,128)} %param.7), kind=kLoop, calls=%fused_computation | loop fusion | flops 65536 | bytes 524288 | tf_op jit(solution)/shard_map/add | solution.py:353
  1.7 5.1 %collective-permute-start.2 = (f32[16,16,128]{2,1,0:T(8,128)S(1)}, f32[16,16,128]{2,1,0:T(8,128)S(1)}, u32[]{:S(2)}, u32[]{:S(2)}) collective-permute-start(f32[16,16,128]{2,1,0:T(8,128)S(1)} %multiply_add_fusion.block_ref.rhs_ref), channel_id=1, source_target_pairs={{1,0},{2,1},{3,2},{4,3},{5,4},{6,5},{7,6},{8,7},{9,8},{10,9},{11,1... | collective-permute-start | bytes 393224 | tf_op jit(solution)/shard_map/ppermute | solution.py:349
  6.9 1.3 %collective-permute-start.1 = (f32[16,16,128]{2,1,0:T(8,128)S(1)}, f32[16,16,128]{2,1,0:T(8,128)S(1)}, u32[]{:S(2)}, u32[]{:S(2)}) collective-permute-start(f32[16,16,128]{2,1,0:T(8,128)S(1)} %multiply_add_fusion.block_ref.rhs_ref), channel_id=1, source_target_pairs={{17,0},{18,1},{19,2},{20,3},{21,4},{22,5},{23,6},{24,7},{25,8},{26... | collective-permute-start | bytes 393224 | tf_op jit(solution)/shard_map/ppermute | solution.py:349
  8.2 1.3 %collective-permute-start = (f32[16,16,128]{2,1,0:T(8,128)S(1)}, f32[16,16,128]{2,1,0:T(8,128)S(1)}, u32[]{:S(2)}, u32[]{:S(2)}) collective-permute-start(f32[16,16,128]{2,1,0:T(8,128)S(1)} %multiply_add_fusion.block_ref.rhs_ref), channel_id=1, source_target_pairs={{16,0},{17,1},{18,2},{19,3},{20,4},{21,5},{22,6},{23,7},{24,8},{25... | collective-permute-start | bytes 393224 | tf_op jit(solution)/shard_map/ppermute | solution.py:349
  10.1 0.0 copy-start.1
  10.1 0.6 %copy-done.1 = s32[1,1,6]{2,1,0:T(1,128)S(1)} copy-done((s32[1,1,6]{2,1,0:T(1,128)S(1)}, s32[1,1,6]{2,1,0:T(1,128)}, u32[]{:S(2)}) %copy-start.1) | copy-done | bytes 48
  10.8 3.7 %prepare.1 = (f32[1024,128]{1,0:T(8,128)S(1)}, f32[128,256]{1,0:T(8,128)S(1)}, f32[256,256]{1,0:T(8,128)S(1)}) custom-call(s32[1,1,6]{2,1,0:T(1,128)S(1)} %copy-done.1, s32[1,1]{1,0:T(1,128)S(6)} %copy.8.shift_ref, f32[32,32,32,32]{3,2,1,0:T(8,128)} %bank_ref.1, f32[16,16,128]{2,1,0:T(8,128)S(1)} %multiply_add_fusion.block_ref.rhs_ref), custom_call_target="tpu_custom_call" | custom-call | flops 400000000 | bytes 8000000 | tf_op jit(solution)/shard_map/prepare/pallas_call | solution.py:172
  14.5 0.0 collective-permute-done.2.b01
  14.5 0.9 %collective-permute-done.1.b11 = f32[16,16,128]{2,1,0:T(8,128)S(1)} collective-permute-done((f32[16,16,128]{2,1,0:T(8,128)S(1)}, f32[16,16,128]{2,1,0:T(8,128)S(1)}, u32[]{:S(2)}, u32[]{:S(2)}) %collective-permute-start.1) | collective-permute-done | bytes 131104 | tf_op jit(solution)/shard_map/ppermute | solution.py:349
  15.4 0.0 collective-permute-done.b10
  15.4 0.0 copy-done
  15.4 2.9 %patches.1 = (f32[16,32,128]{2,1,0:T(8,128)S(1)}, f32[1280,128]{1,0:T(8,128)S(1)}, f32[1280,128]{1,0:T(8,128)S(1)}, f32[256,1,128]{2,1,0:T(1,128)}) custom-call(f32[128,256]{1,0:T(8,128)S(1)} %get-tuple-element.11.window_ref, f32[1024,128]{1,0:T(8,128)S(1)} %get-tuple-element.12.spectra_ref, f32[256,256]{1,0:T(8,128)S(1)} %get-tuple-element.13.own_ref, ...), custom_call_target="tpu_custom_call" | custom-call | flops 800000000 | bytes 4000000 | tf_op jit(solution)/shard_map/patches/pallas_call | solution.py:258
  18.3 3.2 %collective-permute-start.3 = (f32[16,32,128]{2,1,0:T(8,128)S(1)}, f32[16,32,128]{2,1,0:T(8,128)S(1)}, u32[]{:S(2)}, u32[]{:S(2)}) collective-permute-start(f32[16,32,128]{2,1,0:T(8,128)S(1)} %get-tuple-element.17), channel_id=1, source_target_pairs={{0,16},{1,17},{2,18},{3,19},{4,20},{5,21},{6,22},{7,23},{8,24},{9,... | collective-permute-start | bytes 786440 | tf_op jit(solution)/shard_map/ppermute | solution.py:349
  21.5 16.1 %all-to-all-start = ((f32[256,1,128]{2,1,0:T(1,128)}), f32[256,1,128]{2,1,0:T(1,128)S(1)}, u32[]{:S(2)}, u32[]{:S(2)}) async-start(f32[256,1,128]{2,1,0:T(1,128)} %get-tuple-element.14), calls=%async_computation | async-start | bytes 262144 | tf_op jit(solution)/shard_map/all_to_all | solution.py:361
  37.6 0.0 collective-permute-done.3.arrived
  37.6 0.6 %near.1 = (f32[16,16,128]{2,1,0:T(8,128)S(1)}, f32[16,16,128]{2,1,0:T(8,128)S(1)}) custom-call(f32[128,256]{1,0:T(8,128)S(1)} %get-tuple-element.11.window_ref, f32[1280,128]{1,0:T(8,128)S(1)} %get-tuple-element.15.real, f32[1280,128]{1,0:T(8,128)S(1)} %get-tuple-element.16.imag, f32[16,16,128]{2,1,0:T(8,128)S(1)} %multiply_add_fusion.block_ref.rhs_ref, ...), custom_call_target="tpu_custom_call" | custom-call | flops 20000000 | bytes 1000000 | tf_op jit(solution)/shard_map/near/pallas_call | solution.py:294
  38.2 3.5 %collective-permute-start.4 = (f32[16,16,128]{2,1,0:T(8,128)S(1)}, f32[16,16,128]{2,1,0:T(8,128)S(1)}, u32[]{:S(2)}, u32[]{:S(2)}) collective-permute-start(f32[16,16,128]{2,1,0:T(8,128)S(1)} %get-tuple-element.19), channel_id=1, source_target_pairs={{0,1},{1,2},{2,3},{3,4},{4,5},{5,6},{6,7},{7,8},{8,9},{9,10},{10,1... | collective-permute-start | bytes 393224 | tf_op jit(solution)/shard_map/ppermute | solution.py:349
  41.8 8.7 %all-to-all-done.sums_ref = f32[256,1,128]{2,1,0:T(1,128)S(1)} async-done(((f32[256,1,128]{2,1,0:T(1,128)}), f32[256,1,128]{2,1,0:T(1,128)S(1)}, u32[]{:S(2)}, u32[]{:S(2)}) %all-to-all-start) | async-done | bytes 131104 | tf_op jit(solution)/shard_map/all_to_all | solution.py:361
  50.5 0.0 collective-permute-done.4.from_y
  50.5 1.1 %finish.1 = (f32[16,16,128]{2,1,0:T(8,128)}, f32[16,16,128]{2,1,0:T(8,128)}) custom-call(f32[256,1,128]{2,1,0:T(1,128)S(1)} %all-to-all-done.sums_ref, f32[16,16,128]{2,1,0:T(8,128)S(1)} %multiply_add_fusion.block_ref.rhs_ref, f32[16,16,128]{2,1,0:T(8,128)S(1)} %get-tuple-element.18.own, f32[16,16,128]{2,1,0:T(8,128)S(1)} %collective-permute-done.4.from_y), custom_call_target="tpu_custom_call" | custom-call | flops 1000000 | bytes 1000000 | tf_op jit(solution)/shard_map/finish/pallas_call | solution.py:329
Async XLA Ops:
  0.6 14.8 %copy-start = (f32[16,16,128]{2,1,0:T(8,128)S(1)}, f32[16,16,128]{2,1,0:T(8,128)}, u32[]{:S(2)}) copy-start(f32[16,16,128]{2,1,0:T(8,128)} %damping_ref.3) | copy-start | bytes 393220
  1.7 12.8 %collective-permute-start.2 = (f32[16,16,128]{2,1,0:T(8,128)S(1)}, f32[16,16,128]{2,1,0:T(8,128)S(1)}, u32[]{:S(2)}, u32[]{:S(2)}) collective-permute-start(f32[16,16,128]{2,1,0:T(8,128)S(1)} %multiply_add_fusion.block_ref.rhs_ref), channel_id=1, source_target_pairs={{1,0},{2,1},{3,2},{4,3},{5,4},{6,5},{7,6},{8,7},{9,8},{10,9},{11,1... | collective-permute-start | bytes 393224 | tf_op jit(solution)/shard_map/ppermute | solution.py:349
  6.9 8.5 %collective-permute-start.1 = (f32[16,16,128]{2,1,0:T(8,128)S(1)}, f32[16,16,128]{2,1,0:T(8,128)S(1)}, u32[]{:S(2)}, u32[]{:S(2)}) collective-permute-start(f32[16,16,128]{2,1,0:T(8,128)S(1)} %multiply_add_fusion.block_ref.rhs_ref), channel_id=1, source_target_pairs={{17,0},{18,1},{19,2},{20,3},{21,4},{22,5},{23,6},{24,7},{25,8},{26... | collective-permute-start | bytes 393224 | tf_op jit(solution)/shard_map/ppermute | solution.py:349
  8.2 7.2 %collective-permute-start = (f32[16,16,128]{2,1,0:T(8,128)S(1)}, f32[16,16,128]{2,1,0:T(8,128)S(1)}, u32[]{:S(2)}, u32[]{:S(2)}) collective-permute-start(f32[16,16,128]{2,1,0:T(8,128)S(1)} %multiply_add_fusion.block_ref.rhs_ref), channel_id=1, source_target_pairs={{16,0},{17,1},{18,2},{19,3},{20,4},{21,5},{22,6},{23,7},{24,8},{25... | collective-permute-start | bytes 393224 | tf_op jit(solution)/shard_map/ppermute | solution.py:349
  10.1 0.7 %copy-start.1 = (s32[1,1,6]{2,1,0:T(1,128)S(1)}, s32[1,1,6]{2,1,0:T(1,128)}, u32[]{:S(2)}) copy-start(s32[1,1,6]{2,1,0:T(1,128)} %index_ref.1) | copy-start | bytes 76
  18.3 19.3 %collective-permute-start.3 = (f32[16,32,128]{2,1,0:T(8,128)S(1)}, f32[16,32,128]{2,1,0:T(8,128)S(1)}, u32[]{:S(2)}, u32[]{:S(2)}) collective-permute-start(f32[16,32,128]{2,1,0:T(8,128)S(1)} %get-tuple-element.17), channel_id=1, source_target_pairs={{0,16},{1,17},{2,18},{3,19},{4,20},{5,21},{6,22},{7,23},{8,24},{9,... | collective-permute-start | bytes 786440 | tf_op jit(solution)/shard_map/ppermute | solution.py:349
  21.5 29.0 %all-to-all-start = ((f32[256,1,128]{2,1,0:T(1,128)}), f32[256,1,128]{2,1,0:T(1,128)S(1)}, u32[]{:S(2)}, u32[]{:S(2)}) async-start(f32[256,1,128]{2,1,0:T(1,128)} %get-tuple-element.14), calls=%async_computation | async-start | bytes 262144 | tf_op jit(solution)/shard_map/all_to_all | solution.py:361
  38.2 12.3 %collective-permute-start.4 = (f32[16,16,128]{2,1,0:T(8,128)S(1)}, f32[16,16,128]{2,1,0:T(8,128)S(1)}, u32[]{:S(2)}, u32[]{:S(2)}) collective-permute-start(f32[16,16,128]{2,1,0:T(8,128)S(1)} %get-tuple-element.19), channel_id=1, source_target_pairs={{0,1},{1,2},{2,3},{3,4},{4,5},{5,6},{6,7},{7,8},{8,9},{9,10},{10,1... | collective-permute-start | bytes 393224 | tf_op jit(solution)/shard_map/ppermute | solution.py:349

commit v9 on v8

--- a/solution.py
+++ b/solution.py
@@ -304,7 +304,11 @@
 
 
 def finish_kernel(sums_ref, rhs_ref, own, from_y, solution_ref, residual_ref, solved, left, sems):
-    totals = jnp.sum(sums_ref[...], axis=(0, 1), keepdims=True)[0]
+    size = sums_ref.shape[0] // 8
+    parts = [jnp.sum(sums_ref[pl.ds(size * c, size)], axis=0) for c in range(8)]
+    while len(parts) > 1:
+        parts = [a + b for a, b in zip(parts[::2], parts[1::2])]
+    totals = parts[0]
     lane = lax.broadcasted_iota(jnp.int32, totals.shape, 1)
     rr = jnp.sum(jnp.where(lane == 0, totals, 0.0), axis=1, keepdims=True)
     dd = jnp.sum(jnp.where(lane == 1, totals, 0.0), axis=1, keepdims=True)

time: 51.9 us -> 51.7 us (level)
  no operation moved by 1% of the time
where the time goes in v9:
time: 51.7 us; the launch traced here: 51.4 us
  starting transfers between devices  30.5 us (59%)
  waiting for transfers between devices  9.6 us (19%)
  Pallas kernels  8.19 us (16%)
  between operations  1.38 us (3%)
  other arithmetic  1.09 us (2%)
  local copies, waits for them, and re-layouts  0.65 us (1%)
    all_to_all x1, starting transfers between devices, body(): sums = lax.all_to_all(sums, ('gx', 'gy'), 0, 0)  16.1 us
    ppermute x5, starting transfers between devices, moved(): return lax.ppermute(x, ('gx', 'gy'), pairs)  14.4 us
    all_to_all x1, waiting for transfers between devices, body(): sums = lax.all_to_all(sums, ('gx', 'gy'), 0, 0)  8.72 us
    pallas_call x1, Pallas kernels, prepare(): pl.pallas_call(prepare_kernel, out_shape=[jax.ShapeDtypeStruct((PATCH * P...  3.71 us
    pallas_call x1, Pallas kernels, patches(): pl.pallas_call(patches_kernel, out_shape=[jax.ShapeDtypeStruct((HALF, PAT...  2.93 us
    add x1, other arithmetic, body(): rhs = migrated + damping * prior_sample  1.09 us
  transfers between devices with their start and end apart: 6, of which 2 were waited for; matrix products, arithmetic and copies ran while one was open for 0% of the time, Pallas kernels for 8%

profile of v9, /device:TPU:1, one launch (start us, length us, event | category | flops | bytes accessed | tf_op | source)
XLA Modules:
  0.0 51.4 jit_solution(15933319622283966051)
XLA Ops:
  0.6 0.0 copy-start
  0.6 1.1 %multiply_add_fusion.block_ref.rhs_ref = f32[16,16,128]{2,1,0:T(8,128)S(1)} fusion(f32[16,16,128]{2,1,0:T(8,128)} %param.6, f32[16,16,128]{2,1,0:T(8,128)} %damping_ref.3, f32[16,16,128]{2,1,0:T(8,128)} %param.7), kind=kLoop, calls=%fused_computation | loop fusion | flops 65536 | bytes 524288 | tf_op jit(solution)/shard_map/add | solution.py:357
  1.7 5.1 %collective-permute-start.2 = (f32[16,16,128]{2,1,0:T(8,128)S(1)}, f32[16,16,128]{2,1,0:T(8,128)S(1)}, u32[]{:S(2)}, u32[]{:S(2)}) collective-permute-start(f32[16,16,128]{2,1,0:T(8,128)S(1)} %multiply_add_fusion.block_ref.rhs_ref), channel_id=1, source_target_pairs={{1,0},{2,1},{3,2},{4,3},{5,4},{6,5},{7,6},{8,7},{9,8},{10,9},{11,1... | collective-permute-start | bytes 393224 | tf_op jit(solution)/shard_map/ppermute | solution.py:353
  6.9 1.3 %collective-permute-start.1 = (f32[16,16,128]{2,1,0:T(8,128)S(1)}, f32[16,16,128]{2,1,0:T(8,128)S(1)}, u32[]{:S(2)}, u32[]{:S(2)}) collective-permute-start(f32[16,16,128]{2,1,0:T(8,128)S(1)} %multiply_add_fusion.block_ref.rhs_ref), channel_id=1, source_target_pairs={{17,0},{18,1},{19,2},{20,3},{21,4},{22,5},{23,6},{24,7},{25,8},{26... | collective-permute-start | bytes 393224 | tf_op jit(solution)/shard_map/ppermute | solution.py:353
  8.2 1.3 %collective-permute-start = (f32[16,16,128]{2,1,0:T(8,128)S(1)}, f32[16,16,128]{2,1,0:T(8,128)S(1)}, u32[]{:S(2)}, u32[]{:S(2)}) collective-permute-start(f32[16,16,128]{2,1,0:T(8,128)S(1)} %multiply_add_fusion.block_ref.rhs_ref), channel_id=1, source_target_pairs={{16,0},{17,1},{18,2},{19,3},{20,4},{21,5},{22,6},{23,7},{24,8},{25... | collective-permute-start | bytes 393224 | tf_op jit(solution)/shard_map/ppermute | solution.py:353
  10.1 0.0 copy-start.1
  10.1 0.6 %copy-done.1 = s32[1,1,6]{2,1,0:T(1,128)S(1)} copy-done((s32[1,1,6]{2,1,0:T(1,128)S(1)}, s32[1,1,6]{2,1,0:T(1,128)}, u32[]{:S(2)}) %copy-start.1) | copy-done | bytes 48
  10.8 3.7 %prepare.1 = (f32[1024,128]{1,0:T(8,128)S(1)}, f32[128,256]{1,0:T(8,128)S(1)}, f32[256,256]{1,0:T(8,128)S(1)}) custom-call(s32[1,1,6]{2,1,0:T(1,128)S(1)} %copy-done.1, s32[1,1]{1,0:T(1,128)S(6)} %copy.8.shift_ref, f32[32,32,32,32]{3,2,1,0:T(8,128)} %bank_ref.1, f32[16,16,128]{2,1,0:T(8,128)S(1)} %multiply_add_fusion.block_ref.rhs_ref), custom_call_target="tpu_custom_call" | custom-call | flops 400000000 | bytes 8000000 | tf_op jit(solution)/shard_map/prepare/pallas_call | solution.py:172
  14.5 0.0 collective-permute-done.2.b01
  14.5 0.9 %collective-permute-done.1.b11 = f32[16,16,128]{2,1,0:T(8,128)S(1)} collective-permute-done((f32[16,16,128]{2,1,0:T(8,128)S(1)}, f32[16,16,128]{2,1,0:T(8,128)S(1)}, u32[]{:S(2)}, u32[]{:S(2)}) %collective-permute-start.1) | collective-permute-done | bytes 131104 | tf_op jit(solution)/shard_map/ppermute | solution.py:353
  15.4 0.0 collective-permute-done.b10
  15.4 0.0 copy-done
  15.4 2.9 %patches.1 = (f32[16,32,128]{2,1,0:T(8,128)S(1)}, f32[1280,128]{1,0:T(8,128)S(1)}, f32[1280,128]{1,0:T(8,128)S(1)}, f32[256,1,128]{2,1,0:T(1,128)}) custom-call(f32[128,256]{1,0:T(8,128)S(1)} %get-tuple-element.11.window_ref, f32[1024,128]{1,0:T(8,128)S(1)} %get-tuple-element.12.spectra_ref, f32[256,256]{1,0:T(8,128)S(1)} %get-tuple-element.13.own_ref, ...), custom_call_target="tpu_custom_call" | custom-call | flops 800000000 | bytes 4000000 | tf_op jit(solution)/shard_map/patches/pallas_call | solution.py:258
  18.3 3.2 %collective-permute-start.3 = (f32[16,32,128]{2,1,0:T(8,128)S(1)}, f32[16,32,128]{2,1,0:T(8,128)S(1)}, u32[]{:S(2)}, u32[]{:S(2)}) collective-permute-start(f32[16,32,128]{2,1,0:T(8,128)S(1)} %get-tuple-element.17), channel_id=1, source_target_pairs={{0,16},{1,17},{2,18},{3,19},{4,20},{5,21},{6,22},{7,23},{8,24},{9,... | collective-permute-start | bytes 786440 | tf_op jit(solution)/shard_map/ppermute | solution.py:353
  21.5 16.1 %all-to-all-start = ((f32[256,1,128]{2,1,0:T(1,128)}), f32[256,1,128]{2,1,0:T(1,128)S(1)}, u32[]{:S(2)}, u32[]{:S(2)}) async-start(f32[256,1,128]{2,1,0:T(1,128)} %get-tuple-element.14), calls=%async_computation | async-start | bytes 262144 | tf_op jit(solution)/shard_map/all_to_all | solution.py:365
  37.6 0.0 collective-permute-done.3.arrived
  37.6 0.6 %near.1 = (f32[16,16,128]{2,1,0:T(8,128)S(1)}, f32[16,16,128]{2,1,0:T(8,128)S(1)}) custom-call(f32[128,256]{1,0:T(8,128)S(1)} %get-tuple-element.11.window_ref, f32[1280,128]{1,0:T(8,128)S(1)} %get-tuple-element.15.real, f32[1280,128]{1,0:T(8,128)S(1)} %get-tuple-element.16.imag, f32[16,16,128]{2,1,0:T(8,128)S(1)} %multiply_add_fusion.block_ref.rhs_ref, ...), custom_call_target="tpu_custom_call" | custom-call | flops 20000000 | bytes 1000000 | tf_op jit(solution)/shard_map/near/pallas_call | solution.py:294
  38.2 3.5 %collective-permute-start.4 = (f32[16,16,128]{2,1,0:T(8,128)S(1)}, f32[16,16,128]{2,1,0:T(8,128)S(1)}, u32[]{:S(2)}, u32[]{:S(2)}) collective-permute-start(f32[16,16,128]{2,1,0:T(8,128)S(1)} %get-tuple-element.19), channel_id=1, source_target_pairs={{0,1},{1,2},{2,3},{3,4},{4,5},{5,6},{6,7},{7,8},{8,9},{9,10},{10,1... | collective-permute-start | bytes 393224 | tf_op jit(solution)/shard_map/ppermute | solution.py:353
  41.8 8.7 %all-to-all-done.sums_ref = f32[256,1,128]{2,1,0:T(1,128)S(1)} async-done(((f32[256,1,128]{2,1,0:T(1,128)}), f32[256,1,128]{2,1,0:T(1,128)S(1)}, u32[]{:S(2)}, u32[]{:S(2)}) %all-to-all-start) | async-done | bytes 131104 | tf_op jit(solution)/shard_map/all_to_all | solution.py:365
  50.5 0.0 collective-permute-done.4.from_y
  50.5 0.9 %finish.1 = (f32[16,16,128]{2,1,0:T(8,128)}, f32[16,16,128]{2,1,0:T(8,128)}) custom-call(f32[256,1,128]{2,1,0:T(1,128)S(1)} %all-to-all-done.sums_ref, f32[16,16,128]{2,1,0:T(8,128)S(1)} %multiply_add_fusion.block_ref.rhs_ref, f32[16,16,128]{2,1,0:T(8,128)S(1)} %get-tuple-element.18.own, f32[16,16,128]{2,1,0:T(8,128)S(1)} %collective-permute-done.4.from_y), custom_call_target="tpu_custom_call" | custom-call | flops 1000000 | bytes 1000000 | tf_op jit(solution)/shard_map/finish/pallas_call | solution.py:333
Async XLA Ops:
  0.6 14.8 %copy-start = (f32[16,16,128]{2,1,0:T(8,128)S(1)}, f32[16,16,128]{2,1,0:T(8,128)}, u32[]{:S(2)}) copy-start(f32[16,16,128]{2,1,0:T(8,128)} %damping_ref.3) | copy-start | bytes 393220
  1.7 12.8 %collective-permute-start.2 = (f32[16,16,128]{2,1,0:T(8,128)S(1)}, f32[16,16,128]{2,1,0:T(8,128)S(1)}, u32[]{:S(2)}, u32[]{:S(2)}) collective-permute-start(f32[16,16,128]{2,1,0:T(8,128)S(1)} %multiply_add_fusion.block_ref.rhs_ref), channel_id=1, source_target_pairs={{1,0},{2,1},{3,2},{4,3},{5,4},{6,5},{7,6},{8,7},{9,8},{10,9},{11,1... | collective-permute-start | bytes 393224 | tf_op jit(solution)/shard_map/ppermute | solution.py:353
  6.9 8.5 %collective-permute-start.1 = (f32[16,16,128]{2,1,0:T(8,128)S(1)}, f32[16,16,128]{2,1,0:T(8,128)S(1)}, u32[]{:S(2)}, u32[]{:S(2)}) collective-permute-start(f32[16,16,128]{2,1,0:T(8,128)S(1)} %multiply_add_fusion.block_ref.rhs_ref), channel_id=1, source_target_pairs={{17,0},{18,1},{19,2},{20,3},{21,4},{22,5},{23,6},{24,7},{25,8},{26... | collective-permute-start | bytes 393224 | tf_op jit(solution)/shard_map/ppermute | solution.py:353
  8.2 7.2 %collective-permute-start = (f32[16,16,128]{2,1,0:T(8,128)S(1)}, f32[16,16,128]{2,1,0:T(8,128)S(1)}, u32[]{:S(2)}, u32[]{:S(2)}) collective-permute-start(f32[16,16,128]{2,1,0:T(8,128)S(1)} %multiply_add_fusion.block_ref.rhs_ref), channel_id=1, source_target_pairs={{16,0},{17,1},{18,2},{19,3},{20,4},{21,5},{22,6},{23,7},{24,8},{25... | collective-permute-start | bytes 393224 | tf_op jit(solution)/shard_map/ppermute | solution.py:353
  10.1 0.7 %copy-start.1 = (s32[1,1,6]{2,1,0:T(1,128)S(1)}, s32[1,1,6]{2,1,0:T(1,128)}, u32[]{:S(2)}) copy-start(s32[1,1,6]{2,1,0:T(1,128)} %index_ref.1) | copy-start | bytes 76
  18.3 19.3 %collective-permute-start.3 = (f32[16,32,128]{2,1,0:T(8,128)S(1)}, f32[16,32,128]{2,1,0:T(8,128)S(1)}, u32[]{:S(2)}, u32[]{:S(2)}) collective-permute-start(f32[16,32,128]{2,1,0:T(8,128)S(1)} %get-tuple-element.17), channel_id=1, source_target_pairs={{0,16},{1,17},{2,18},{3,19},{4,20},{5,21},{6,22},{7,23},{8,24},{9,... | collective-permute-start | bytes 786440 | tf_op jit(solution)/shard_map/ppermute | solution.py:353
  21.5 29.0 %all-to-all-start = ((f32[256,1,128]{2,1,0:T(1,128)}), f32[256,1,128]{2,1,0:T(1,128)S(1)}, u32[]{:S(2)}, u32[]{:S(2)}) async-start(f32[256,1,128]{2,1,0:T(1,128)} %get-tuple-element.14), calls=%async_computation | async-start | bytes 262144 | tf_op jit(solution)/shard_map/all_to_all | solution.py:365
  38.2 12.3 %collective-permute-start.4 = (f32[16,16,128]{2,1,0:T(8,128)S(1)}, f32[16,16,128]{2,1,0:T(8,128)S(1)}, u32[]{:S(2)}, u32[]{:S(2)}) collective-permute-start(f32[16,16,128]{2,1,0:T(8,128)S(1)} %get-tuple-element.19), channel_id=1, source_target_pairs={{0,1},{1,2},{2,3},{3,4},{4,5},{5,6},{6,7},{7,8},{8,9},{9,10},{10,1... | collective-permute-start | bytes 393224 | tf_op jit(solution)/shard_map/ppermute | solution.py:353

commit v10 on v9

--- a/solution.py
+++ b/solution.py
@@ -197,7 +197,7 @@
 
 
 def patches_kernel(window_ref, spectra_ref, own_ref, rhs_ref, damping_ref, b10, b11, b01,
-                   upper, real, imag, sums_ref, held, sums, sem):
+                   upper, real, imag, sums_ref, sums, sem):
     window = halves(window_ref[...])
 
     for xq, yq, block in ((0, 0, None), (1, 0, b10), (0, 1, b01), (1, 1, b11)):
@@ -246,10 +246,12 @@
         for y, (re, im) in enumerate(out):
             real[strided(h, y), :] = re * TAPER[y]
             imag[strided(h, y), :] = im * TAPER[y]
-    for i in range(HALF):
-        rows = pl.ds((HALF + i) * PITCH, PATCH)
-        held[pl.ds(i * PATCH, PATCH), :] = jnp.concatenate([real[rows, :], imag[rows, :]], axis=1)
-    upper[...] = dot3(halves(held[...]), window, 1).reshape(upper.shape)
+    both = [
+        jnp.concatenate([part[pl.ds((HALF + i) * PITCH, PATCH), :] for i in range(HALF)], axis=0)
+        for part in (real, imag)
+    ]
+    both = jnp.concatenate(both, axis=1)
+    upper[...] = dot3(halves(both), window, 1).reshape(upper.shape)
     leaving.wait()
 
 
@@ -263,7 +265,6 @@
         in_specs=[vmem] * 8,
         out_specs=[vmem] * 3 + [pl.BlockSpec(memory_space=pltpu.HBM)],
         scratch_shapes=[
-            VMEM((HALF * PATCH, 2 * LANES), jnp.float32),
             VMEM((copies, 1, LANES), jnp.float32),
             pltpu.SemaphoreType.DMA,
         ],

time: 51.7 us -> 51.7 us (level)
  no operation moved by 1% of the time
where the time goes in v10:
time: 51.7 us; the launch traced here: 51.4 us
  starting transfers between devices  30.5 us (59%)
  waiting for transfers between devices  9.6 us (19%)
  Pallas kernels  8.19 us (16%)
  between operations  1.38 us (3%)
  other arithmetic  1.09 us (2%)
  local copies, waits for them, and re-layouts  0.65 us (1%)
    all_to_all x1, starting transfers between devices, body(): sums = lax.all_to_all(sums, ('gx', 'gy'), 0, 0)  16.1 us
    ppermute x5, starting transfers between devices, moved(): return lax.ppermute(x, ('gx', 'gy'), pairs)  14.4 us
    all_to_all x1, waiting for transfers between devices, body(): sums = lax.all_to_all(sums, ('gx', 'gy'), 0, 0)  8.72 us
    pallas_call x1, Pallas kernels, prepare(): pl.pallas_call(prepare_kernel, out_shape=[jax.ShapeDtypeStruct((PATCH * P...  3.71 us
    pallas_call x1, Pallas kernels, patches(): pl.pallas_call(patches_kernel, out_shape=[jax.ShapeDtypeStruct((HALF, PAT...  2.93 us
    add x1, other arithmetic, body(): rhs = migrated + damping * prior_sample  1.09 us
  transfers between devices with their start and end apart: 6, of which 2 were waited for; matrix products, arithmetic and copies ran while one was open for 0% of the time, Pallas kernels for 8%

profile of v10, /device:TPU:1, one launch (start us, length us, event | category | flops | bytes accessed | tf_op | source)
XLA Modules:
  0.0 51.4 jit_solution(15933319622283966051)
XLA Ops:
  0.6 0.0 copy-start
  0.6 1.1 %multiply_add_fusion.block_ref.rhs_ref = f32[16,16,128]{2,1,0:T(8,128)S(1)} fusion(f32[16,16,128]{2,1,0:T(8,128)} %param.6, f32[16,16,128]{2,1,0:T(8,128)} %damping_ref.3, f32[16,16,128]{2,1,0:T(8,128)} %param.7), kind=kLoop, calls=%fused_computation | loop fusion | flops 65536 | bytes 524288 | tf_op jit(solution)/shard_map/add | solution.py:358
  1.7 5.1 %collective-permute-start.2 = (f32[16,16,128]{2,1,0:T(8,128)S(1)}, f32[16,16,128]{2,1,0:T(8,128)S(1)}, u32[]{:S(2)}, u32[]{:S(2)}) collective-permute-start(f32[16,16,128]{2,1,0:T(8,128)S(1)} %multiply_add_fusion.block_ref.rhs_ref), channel_id=1, source_target_pairs={{1,0},{2,1},{3,2},{4,3},{5,4},{6,5},{7,6},{8,7},{9,8},{10,9},{11,1... | collective-permute-start | bytes 393224 | tf_op jit(solution)/shard_map/ppermute | solution.py:354
  6.9 1.3 %collective-permute-start.1 = (f32[16,16,128]{2,1,0:T(8,128)S(1)}, f32[16,16,128]{2,1,0:T(8,128)S(1)}, u32[]{:S(2)}, u32[]{:S(2)}) collective-permute-start(f32[16,16,128]{2,1,0:T(8,128)S(1)} %multiply_add_fusion.block_ref.rhs_ref), channel_id=1, source_target_pairs={{17,0},{18,1},{19,2},{20,3},{21,4},{22,5},{23,6},{24,7},{25,8},{26... | collective-permute-start | bytes 393224 | tf_op jit(solution)/shard_map/ppermute | solution.py:354
  8.2 1.3 %collective-permute-start = (f32[16,16,128]{2,1,0:T(8,128)S(1)}, f32[16,16,128]{2,1,0:T(8,128)S(1)}, u32[]{:S(2)}, u32[]{:S(2)}) collective-permute-start(f32[16,16,128]{2,1,0:T(8,128)S(1)} %multiply_add_fusion.block_ref.rhs_ref), channel_id=1, source_target_pairs={{16,0},{17,1},{18,2},{19,3},{20,4},{21,5},{22,6},{23,7},{24,8},{25... | collective-permute-start | bytes 393224 | tf_op jit(solution)/shard_map/ppermute | solution.py:354
  10.1 0.0 copy-start.1
  10.1 0.6 %copy-done.1 = s32[1,1,6]{2,1,0:T(1,128)S(1)} copy-done((s32[1,1,6]{2,1,0:T(1,128)S(1)}, s32[1,1,6]{2,1,0:T(1,128)}, u32[]{:S(2)}) %copy-start.1) | copy-done | bytes 48
  10.8 3.7 %prepare.1 = (f32[1024,128]{1,0:T(8,128)S(1)}, f32[128,256]{1,0:T(8,128)S(1)}, f32[256,256]{1,0:T(8,128)S(1)}) custom-call(s32[1,1,6]{2,1,0:T(1,128)S(1)} %copy-done.1, s32[1,1]{1,0:T(1,128)S(6)} %copy.8.shift_ref, f32[32,32,32,32]{3,2,1,0:T(8,128)} %bank_ref.1, f32[16,16,128]{2,1,0:T(8,128)S(1)} %multiply_add_fusion.block_ref.rhs_ref), custom_call_target="tpu_custom_call" | custom-call | flops 400000000 | bytes 8000000 | tf_op jit(solution)/shard_map/prepare/pallas_call | solution.py:172
  14.5 0.0 collective-permute-done.2.b01
  14.5 0.9 %collective-permute-done.1.b11 = f32[16,16,128]{2,1,0:T(8,128)S(1)} collective-permute-done((f32[16,16,128]{2,1,0:T(8,128)S(1)}, f32[16,16,128]{2,1,0:T(8,128)S(1)}, u32[]{:S(2)}, u32[]{:S(2)}) %collective-permute-start.1) | collective-permute-done | bytes 131104 | tf_op jit(solution)/shard_map/ppermute | solution.py:354
  15.4 0.0 collective-permute-done.b10
  15.4 0.0 copy-done
  15.4 2.9 %patches.1 = (f32[16,32,128]{2,1,0:T(8,128)S(1)}, f32[1280,128]{1,0:T(8,128)S(1)}, f32[1280,128]{1,0:T(8,128)S(1)}, f32[256,1,128]{2,1,0:T(1,128)}) custom-call(f32[128,256]{1,0:T(8,128)S(1)} %get-tuple-element.11.window_ref, f32[1024,128]{1,0:T(8,128)S(1)} %get-tuple-element.12.spectra_ref, f32[256,256]{1,0:T(8,128)S(1)} %get-tuple-element.13.own_ref, ...), custom_call_target="tpu_custom_call" | custom-call | flops 800000000 | bytes 4000000 | tf_op jit(solution)/shard_map/patches/pallas_call | solution.py:260
  18.3 3.2 %collective-permute-start.3 = (f32[16,32,128]{2,1,0:T(8,128)S(1)}, f32[16,32,128]{2,1,0:T(8,128)S(1)}, u32[]{:S(2)}, u32[]{:S(2)}) collective-permute-start(f32[16,32,128]{2,1,0:T(8,128)S(1)} %get-tuple-element.17), channel_id=1, source_target_pairs={{0,16},{1,17},{2,18},{3,19},{4,20},{5,21},{6,22},{7,23},{8,24},{9,... | collective-permute-start | bytes 786440 | tf_op jit(solution)/shard_map/ppermute | solution.py:354
  21.5 16.1 %all-to-all-start = ((f32[256,1,128]{2,1,0:T(1,128)}), f32[256,1,128]{2,1,0:T(1,128)S(1)}, u32[]{:S(2)}, u32[]{:S(2)}) async-start(f32[256,1,128]{2,1,0:T(1,128)} %get-tuple-element.14), calls=%async_computation | async-start | bytes 262144 | tf_op jit(solution)/shard_map/all_to_all | solution.py:366
  37.6 0.0 collective-permute-done.3.arrived
  37.6 0.6 %near.1 = (f32[16,16,128]{2,1,0:T(8,128)S(1)}, f32[16,16,128]{2,1,0:T(8,128)S(1)}) custom-call(f32[128,256]{1,0:T(8,128)S(1)} %get-tuple-element.11.window_ref, f32[1280,128]{1,0:T(8,128)S(1)} %get-tuple-element.15.real, f32[1280,128]{1,0:T(8,128)S(1)} %get-tuple-element.16.imag, f32[16,16,128]{2,1,0:T(8,128)S(1)} %multiply_add_fusion.block_ref.rhs_ref, ...), custom_call_target="tpu_custom_call" | custom-call | flops 20000000 | bytes 1000000 | tf_op jit(solution)/shard_map/near/pallas_call | solution.py:295
  38.2 3.5 %collective-permute-start.4 = (f32[16,16,128]{2,1,0:T(8,128)S(1)}, f32[16,16,128]{2,1,0:T(8,128)S(1)}, u32[]{:S(2)}, u32[]{:S(2)}) collective-permute-start(f32[16,16,128]{2,1,0:T(8,128)S(1)} %get-tuple-element.19), channel_id=1, source_target_pairs={{0,1},{1,2},{2,3},{3,4},{4,5},{5,6},{6,7},{7,8},{8,9},{9,10},{10,1... | collective-permute-start | bytes 393224 | tf_op jit(solution)/shard_map/ppermute | solution.py:354
  41.8 8.7 %all-to-all-done.sums_ref = f32[256,1,128]{2,1,0:T(1,128)S(1)} async-done(((f32[256,1,128]{2,1,0:T(1,128)}), f32[256,1,128]{2,1,0:T(1,128)S(1)}, u32[]{:S(2)}, u32[]{:S(2)}) %all-to-all-start) | async-done | bytes 131104 | tf_op jit(solution)/shard_map/all_to_all | solution.py:366
  50.5 0.0 collective-permute-done.4.from_y
  50.5 0.9 %finish.1 = (f32[16,16,128]{2,1,0:T(8,128)}, f32[16,16,128]{2,1,0:T(8,128)}) custom-call(f32[256,1,128]{2,1,0:T(1,128)S(1)} %all-to-all-done.sums_ref, f32[16,16,128]{2,1,0:T(8,128)S(1)} %multiply_add_fusion.block_ref.rhs_ref, f32[16,16,128]{2,1,0:T(8,128)S(1)} %get-tuple-element.18.own, f32[16,16,128]{2,1,0:T(8,128)S(1)} %collective-permute-done.4.from_y), custom_call_target="tpu_custom_call" | custom-call | flops 1000000 | bytes 1000000 | tf_op jit(solution)/shard_map/finish/pallas_call | solution.py:334
Async XLA Ops:
  0.6 14.8 %copy-start = (f32[16,16,128]{2,1,0:T(8,128)S(1)}, f32[16,16,128]{2,1,0:T(8,128)}, u32[]{:S(2)}) copy-start(f32[16,16,128]{2,1,0:T(8,128)} %damping_ref.3) | copy-start | bytes 393220
  1.7 12.8 %collective-permute-start.2 = (f32[16,16,128]{2,1,0:T(8,128)S(1)}, f32[16,16,128]{2,1,0:T(8,128)S(1)}, u32[]{:S(2)}, u32[]{:S(2)}) collective-permute-start(f32[16,16,128]{2,1,0:T(8,128)S(1)} %multiply_add_fusion.block_ref.rhs_ref), channel_id=1, source_target_pairs={{1,0},{2,1},{3,2},{4,3},{5,4},{6,5},{7,6},{8,7},{9,8},{10,9},{11,1... | collective-permute-start | bytes 393224 | tf_op jit(solution)/shard_map/ppermute | solution.py:354
  6.9 8.5 %collective-permute-start.1 = (f32[16,16,128]{2,1,0:T(8,128)S(1)}, f32[16,16,128]{2,1,0:T(8,128)S(1)}, u32[]{:S(2)}, u32[]{:S(2)}) collective-permute-start(f32[16,16,128]{2,1,0:T(8,128)S(1)} %multiply_add_fusion.block_ref.rhs_ref), channel_id=1, source_target_pairs={{17,0},{18,1},{19,2},{20,3},{21,4},{22,5},{23,6},{24,7},{25,8},{26... | collective-permute-start | bytes 393224 | tf_op jit(solution)/shard_map/ppermute | solution.py:354
  8.2 7.2 %collective-permute-start = (f32[16,16,128]{2,1,0:T(8,128)S(1)}, f32[16,16,128]{2,1,0:T(8,128)S(1)}, u32[]{:S(2)}, u32[]{:S(2)}) collective-permute-start(f32[16,16,128]{2,1,0:T(8,128)S(1)} %multiply_add_fusion.block_ref.rhs_ref), channel_id=1, source_target_pairs={{16,0},{17,1},{18,2},{19,3},{20,4},{21,5},{22,6},{23,7},{24,8},{25... | collective-permute-start | bytes 393224 | tf_op jit(solution)/shard_map/ppermute | solution.py:354
  10.1 0.7 %copy-start.1 = (s32[1,1,6]{2,1,0:T(1,128)S(1)}, s32[1,1,6]{2,1,0:T(1,128)}, u32[]{:S(2)}) copy-start(s32[1,1,6]{2,1,0:T(1,128)} %index_ref.1) | copy-start | bytes 76
  18.3 19.3 %collective-permute-start.3 = (f32[16,32,128]{2,1,0:T(8,128)S(1)}, f32[16,32,128]{2,1,0:T(8,128)S(1)}, u32[]{:S(2)}, u32[]{:S(2)}) collective-permute-start(f32[16,32,128]{2,1,0:T(8,128)S(1)} %get-tuple-element.17), channel_id=1, source_target_pairs={{0,16},{1,17},{2,18},{3,19},{4,20},{5,21},{6,22},{7,23},{8,24},{9,... | collective-permute-start | bytes 786440 | tf_op jit(solution)/shard_map/ppermute | solution.py:354
  21.5 29.0 %all-to-all-start = ((f32[256,1,128]{2,1,0:T(1,128)}), f32[256,1,128]{2,1,0:T(1,128)S(1)}, u32[]{:S(2)}, u32[]{:S(2)}) async-start(f32[256,1,128]{2,1,0:T(1,128)} %get-tuple-element.14), calls=%async_computation | async-start | bytes 262144 | tf_op jit(solution)/shard_map/all_to_all | solution.py:366
  38.2 12.3 %collective-permute-start.4 = (f32[16,16,128]{2,1,0:T(8,128)S(1)}, f32[16,16,128]{2,1,0:T(8,128)S(1)}, u32[]{:S(2)}, u32[]{:S(2)}) collective-permute-start(f32[16,16,128]{2,1,0:T(8,128)S(1)} %get-tuple-element.19), channel_id=1, source_target_pairs={{0,1},{1,2},{2,3},{3,4},{4,5},{5,6},{6,7},{7,8},{8,9},{9,10},{10,1... | collective-permute-start | bytes 393224 | tf_op jit(solution)/shard_map/ppermute | solution.py:354
